TPU v7x, 32 devices: a whole 2x2x4 slice. The times are simulated.
32 devices in a mesh: rep: 4 (over z), grp: 8 (over y, x, core).
Axes of the slice: x: 2, y: 2, z: 4, core: 2. Of those that a mesh axis runs over, the one named last changes fastest.
Arguments:
- tokens: bfloat16 [16384, 1792], P(('rep', 'grp')), may hold values from -6 to 6
- seg_ids: int32 [16384], P(('rep', 'grp')), may hold values from 0 to 16383, as said below
- valid_mask: int32 [16384], P(('rep', 'grp')), may hold values 0 or 1
- norm_gain: float32 [1792], replicated, may hold values from 0.5 to 1.5
- conv_taps: float32 [1792, 3], replicated, may hold values from -4 to 4
- mix_in: bfloat16 [1792, 2304], P('grp'), may hold values from -0.25 to 0.25
- mix_out: bfloat16 [1792, 1792], P('grp'), may hold values from -1 to 1
- ffn_gain: float32 [1792], replicated, may hold values from 0.5 to 1.5
- ffn_in: bfloat16 [3584, 3584], P('grp'), may hold values from -0.125 to 0.125
- ffn_out: bfloat16 [3584, 1792], P('grp'), may hold values from -0.09375 to 0.09375
- grad_out: bfloat16 [16384, 1792], P(('rep', 'grp')), may hold values from -6 to 6
Outputs:
- mixed_out: bfloat16 [16384, 1792], P(('rep', 'grp'))
- grad_tokens: bfloat16 [16384, 1792], P(('rep', 'grp'))
- grad_norm_gain: float32 [1792], replicated
- grad_conv_taps: float32 [1792, 3], replicated
- grad_mix_in: float32 [1792, 2304], P('grp')
- grad_mix_out: float32 [1792, 1792], P('grp')
- grad_ffn_gain: float32 [1792], replicated
- grad_ffn_in: float32 [3584, 3584], P('grp')
- grad_ffn_out: float32 [3584, 1792], P('grp')
- layer_stats: float32 [3], replicated
Inputs may be any that keep to these rules, and one draw needn't show every extreme that they name: `seg_ids`: ids never fall; the first token of every block of 4096 tokens has a larger id than the token before it; the first token's id is 0 and the last token's id is 16383.
All inputs are finite; a program needn't handle non-finite values. No bound on the sum of `valid_mask` on one device may be relied on, other than what follows from the above.
Results may differ from a plain program's by a relative error of at most 0.018.
The roundings to bfloat16 on the way count: a program that leaves them out, or rounds other values in their place, can miss the bound.
Values may be sent and summed in bfloat16 or wider, within the bound.
No kernel may reach another device: no remote copies, remote signals or barrier semaphores. Data moves between devices by JAX's collectives and lax.ppermute only.
A program may use at most 448 MiB of HBM per device.

v0:
```python
import math

import jax
import jax.numpy as jnp
from jax import lax
from jax.sharding import PartitionSpec as P

HEADS = 16
FEAT = 16
VDIM = 112
PHI = 273


EPSILON = 1e-05
HIGHEST = lax.Precision.HIGHEST
OUTER_SCALE = 0.25 / math.sqrt(2.0)


def passed_along(block, axis, distance):
    devices = range(lax.axis_size(axis))
    route = [(i - distance, i) for i in devices if i - distance in devices]
    return lax.ppermute(block, axis, route)


def prefix(value, axis, join, neutral):
    count, mine = (lax.axis_size(axis), lax.axis_index(axis))
    pieces = jax.tree.map(lambda part: lax.all_gather(part, axis), value)
    so_far = jax.tree.map(
        lambda part, zero: jnp.full_like(part, 0) + jnp.asarray(zero, part.dtype), value, neutral
    )

    def lap(position, so_far):
        longer = join(so_far, jax.tree.map(lambda part: part[position], pieces))
        return jax.tree.map(lambda new, old: jnp.where(position < mine, new, old), longer, so_far)

    return lax.fori_loop(0, count - 1, lap, so_far)


def prefix_2(array, axis, join, neutral):
    count = lax.axis_size(axis)
    place = lax.axis_index(axis)
    ahead = count - 1 - place
    gathered = jax.tree.map(
        lambda a, kind: lax.all_gather(a.astype(kind), axis),
        array,
        jax.tree.map(lambda a: jnp.bfloat16 if a.dtype == jnp.float32 else a.dtype, array),
    )
    state = jax.tree.map(lambda a, e: jnp.zeros_like(a) + jnp.asarray(e, a.dtype), array, neutral)

    def one(lap, state):
        source = count - 1 - lap
        return join(
            state,
            jax.tree.map(
                lambda a, own: lax.dynamic_index_in_dim(a, source, 0, False).astype(own.dtype),
                gathered,
                array,
            ),
        )

    return lax.fori_loop(0, ahead, one, state)


def feature_map(inputs):
    lead = inputs.shape[:-1]
    outer = (inputs[..., :, None] * inputs[..., None, :]).reshape(lead + (FEAT * FEAT,))
    return jnp.concatenate(
        [jnp.ones_like(inputs[..., :1]), inputs * 0.5, outer * OUTER_SCALE], axis=-1
    )


def feature_back(inputs, grads):
    lead = inputs.shape[:-1]
    linear = grads[..., 1 : FEAT + 1] * 0.5
    square = grads[..., FEAT + 1 :].reshape(lead + (FEAT, FEAT))
    both_ways = square + jnp.swapaxes(square, -1, -2)
    return (
        linear + jnp.einsum("...ij,...j->...i", both_ways, inputs, precision=HIGHEST) * OUTER_SCALE
    )


def contract_last(left, right):
    return lax.dot_general(
        left, right, (((1,), (1,)), ((), ())), preferred_element_type=jnp.float32
    )


def contract_first(left, right):
    return lax.dot_general(
        left, right, (((0,), (0,)), ((), ())), preferred_element_type=jnp.float32
    )


def silu_grad(values):
    sigma = jax.nn.sigmoid(values)
    return sigma * (1.0 + values * (1.0 - sigma))


def row_scale(values):
    return lax.rsqrt(jnp.mean(values * values, axis=-1, keepdims=True) + EPSILON)


def body(
    tokens,
    seg_ids,
    valid_mask,
    norm_gain,
    conv_taps,
    mix_in,
    mix_out,
    ffn_gain,
    ffn_in,
    ffn_out,
    grad_out,
):
    row_count = tokens.shape[0]
    model_width = tokens.shape[1]
    qk_width = HEADS * FEAT
    x_full = tokens.astype(jnp.float32)
    id_float = seg_ids.astype(jnp.float32)
    keep_rows = valid_mask.astype(jnp.float32)
    tail_rows, tail_ids = passed_along(
        (x_full[row_count - 2 :], id_float[row_count - 2 :]), "grp", 1
    )
    ext_x = jnp.concatenate([tail_rows, x_full], axis=0)
    ext_ids = jnp.concatenate([tail_ids, id_float], axis=0)
    ext_scale = row_scale(ext_x)
    ext_unit = ext_x * ext_scale
    ext_norm = ext_unit * norm_gain
    normed = ext_norm[2:]
    unit_in = ext_unit[2:]
    scale_in = ext_scale[2:]
    same_one = (ext_ids[1 : row_count + 1] == id_float).astype(jnp.float32)[:, None]
    same_two = (ext_ids[:row_count] == id_float).astype(jnp.float32)[:, None]
    back_one = ext_norm[1 : row_count + 1] * same_one
    back_two = ext_norm[:row_count] * same_two
    conv_out = conv_taps[:, 0] * normed + conv_taps[:, 1] * back_one + conv_taps[:, 2] * back_two
    gated = jax.nn.silu(normed)
    mixed = (conv_out * gated).astype(jnp.bfloat16)
    full_in, full_out = (
        lax.all_gather(mix_in, "grp", axis=0, tiled=True),
        lax.all_gather(mix_out, "grp", axis=0, tiled=True),
    )
    projected = jnp.dot(mixed, full_in, preferred_element_type=jnp.float32)
    queries = projected[:, :qk_width].astype(jnp.bfloat16).reshape(row_count, HEADS, FEAT)
    keys_all = (
        projected[:, qk_width : 2 * qk_width].astype(jnp.bfloat16).reshape(row_count, HEADS, FEAT)
    )
    values = projected[:, 2 * qk_width :].astype(jnp.bfloat16).reshape(row_count, HEADS, VDIM)
    last_id = seg_ids[row_count - 1]
    own_rows = (seg_ids == last_id).astype(jnp.float32) * keep_rows
    key_feat = feature_map(keys_all.astype(jnp.float32))
    key_low = key_feat.astype(jnp.bfloat16)
    own_low = own_rows.astype(jnp.bfloat16)[:, None, None]
    local_state = jnp.einsum(
        "thf,thv->hfv", key_low * own_low, values, preferred_element_type=jnp.float32
    )
    local_total = jnp.einsum("thf,t->hf", key_feat, own_rows, precision=HIGHEST)

    def join_states(earlier, later):
        early_first, early_last, early_state, early_total = earlier
        late_first, late_last, late_state, late_total = later
        passes = jnp.logical_and(
            jnp.logical_or(late_first == late_last, late_first < 0),
            jnp.logical_or(early_last == late_first, late_first < 0),
        )
        factor = passes.astype(jnp.float32)
        return (
            jnp.where(early_first < 0, late_first, early_first),
            jnp.where(late_last < 0, early_last, late_last),
            late_state + factor * early_state,
            late_total + factor * early_total,
        )

    empty_entry = (
        jnp.float32(-1.0),
        jnp.float32(-1.0),
        jnp.zeros((HEADS, PHI, VDIM), jnp.float32),
        jnp.zeros((HEADS, PHI), jnp.float32),
    )
    in_first, in_last, in_state, in_total = prefix(
        (id_float[0], id_float[row_count - 1], local_state, local_total),
        "grp",
        join_states,
        empty_entry,
    )
    carried = (id_float == in_last).astype(jnp.float32)
    positions = jnp.arange(row_count)
    allowed = (
        (positions[:, None] >= positions[None, :]) & (seg_ids[:, None] == seg_ids[None, :])
    ).astype(jnp.float32) * keep_rows[None, :]
    query_heads = jnp.transpose(queries, (1, 0, 2))
    key_heads = jnp.transpose(keys_all, (1, 0, 2))
    value_heads = jnp.transpose(values, (1, 0, 2))

    def head_forward(pieces):
        query_head, key_head, value_head, state_head, total_head = pieces
        scores = contract_last(query_head, key_head) * 0.25
        weights = (1.0 + scores + 0.5 * scores * scores) * allowed
        query_feat = feature_map(query_head.astype(jnp.float32))
        numerator = jnp.dot(
            weights.astype(jnp.bfloat16), value_head, preferred_element_type=jnp.float32
        ) + carried[:, None] * jnp.dot(
            query_feat.astype(jnp.bfloat16),
            state_head.astype(jnp.bfloat16),
            preferred_element_type=jnp.float32,
        )
        denominator = jnp.sum(weights, axis=1) + carried * jnp.dot(
            query_feat, total_head, precision=HIGHEST
        )
        return numerator / jnp.maximum(denominator, 1.0)[:, None]

    head_out = lax.map(head_forward, (query_heads, key_heads, value_heads, in_state, in_total))
    attended = (
        jnp.transpose(head_out, (1, 0, 2)).reshape(row_count, HEADS * VDIM).astype(jnp.bfloat16)
    )
    branch = jnp.dot(attended, full_out, preferred_element_type=jnp.float32)
    residual = x_full + branch
    scale_mid = row_scale(residual)
    unit_mid = residual * scale_mid
    normed_mid = (unit_mid * ffn_gain).astype(jnp.bfloat16)

    def ffn_inner(piece_in):
        gate_val = contract_last(normed_mid, piece_in[:, :model_width])
        up_val = contract_last(normed_mid, piece_in[:, model_width:])
        return (gate_val, up_val)

    pieces = (
        lax.all_gather(ffn_in, "grp", axis=0, tiled=True),
        lax.all_gather(ffn_out, "grp", axis=0, tiled=True),
    )
    gate_val, up_val = ffn_inner(pieces[0])
    activation = (jax.nn.silu(gate_val) * up_val).astype(jnp.bfloat16)
    ffn_result = jnp.dot(activation, pieces[1], preferred_element_type=jnp.float32)
    mixed_out = (residual + ffn_result).astype(jnp.bfloat16)
    sum_input = jnp.sum(keep_rows * jnp.sum(x_full * x_full, axis=1))
    sum_branch = jnp.sum(keep_rows * jnp.sum(branch * branch, axis=1))
    sum_ffn = jnp.sum(keep_rows * jnp.sum(ffn_result * ffn_result, axis=1))
    valid_count = jnp.sum(keep_rows)
    grad_y = grad_out.astype(jnp.float32)
    piece_in = lax.all_gather(ffn_in, "grp", axis=0, tiled=True)
    piece_out = lax.all_gather(ffn_out, "grp", axis=0, tiled=True)
    gate_val, up_val = ffn_inner(piece_in)
    silu_gate = jax.nn.silu(gate_val)
    activation = (silu_gate * up_val).astype(jnp.bfloat16)
    grad_act = contract_last(grad_out, piece_out)
    grad_gate = (grad_act * up_val * silu_grad(gate_val)).astype(jnp.bfloat16)
    grad_up = (grad_act * silu_gate).astype(jnp.bfloat16)
    grad_normed = jnp.dot(
        grad_gate, piece_in[:, :model_width], preferred_element_type=jnp.float32
    ) + jnp.dot(grad_up, piece_in[:, model_width:], preferred_element_type=jnp.float32)
    stacked = jnp.stack([activation, grad_gate, grad_up])
    grad_normed_mid = grad_normed
    grad_unit_mid = grad_normed_mid * ffn_gain
    grad_ffn_gain = jnp.sum(grad_normed_mid * unit_mid, axis=0)
    grad_mid = grad_y + scale_mid * (
        grad_unit_mid - unit_mid * jnp.mean(grad_unit_mid * unit_mid, axis=1, keepdims=True)
    )
    grad_branch = grad_mid.astype(jnp.bfloat16)
    back_in, back_out = (
        lax.all_gather(mix_in, "grp", axis=0, tiled=True),
        lax.all_gather(mix_out, "grp", axis=0, tiled=True),
    )
    grad_att = contract_last(grad_branch, back_out)
    grad_heads = jnp.transpose(grad_att.reshape(row_count, HEADS, VDIM), (1, 0, 2))

    def head_backward(pieces):
        query_head, key_head, value_head, state_head, total_head, grad_head = pieces
        scores = contract_last(query_head, key_head) * 0.25
        weights = (1.0 + scores + 0.5 * scores * scores) * allowed
        weights_low = weights.astype(jnp.bfloat16)
        query_feat = feature_map(query_head.astype(jnp.float32))
        query_low = query_feat.astype(jnp.bfloat16)
        state_low = state_head.astype(jnp.bfloat16)
        numerator = jnp.dot(weights_low, value_head, preferred_element_type=jnp.float32) + carried[
            :, None
        ] * jnp.dot(query_low, state_low, preferred_element_type=jnp.float32)
        denom_raw = jnp.sum(weights, axis=1) + carried * jnp.dot(
            query_feat, total_head, precision=HIGHEST
        )
        denominator = jnp.maximum(denom_raw, 1.0)
        output = numerator / denominator[:, None]
        grad_numer = (grad_head / denominator[:, None]).astype(jnp.bfloat16)
        grad_denom = (
            -jnp.sum(grad_head * output, axis=1)
            / denominator
            * (denom_raw > 1.0).astype(jnp.float32)
        )
        grad_weights = contract_last(grad_numer, value_head) + grad_denom[:, None]
        grad_scores = (grad_weights * allowed * (1.0 + scores)).astype(jnp.bfloat16)
        grad_query = jnp.dot(grad_scores, key_head, preferred_element_type=jnp.float32) * 0.25
        grad_key = contract_first(grad_scores, query_head) * 0.25
        grad_value = contract_first(weights_low, grad_numer)
        grad_kept = grad_numer * carried.astype(jnp.bfloat16)[:, None]
        grad_qfeat = carried[:, None] * (
            contract_last(grad_numer, state_low) + grad_denom[:, None] * total_head[None, :]
        )
        grad_query = grad_query + feature_back(query_head.astype(jnp.float32), grad_qfeat)
        grad_state = contract_first(query_low, grad_kept)
        grad_total = jnp.dot(carried * grad_denom, query_feat, precision=HIGHEST)
        return (grad_query, grad_key, grad_value, grad_state, grad_total)

    head_grads = lax.map(
        head_backward, (query_heads, key_heads, value_heads, in_state, in_total, grad_heads)
    )
    grad_query_h, grad_key_h, grad_value_h, state_grads, total_grads = head_grads

    def join_grads(earlier, later):
        early_pass, early_state, early_total = earlier
        late_pass, late_state, late_total = later
        return (
            late_pass * early_pass,
            late_state + late_pass * early_state,
            late_total + late_pass * early_total,
        )

    grad_empty = (
        jnp.float32(1.0),
        jnp.zeros((HEADS, PHI, VDIM), jnp.float32),
        jnp.zeros((HEADS, PHI), jnp.float32),
    )
    pass_unused, out_state, out_total = prefix_2(
        (carried[row_count - 1], state_grads, total_grads), "grp", join_grads, grad_empty
    )
    own_weight = own_rows[:, None, None]
    grad_kfeat = own_weight * (
        jnp.einsum("thv,hfv->thf", values.astype(jnp.float32), out_state, precision=HIGHEST)
        + out_total[None]
    )
    grad_value_tail = own_weight * jnp.einsum(
        "thf,hfv->thv", key_low.astype(jnp.float32), out_state, precision=HIGHEST
    )
    grad_query_all = jnp.transpose(grad_query_h, (1, 0, 2))
    grad_key_all = jnp.transpose(grad_key_h, (1, 0, 2)) + feature_back(
        keys_all.astype(jnp.float32), grad_kfeat
    )
    grad_value_all = jnp.transpose(grad_value_h, (1, 0, 2)) + grad_value_tail
    grad_projected = jnp.concatenate(
        [
            grad_query_all.reshape(row_count, qk_width),
            grad_key_all.reshape(row_count, qk_width),
            grad_value_all.reshape(row_count, HEADS * VDIM),
        ],
        axis=1,
    ).astype(jnp.bfloat16)
    grad_mixed = contract_last(grad_projected, back_in)
    grad_conv = grad_mixed * gated
    grad_normed = grad_mixed * conv_out * silu_grad(normed)
    next_grad, next_ids = passed_along((grad_conv[:2], id_float[:2]), "grp", -1)
    ext_grad = jnp.concatenate([grad_conv, next_grad], axis=0)
    ext_grad_ids = jnp.concatenate([id_float, next_ids], axis=0)
    ahead_one = (ext_grad_ids[1 : row_count + 1] == id_float).astype(jnp.float32)[:, None]
    ahead_two = (ext_grad_ids[2:] == id_float).astype(jnp.float32)[:, None]
    grad_normed = (
        grad_normed
        + conv_taps[:, 0] * grad_conv
        + conv_taps[:, 1] * (ext_grad[1 : row_count + 1] * ahead_one)
        + conv_taps[:, 2] * (ext_grad[2:] * ahead_two)
    )
    grad_taps = jnp.stack(
        [
            jnp.sum(grad_conv * normed, axis=0),
            jnp.sum(grad_conv * back_one, axis=0),
            jnp.sum(grad_conv * back_two, axis=0),
        ],
        axis=1,
    )
    grad_unit_in = grad_normed * norm_gain
    grad_norm_gain = jnp.sum(grad_normed * unit_in, axis=0)
    grad_tokens = (
        grad_mid
        + scale_in
        * (grad_unit_in - unit_in * jnp.mean(grad_unit_in * unit_in, axis=1, keepdims=True))
    ).astype(jnp.bfloat16)
    in_terms = contract_first(mixed, grad_projected)
    out_terms = contract_first(attended, grad_branch)
    attn_grads = lax.psum_scatter(
        jnp.concatenate([in_terms, out_terms], axis=1).astype(jnp.bfloat16),
        "grp",
        scatter_dimension=0,
        tiled=True,
    ).astype(jnp.float32)
    gate_terms = contract_first(stacked[1], normed_mid)
    up_terms = contract_first(stacked[2], normed_mid)
    down_terms = contract_first(stacked[0], grad_out)
    ffn_grads = lax.psum_scatter(
        jnp.concatenate([gate_terms, up_terms, down_terms], axis=1).astype(jnp.bfloat16),
        "grp",
        scatter_dimension=0,
        tiled=True,
    ).astype(jnp.float32)
    attn_grads, ffn_grads = (
        lax.psum(attn_grads.astype(jnp.bfloat16), "rep").astype(jnp.float32),
        lax.psum(ffn_grads.astype(jnp.bfloat16), "rep").astype(jnp.float32),
    )
    stat_terms = jnp.stack([sum_input, sum_branch, sum_ffn, valid_count])
    grad_norm_gain, grad_taps, grad_ffn_gain, stat_terms = lax.psum(
        (grad_norm_gain, grad_taps, grad_ffn_gain, stat_terms), ("rep", "grp")
    )
    layer_stats = jnp.sqrt(stat_terms[:3] / (jnp.maximum(stat_terms[3], 1.0) * model_width))
    proj_width = 2 * qk_width + HEADS * VDIM
    grad_mix_in = attn_grads[:, :proj_width]
    grad_mix_out = attn_grads[:, proj_width:]
    grad_ffn_in = ffn_grads[:, : 2 * model_width]
    grad_ffn_out = ffn_grads[:, 2 * model_width :]
    return (
        mixed_out,
        grad_tokens,
        grad_norm_gain,
        grad_taps,
        grad_mix_in,
        grad_mix_out,
        grad_ffn_gain,
        grad_ffn_in,
        grad_ffn_out,
        layer_stats,
    )


def solution(mesh):
    placed = (
        P(("rep", "grp"), None),
        P(("rep", "grp")),
        P(("rep", "grp")),
        P(),
        P(),
        P("grp", None),
        P("grp", None),
        P(),
        P("grp", None),
        P("grp", None),
        P(("rep", "grp"), None),
    )
    return jax.shard_map(
        body,
        mesh=mesh,
        in_specs=placed,
        out_specs=(
            P(("rep", "grp"), None),
            P(("rep", "grp"), None),
            P(),
            P(),
            P("grp", None),
            P("grp", None),
            P(),
            P("grp", None),
            P("grp", None),
            P(),
        ),
        check_vma=False,
    )
```

profile of v0, /device:TPU:0, one launch (start us, length us, event | category | flops | bytes accessed | tf_op | source)
XLA Modules:
  0.0 1519.0 jit_solution(8327638019958223831)
XLA Ops:
  30.1 36.4 %all-gather.11.cloned.1.call-done = bf16[1792,2304]{1,0:T(8,128)(2,1)} async-done(((bf16[224,2304]{1,0:T(8,128)(2,1)}), bf16[1792,2304]{1,0:T(8,128)(2,1)}) %all-gather.11.cloned.1.call-update) | async-done | bytes 8257552 | tf_op jit(solution)/shard_map/all_gather | solution.py:141
  88.7 13.6 all-reduce.4
  107.1 12.2 fusion.106
  129.2 13.4 all-gather.17.cloned.1.call-done
  154.3 88.8 %all-gather.19.cloned.1.call-done = f32[128,273,112]{2,0,1:T(8,128)} async-done(((f32[16,273,112]{2,0,1:T(8,128)}), f32[128,273,112]{2,0,1:T(8,128)}) %all-gather.19.cloned.1.call-update) | async-done | bytes 15654928 | tf_op jit(solution)/shard_map/all_gather | solution.py:27
  243.1 74.2 %while.75 = (s32[]{:T(128)}, f32[]{:T(128)}, f32[16,273,112]{2,1,0:T(8,128)}, f32[16,273]{1,0:T(8,128)S(1)}, s32[]{:T(128)}, /*index=5*/f32[8]{0:T(128)S(1)}, f3...) while((s32[]{:T(128)}, f32[]{:T(128)}, f32[16,273,112]{2,1,0:T(8,128)}, ...), condition=%wide.region_2.3_spmd.clone.clone, body=%wide.region_1.2_spmd.clone.sunk.clone | while | flops 1974350 | bytes 9836983 | solution.py:36
  320.6 69.1 %while.73 = (s32[]{:T(128)}, bf16[16,512,112]{1,2,0:T(8,128)(2,1)}, bf16[16,512,16]{1,2,0:T(8,128)(2,1)S(1)}, bf16[16,512,16]{1,2,0:T(8,128)(2,1)S(1)}, bf16[16,...) while((s32[]{:T(128)}, bf16[16,512,112]{1,2,0:T(8,128)(2,1)}, ...), condition=%wide.region_5.6_spmd.clone.clone, body=%wide.region_3.5_spmd.clone.sunk.clone | while | flops 104819712 | bytes 3772173 | solution.py:213
  400.3 19.9 %all-gather.15.cloned.1.call-done = bf16[3584,3584]{1,0:T(8,128)(2,1)} async-done(((bf16[448,3584]{1,0:T(8,128)(2,1)}), bf16[3584,3584]{1,0:T(8,128)(2,1)}) %all-gather.15.cloned.1.call-update) | async-done | bytes 25690128 | tf_op jit(solution)/shard_map/all_gather | solution.py:229
  432.0 17.5 %multiply_convert_fusion.1 = (bf16[512,3584]{1,0:T(8,128)(2,1)}, bf16[512,3584]{1,0:T(8,128)(2,1)}, bf16[512,3584]{1,0:T(8,128)(2,1)}) fusion(f32[512,3584]{1,0:T(8,128)} %fusion.152, f32[512,3584]{1,0:T(8,128)} %fusion.96, bf16[512,1792]{1,0:T(8,128)(2,1)S(1)} %multiply_convert_fusion.3, bf16[3584,3584]{1,0:T(8,128)(2,1)} %all-gather.15.cloned.1.call-done), kind=kOutput, calls=%fused_computation.148 | convolution fusion | flops 6604193792 | bytes 40370176 | tf_op jit(solution)/shard_map/dot_general | solution.py:83
  449.4 13.6 fusion.94
  463.0 15.2 multiply_reduce_fusion.4
  478.2 15.3 %multiply_reduce_fusion.1 = (f32[512]{0:T(512)}, bf16[512,1792]{1,0:T(8,128)(2,1)}, f32[512,1792]{1,0:T(8,128)S(1)}) fusion(f32[512,1792]{1,0:T(8,128)S(1)} %copy-done.13, f32[512]{0:T(512)S(1)} %broadcast_multiply_fusion.5, f32[512,1792]{1,0:T(8,128)} %get-tuple-element.920, f32[1792]{0:T(1024)S(1)} %copy-done.42, f32[512]{0:T(512)S(1)} %add_rsqrt_fusion.1, ...), kind=kOutput, calls=%fused_computation.174 | convolution fusion | flops 6586760704 | bytes 31208448 | tf_op jit(solution)/shard_map/dot_general | solution.py:234
  499.0 284.0 %while.74 = (s32[]{:T(128)}, bf16[16,512,16]{1,2,0:T(8,128)(2,1)S(1)}, f32[16,512,16]{1,2,0:T(8,128)}, f32[16,512,112]{1,2,0:T(8,128)}, bf16[16,273,112]{2,0,1:T...) while((s32[]{:T(128)}, ...), condition=%wide.region_11.12_spmd.clone.clone, body=%wide.region_8.11_spmd.clone.sunk.clone | while | flops 314066944 | bytes 13686121 | solution.py:303
  783.9 12.8 convolution_convert_fusion
  817.0 27.0 %pad_maximum_fusion.5 = bf16[3584,5376]{0,1:T(8,128)(2,1)} fusion(bf16[3584,1792]{0,1:T(8,128)(2,1)} %convolution_convert_fusion, bf16[3584,1792]{0,1:T(8,128)(2,1)} %convolution_convert_fusion.1, bf16[3584,1792]{0,1:T(8,128)(2,1)} %convolution_convert_fusion.2), kind=kLoop, calls=%fused_computation.125 | loop fusion | flops 115605504 | bytes 77070336 | tf_op jit(solution)/shard_map/concatenate | solution.py:387
  844.0 46.0 %copy.81 = bf16[3584,5376]{1,0:T(8,128)(2,1)} copy(bf16[3584,5376]{0,1:T(8,128)(2,1)} %pad_maximum_fusion.5) | data formatting | bytes 77070336
  892.5 14.0 all-reduce.2
  923.2 25.3 %while.72 = (s32[]{:T(128)}, f32[16,273,112]{2,1,0:T(8,128)S(1)}, f32[16,273]{1,0:T(8,128)S(1)}, s32[]{:T(128)}, bf16[8,16,273,112]{3,1,0,2:T(8,128)(2,1)}, /*in...) while((s32[]{:T(128)}, f32[16,273,112]{2,1,0:T(8,128)S(1)}, f32[16,273]{1,0:T(8,128)S(1)}, ...), condition=%wide.region_13.14_spmd.clone, body=%wide.region_12.13_spmd.sunk.clone | while | flops 1480759 | bytes 6892865 | solution.py:61
  960.4 16.0 %fusion.104 = f32[512,16,16]{0,2,1:T(8,128)S(1)} fusion(f32[512,16,16,16]{0,3,2,1:T(8,128)} %bitcast.374, f32[512,16,16]{0,2,1:T(8,128)S(1)} %copy-done.8), kind=kLoop, calls=%fused_computation.144 | loop fusion | flops 6160384 | bytes 9437184 | tf_op jit(solution)/shard_map/...ij,...j->...i/dot_general | solution.py:78
  1001.3 118.1 %reduce-scatter.7.cloned.1.call-done = bf16[448,5376]{1,0:T(8,128)(2,1)} async-done(((bf16[3584,5376]{1,0:T(8,128)(2,1)}), bf16[448,5376]{1,0:T(8,128)(2,1)}) %reduce-scatter.7.cloned.1.call-update) | async-done | bytes 4816912
  1127.1 99.3 %reduce-scatter.5.cloned.1.call-done = bf16[224,4096]{1,0:T(8,128)(2,1)} async-done(((bf16[1792,4096]{1,0:T(8,128)(2,1)}), bf16[224,4096]{1,0:T(8,128)(2,1)}) %reduce-scatter.5.cloned.1.call-update) | async-done | bytes 1835024 | tf_op jit(solution)/shard_map/reduce_scatter | solution.py:377
  1230.6 14.6 multiply_reduce_fusion.7
  1261.4 48.7 %all-reduce.3 = (f32[1792]{0:T(1024)}, f32[1792,3]{0,1:T(4,128)}, f32[1792]{0:T(1024)}, f32[4]{0:T(128)S(1)}) all-reduce(f32[1792]{0:T(1024)S(1)} %get-tuple-element.777, f32[1792,3]{0,1:T(4,128)S(1)} %pad_maximum_fusion.14, f32[1792]{0:T(1024)S(1)} %copy-done.49, ...), channel_id=1, replica_groups=mesh['rep'=4,'grp'=8] {'rep','grp'}, use_global_device_ids=true, to_apply=%region_16.17 | all-reduce | flops 8964 | bytes 71712 | tf_op jit(solution)/shard_map/psum | solution.py:397
  1318.4 169.3 %all-reduce.8.cloned.1.call-done = (bf16[224,4096]{1,0:T(8,128)(2,1)}, bf16[448,5376]{0,1:T(8,128)(2,1)}) async-done(((bf16[224,4096]{1,0:T(8,128)(2,1)}, bf16[448,5376]{0,1:T(8,128)(2,1)}), (bf16[224,4096]{1,0:T(8,128)(2,1)}, bf16[448,5376]{0,1:T(8,128)(2,1)})) %all-reduce.8.cloned.1.call-update) | async-done | bytes 6651920 | tf_op jit(solution)/shard_map/psum | solution.py:393
  (842 shorter events, 657.0 us)
Async XLA Ops:
  7.2 59.3 %all-gather.11.cloned.1.call-start = ((), (), s32[]{:S(2)}) async-start(), calls=%async_computation.2 | async-start | bytes 9289728 | tf_op jit(solution)/shard_map/all_gather | solution.py:141
  8.0 134.6 %all-gather.17.cloned.1.call-start = ((), (), s32[]{:S(2)}) async-start(), calls=%async_computation.5 | async-start | bytes 14450688 | tf_op jit(solution)/shard_map/all_gather | solution.py:230
  8.7 234.4 %all-gather.19.cloned.1.call-start = ((), (), s32[]{:S(2)}) async-start(), calls=%async_computation.7 | async-start | bytes 20127744 | tf_op jit(solution)/shard_map/all_gather | solution.py:27
  9.5 12.0 collective-permute-start
  12.6 8.1 collective-permute-start.3
  13.9 6.8 collective-permute-start.1
  19.9 87.2 %copy-start.37 = (f32[273]{0:T(512)}, f32[273]{0:T(512)S(1)}, u32[]{:S(2)}) copy-start(f32[273]{0:T(512)S(1)} %pad.25.clone) | copy-start | bytes 3280
  20.7 86.4 %copy-start.32 = (f32[512]{0:T(512)}, f32[512]{0:T(512)S(1)}, u32[]{:S(2)}) copy-start(f32[512]{0:T(512)S(1)} %get-tuple-element.887) | copy-start | bytes 6148
  30.1 44.4 %copy-start.17 = (bf16[512,1792]{1,0:T(8,128)(2,1)}, bf16[512,1792]{1,0:T(8,128)(2,1)S(1)}, u32[]{:S(2)}) copy-start(bf16[512,1792]{1,0:T(8,128)(2,1)S(1)} %get-tuple-element.888) | copy-start | bytes 5505028
  79.0 25.5 %copy-start.6 = (bf16[512,1792]{0,1:T(8,128)(2,1)}, bf16[512,1792]{0,1:T(8,128)(2,1)S(1)}, u32[]{:S(2)}) copy-start(bf16[512,1792]{0,1:T(8,128)(2,1)S(1)} %copy.54) | copy-start | bytes 5505028
  79.1 28.0 %copy-start.10 = (f32[512,16,16]{0,2,1:T(8,128)}, f32[512,16,16]{0,2,1:T(8,128)S(1)}, u32[]{:S(2)}) copy-start(f32[512,16,16]{0,2,1:T(8,128)S(1)} %broadcast_multiply_fusion.3) | copy-start | bytes 1572868
  85.5 304.3 %all-gather.13.cloned.1.call-start = ((), (), s32[]{:S(2)}) async-start(), calls=%async_computation.3 | async-start | bytes 7225344 | tf_op jit(solution)/shard_map/all_gather | solution.py:142
  86.1 334.2 %all-gather.15.cloned.1.call-start = ((), (), s32[]{:S(2)}) async-start(), calls=%async_computation.4 | async-start | bytes 28901376 | tf_op jit(solution)/shard_map/all_gather | solution.py:229
  86.6 836.4 %all-gather.21.cloned.1.call-start = ((), (), s32[]{:S(2)}) async-start(), calls=%async_computation.8 | async-start | bytes 10063872 | tf_op jit(solution)/shard_map/all_gather | solution.py:44
  107.1 35.4 %copy-start.55 = (bf16[512,1792]{1,0:T(8,128)(2,1)S(1)}, bf16[512,1792]{1,0:T(8,128)(2,1)}, u32[]{:S(2)}) copy-start(bf16[512,1792]{1,0:T(8,128)(2,1)} %param.29) | copy-start | bytes 5505028
  320.0 69.7 %copy-start.16 = (bf16[512,1792]{1,0:T(8,128)(2,1)S(1)}, bf16[512,1792]{1,0:T(8,128)(2,1)}, u32[]{:S(2)}) copy-start(bf16[512,1792]{1,0:T(8,128)(2,1)} %param.19) | copy-start | bytes 5505028
  400.3 31.7 %copy-start.20 = (bf16[512,1792]{1,0:T(8,128)(2,1)}, bf16[512,1792]{1,0:T(8,128)(2,1)S(1)}, u32[]{:S(2)}) copy-start(bf16[512,1792]{1,0:T(8,128)(2,1)S(1)} %multiply_convert_fusion.3) | copy-start | bytes 5505028
  449.4 44.0 %slice-start.2 = ((s8[6422528]{0:T(1024)(128)(4,1)}), s8[4194304]{0:T(1024)(128)(4,1)S(1)}, s32[]{:S(2)}) async-start(s8[6422528]{0:T(1024)(128)(4,1)} %bitcast.404), calls=%async_computation.13 | async-start | bytes 8388608
  463.0 30.5 %slice-start.3 = ((s8[6422528]{0:T(1024)(128)(4,1)}), s8[2228224]{0:T(1024)(128)(4,1)S(1)}, s32[]{:S(2)}) async-start(s8[6422528]{0:T(1024)(128)(4,1)} %bitcast.404), calls=%async_computation.14 | async-start | bytes 4456448
  783.8 335.6 %reduce-scatter.7.cloned.1.call-start = ((), (), s32[]{:S(2)}) async-start(), calls=%async_computation.9 | async-start | bytes 43352064
  890.0 336.5 %reduce-scatter.5.cloned.1.call-start = ((), (), s32[]{:S(2)}) async-start(), calls=%async_computation.6 | async-start | bytes 16515072 | tf_op jit(solution)/shard_map/reduce_scatter | solution.py:377
  923.2 25.3 %copy-start.33 = (f32[512]{0:T(512)S(1)}, f32[512]{0:T(512)}, u32[]{:S(2)}) copy-start(f32[512]{0:T(512)} %copy-done.32) | copy-start | bytes 6148
  1001.0 486.7 %all-reduce.8.cloned.1.call-start = ((), (), s32[]{:S(2)}) async-start(), calls=%async_computation.10 | async-start | bytes 14680064 | tf_op jit(solution)/shard_map/psum | solution.py:393
  1246.0 3.1 collective-permute-start.2
  (56 other events, 492.5 us)
Sparse Core Ops, SparseCore 0:
  9.9 56.5 all-gather.10
  68.4 74.0 all-gather.16
  145.0 98.0 all-gather.18
  244.8 46.0 all-gather.12
  292.6 127.5 all-gather.14
  783.9 58.4 all-gather.20
  890.1 229.2 reduce-scatter.6
  1122.9 103.5 reduce-scatter.4
  1229.5 258.1 all-reduce.7
where the time goes:
time: 1540 us; the launch traced here: 1520 us
  waiting for transfers between devices  549 us (36%)
  matrix products  453 us (29%)
  local copies, waits for them, and re-layouts  233 us (15%)
  other arithmetic  129 us (8%)
  blocking collectives  94.3 us (6%)
  loops' own time  34.7 us (2%)
  between operations  15.8 us (1%)
    psum x1, waiting for transfers between devices, body(): lax.psum(attn_grads.astype(jnp.bfloat16), 'rep').astype(jnp.float32)  169 us
    dot_general x69, matrix products, contract_last(): lax.dot_general(left, right, (((1,), (1,)), ((), ())), preferred_element_...  122 us
    unnamed x10, waiting for transfers between devices  121 us
    dot_general x53, matrix products, contract_first(): lax.dot_general(left, right, (((0,), (0,)), ((), ())), preferred_element_...  116 us
    reduce_scatter x1, waiting for transfers between devices, body(): lax.psum_scatter(jnp.concatenate([in_terms, out_terms], axis=1).astype(jn...  99.3 us
    all_gather x1, waiting for transfers between devices, prefix(): pieces = jax.tree.map(lambda part: lax.all_gather(part, axis), value)  88.8 us
    dynamic_update_slice x48, local copies, waits for them, and re-layouts, body(): lax.map(head_backward, (query_heads, key_heads, value_heads, in_state, in...  86.1 us
    unnamed x146, local copies, waits for them, and re-layouts  82.8 us
  transfers between devices with their start and end apart: 13, of which 8 were waited for; matrix products, arithmetic and copies ran while one was open for 28% of the time, Pallas kernels for 0%

commit v1 on v0

v1 whole, which is shorter than its diff:
```python
import functools
import math

import jax
import jax.numpy as jnp
import numpy as np
from jax import lax
from jax.experimental import pallas as pl
from jax.experimental.pallas import tpu as pltpu
from jax.sharding import PartitionSpec as P

HEADS = 16
FEAT = 16
VDIM = 112
PAIRS = FEAT * (FEAT + 1) // 2
FROWS = 160
LANES = 128
EXT = 32
EPSILON = 1e-05
OUTER_SCALE = 0.25 / math.sqrt(2.0)
BF = jnp.bfloat16
F32 = jnp.float32
VMEM_LIMIT = 50 * 1024 * 1024


def feature_tables():
    left = np.zeros((FROWS, EXT), np.float32)
    right = np.zeros((FROWS, EXT), np.float32)
    key_scale = np.zeros((FROWS, 1), np.float32)
    query_scale = np.zeros((FROWS, 1), np.float32)
    row = 0
    for i in range(FEAT):
        for j in range(i, FEAT):
            left[row, i] = 1.0
            right[row, j] = 1.0
            key_scale[row] = OUTER_SCALE
            query_scale[row] = OUTER_SCALE * (1.0 if i == j else 2.0)
            row += 1
    for i in range(FEAT):
        left[row, i] = 1.0
        right[row, FEAT] = 1.0
        key_scale[row] = query_scale[row] = 0.5
        row += 1
    left[row, FEAT] = right[row, FEAT] = 1.0
    key_scale[row] = query_scale[row] = 1.0
    return left, right, key_scale, query_scale


def dot(left, right, left_dim, right_dim):
    return lax.dot_general(
        left, right, (((left_dim,), (right_dim,)), ((), ())), preferred_element_type=F32
    )


def extended(vectors):
    rows = lax.broadcasted_iota(jnp.int32, (EXT - FEAT, vectors.shape[1]), 0)
    return jnp.concatenate([vectors, jnp.where(rows == 0, 1.0, 0.0).astype(BF)], axis=0)


def feature_parts(vectors, left, right):
    ext = extended(vectors)
    return dot(left, ext, 1, 0), dot(right, ext, 1, 0)


def padded_values(values):
    return jnp.concatenate(
        [values, jnp.zeros((LANES - VDIM, values.shape[1]), values.dtype)], axis=0
    )


def with_totals(state, total, high_id=None, low_id=None):
    lane = lax.broadcasted_iota(jnp.int32, state.shape, 1)
    high = total.astype(BF).astype(F32)
    out = jnp.where(lane == VDIM, high, state)
    out = jnp.where(lane == VDIM + 1, total - high, out)
    if high_id is not None:
        out = jnp.where(lane == VDIM + 2, high_id, out)
        out = jnp.where(lane == VDIM + 3, low_id, out)
    return out.astype(BF)


def total_of(state):
    lane = lax.broadcasted_iota(jnp.int32, state.shape, 1)
    return jnp.sum(
        jnp.where((lane == VDIM) | (lane == VDIM + 1), state, 0.0), axis=1, keepdims=True
    )


def state_kernel(ids_ref, keys_ref, values_ref, own_ref, left_ref, right_ref, scale_ref, out_ref):
    one, two = feature_parts(keys_ref[...], left_ref[...], right_ref[...])
    feats = one * two * scale_ref[...] * own_ref[...]
    state = dot(feats.astype(BF), padded_values(values_ref[...]), 1, 1)
    total = jnp.sum(feats, axis=1, keepdims=True)
    out_ref[0] = with_totals(state, total, ids_ref[0], ids_ref[1])


def tiles_of(count):
    half = count // 2
    return [(0, half, half), (half, count - half, count)]


def local_kernel(queries_ref, keys_ref, values_ref, allowed_ref, num_ref, den_ref):
    count = queries_ref.shape[1]
    for begin, width, seen in tiles_of(count):
        span = pl.ds(begin, width)
        scores = dot(keys_ref[:, :seen], queries_ref[:, span], 0, 0) * 0.25
        weights = (1.0 + scores + 0.5 * scores * scores) * allowed_ref[:seen, span]
        num_ref[:, span] = dot(values_ref[:, :seen], weights.astype(BF), 1, 0)
        den_ref[0, :, span] = jnp.sum(weights, axis=0, keepdims=True)


def carried_kernel(
    marks_ref, queries_ref, gathered_ref, num_ref, den_ref, cont_ref, left_ref, right_ref,
    scale_ref, attended_ref, output_ref, denom_ref, state_ref,
):
    blocks = gathered_ref.shape[0]
    state = gathered_ref[0, 0].astype(F32) * marks_ref[0]
    for block in range(1, blocks):
        state = state + gathered_ref[block, 0].astype(F32) * marks_ref[block]
    state_ref[0] = state
    total = total_of(state)
    one, two = feature_parts(queries_ref[...], left_ref[...], right_ref[...])
    feats = one * two * scale_ref[...]
    cont = cont_ref[...]
    extra = dot(state.astype(BF), feats.astype(BF), 0, 0)[:VDIM]
    denom = den_ref[0] + cont * jnp.sum(feats * total, axis=0, keepdims=True)
    output = (num_ref[...] + cont * extra) / jnp.maximum(denom, 1.0)
    output_ref[...] = output
    attended_ref[...] = output.astype(BF)
    denom_ref[0] = denom


def state_grad_kernel(
    grad_ref, output_ref, denom_ref, queries_ref, cont_ref, left_ref, right_ref, scale_ref,
    out_ref, dnum_ref, dden_ref,
):
    denom = denom_ref[0]
    floor = jnp.maximum(denom, 1.0)
    grad = grad_ref[...]
    dnum = (grad / floor).astype(BF)
    dden = jnp.where(
        denom > 1.0, -jnp.sum(grad * output_ref[...], axis=0, keepdims=True) / floor, 0.0
    )
    dnum_ref[...] = dnum
    dden_ref[0] = dden
    cont = cont_ref[...]
    one, two = feature_parts(queries_ref[...], left_ref[...], right_ref[...])
    feats = one * two * scale_ref[...]
    state = dot(feats.astype(BF), padded_values(dnum * cont.astype(BF)), 1, 1)
    total = jnp.sum(feats * (cont * dden), axis=1, keepdims=True)
    out_ref[0] = with_totals(state, total)


def feature_back(grads, one, two, scale, left_t, right_t):
    scaled = grads * scale
    return (
        dot(left_t, (scaled * two).astype(BF), 1, 0) + dot(right_t, (scaled * one).astype(BF), 1, 0)
    )[:FEAT]


def local_grad_kernel(
    queries_ref, keys_ref, values_ref, dnum_ref, dden_ref, allowed_ref, state_ref, cont_ref,
    left_ref, right_ref, left_t_ref, right_t_ref, scale_ref, dq_ref, dk_ref, dv_ref,
):
    count = queries_ref.shape[1]
    state = state_ref[0]
    total = total_of(state)
    dnum = dnum_ref[...]
    one, two = feature_parts(queries_ref[...], left_ref[...], right_ref[...])
    grads = cont_ref[...] * (
        dot(state.astype(BF), padded_values(dnum), 1, 0) + total * dden_ref[0]
    )
    carried = feature_back(grads, one, two, scale_ref[...], left_t_ref[...], right_t_ref[...])
    for begin, width, seen in tiles_of(count):
        span = pl.ds(begin, width)
        keys = keys_ref[:, :seen]
        queries = queries_ref[:, span]
        scores = dot(keys, queries, 0, 0) * 0.25
        allowed = allowed_ref[:seen, span]
        weights = ((1.0 + scores + 0.5 * scores * scores) * allowed).astype(BF)
        dnum_part = dnum_ref[:, span]
        dweights = dot(values_ref[:, :seen], dnum_part, 0, 0) + dden_ref[0, :, span]
        dscores = (dweights * allowed * (1.0 + scores)).astype(BF)
        dq = dot(keys, dscores, 1, 0) * 0.25 + carried[:, begin : begin + width]
        dq_ref[:, span] = dq.astype(BF)
        dk = dot(queries, dscores, 1, 1) * 0.25
        dv = dot(dnum_part, weights, 1, 1)
        if begin == 0:
            dk_ref[:, :seen] = dk
            dv_ref[:, :seen] = dv
        else:
            dk_ref[:, :begin] += dk[:, :begin]
            dv_ref[:, :begin] += dv[:, :begin]
            dk_ref[:, span] = dk[:, begin:]
            dv_ref[:, span] = dv[:, begin:]


def late_grad_kernel(
    marks_ref, gathered_ref, keys_ref, values_ref, own_ref, dk_in_ref, dv_in_ref, left_ref,
    right_ref, left_t_ref, right_t_ref, scale_ref, dk_ref, dv_ref,
):
    blocks = gathered_ref.shape[0]
    state = gathered_ref[0, 0].astype(F32) * marks_ref[0]
    for block in range(1, blocks):
        state = state + gathered_ref[block, 0].astype(F32) * marks_ref[block]
    total = total_of(state)
    low = state.astype(BF)
    own = own_ref[...]
    one, two = feature_parts(keys_ref[...], left_ref[...], right_ref[...])
    feats = (one * two * scale_ref[...]).astype(BF)
    grads = own * (dot(low, padded_values(values_ref[...]), 1, 0) + total)
    back = feature_back(grads, one, two, scale_ref[...], left_t_ref[...], right_t_ref[...])
    dk_ref[...] = (dk_in_ref[...] + back).astype(BF)
    dv_ref[...] = (dv_in_ref[...] + own * dot(low, feats, 0, 0)[:VDIM]).astype(BF)


def ffn_kernel(x_ref, dy_ref, w_in_ref, w_out_ref, act_ref, gate_ref, up_ref, back_ref):
    width = x_ref.shape[1]
    x = x_ref[...]
    gate = dot(x, w_in_ref[:, :width], 1, 1)
    up = dot(x, w_in_ref[:, width:], 1, 1)
    dact = dot(dy_ref[...], w_out_ref[...], 1, 1)
    sigma = 1.0 / (1.0 + jnp.exp(-gate))
    silu = gate * sigma
    act_ref[...] = (silu * up).astype(BF)
    dgate = (dact * up * (sigma * (1.0 + gate * (1.0 - sigma)))).astype(BF)
    dup = (dact * silu).astype(BF)
    gate_ref[...] = dgate
    up_ref[...] = dup
    back_ref[...] = (
        dot(dgate, w_in_ref[:, :width], 1, 0) + dot(dup, w_in_ref[:, width:], 1, 0)
    ).astype(BF)


def ffn_grad_kernel(
    x_ref, dy_ref, act_ref, gate_ref, up_ref, w_out_ref, result_ref, grads_ref, total_ref
):
    width = x_ref.shape[1]
    step = pl.program_id(0)
    act = act_ref[...]
    result_ref[...] = dot(act, w_out_ref[...], 1, 0).astype(BF)
    terms = (
        (gate_ref[...], x_ref[...]),
        (up_ref[...], x_ref[...]),
        (act, dy_ref[...]),
    )
    for place, (left, right) in enumerate(terms):
        span = pl.ds(place * width, width)
        term = dot(left, right, 0, 0)

        @pl.when(step == 0)
        def _():
            total_ref[:, span] = term

        @pl.when(step > 0)
        def _():
            total_ref[:, span] += term

    @pl.when(step == pl.num_programs(0) - 1)
    def _():
        grads_ref[...] = total_ref[...].astype(BF)


def call(kernel, outs, grid, in_specs, out_specs, flops, moved, *args, scratch=()):
    return pl.pallas_call(
        kernel,
        out_shape=outs,
        grid=grid,
        in_specs=in_specs,
        out_specs=out_specs,
        scratch_shapes=list(scratch),
        compiler_params=pltpu.CompilerParams(vmem_limit_bytes=VMEM_LIMIT),
        cost_estimate=pl.CostEstimate(flops=flops, bytes_accessed=moved, transcendentals=0),
    )(*args)


def passed_along(block, axis, distance):
    devices = range(lax.axis_size(axis))
    route = [(i - distance, i) for i in devices if i - distance in devices]
    return lax.ppermute(block, axis, route)


def silu_grad(values):
    sigma = jax.nn.sigmoid(values)
    return sigma * (1.0 + values * (1.0 - sigma))


def row_scale(values):
    return lax.rsqrt(jnp.mean(values * values, axis=-1, keepdims=True) + EPSILON)


def rep_sum(terms):
    count = lax.axis_size("rep")
    mine = lax.axis_index("rep")
    rows = terms.shape[0] // count

    def part(index):
        return lax.dynamic_slice_in_dim(terms, lax.rem(index + count, count) * rows, rows, 0)

    total = part(mine).astype(F32)
    for shift in range(1, count):
        route = [(i, (i + shift) % count) for i in range(count)]
        total = total + lax.ppermute(part(mine + shift), "rep", route).astype(F32)
    low = total.astype(BF)
    whole = jnp.zeros(terms.shape, F32)
    whole = lax.dynamic_update_slice_in_dim(whole, low.astype(F32), mine * rows, 0)
    for shift in range(1, count):
        route = [(i, (i + shift) % count) for i in range(count)]
        other = lax.ppermute(low, "rep", route).astype(F32)
        whole = lax.dynamic_update_slice_in_dim(
            whole, other, lax.rem(mine - shift + count, count) * rows, 0
        )
    return whole


def body(
    tokens, seg_ids, valid_mask, norm_gain, conv_taps, mix_in, mix_out, ffn_gain, ffn_in, ffn_out,
    grad_out,
):
    row_count, model_width = tokens.shape
    group = lax.axis_size("grp")
    mine = lax.axis_index("grp")
    qk_width = HEADS * FEAT
    v_width = HEADS * VDIM
    hidden = ffn_in.shape[0]

    full_in = lax.all_gather(mix_in, "grp", axis=0, tiled=True)
    full_out = lax.all_gather(mix_out, "grp", axis=0, tiled=True)
    all_dy = lax.all_gather(grad_out, "grp", axis=0, tiled=True)

    x_full = tokens.astype(F32)
    id_float = seg_ids.astype(F32)
    keep_rows = valid_mask.astype(F32)
    edge = jnp.concatenate([x_full[row_count - 2 :], id_float[row_count - 2 :, None]], axis=1)
    edge = passed_along(edge, "grp", 1)
    ext_x = jnp.concatenate([edge[:, :model_width], x_full], axis=0)
    ext_ids = jnp.concatenate([edge[:, model_width], id_float], axis=0)
    ext_scale = row_scale(ext_x)
    ext_unit = ext_x * ext_scale
    ext_norm = ext_unit * norm_gain
    normed = ext_norm[2:]
    unit_in = ext_unit[2:]
    scale_in = ext_scale[2:]
    same_one = (ext_ids[1 : row_count + 1] == id_float).astype(F32)[:, None]
    same_two = (ext_ids[:row_count] == id_float).astype(F32)[:, None]
    back_one = ext_norm[1 : row_count + 1] * same_one
    back_two = ext_norm[:row_count] * same_two
    conv_out = conv_taps[:, 0] * normed + conv_taps[:, 1] * back_one + conv_taps[:, 2] * back_two
    gated = jax.nn.silu(normed)
    mixed = (conv_out * gated).astype(BF)

    positions = jnp.arange(row_count)
    allowed = (
        (positions[:, None] <= positions[None, :]) & (seg_ids[:, None] == seg_ids[None, :])
    ).astype(F32) * keep_rows[:, None]
    last_id = seg_ids[row_count - 1]
    own = ((seg_ids == last_id).astype(F32) * keep_rows)[None, :]
    left, right, key_scale, query_scale = feature_tables()
    left_low, right_low = jnp.asarray(left, BF), jnp.asarray(right, BF)
    left_t, right_t = jnp.asarray(left.T, BF), jnp.asarray(right.T, BF)
    key_scale, query_scale = jnp.asarray(key_scale), jnp.asarray(query_scale)

    def whole(*shape):
        return pl.BlockSpec(shape, lambda h: (0,) * len(shape))

    smem = pl.BlockSpec(memory_space=pltpu.SMEM)
    qk_spec = pl.BlockSpec((FEAT, row_count), lambda h: (h, 0))
    k_spec = pl.BlockSpec((FEAT, row_count), lambda h: (HEADS + h, 0))
    v_spec = pl.BlockSpec((VDIM, row_count), lambda h: (h, 0))
    row_spec = pl.BlockSpec((1, 1, row_count), lambda h: (h, 0, 0))
    state_spec = pl.BlockSpec((1, FROWS, LANES), lambda h: (h, 0, 0))
    all_states_spec = pl.BlockSpec((group, 1, FROWS, LANES), lambda h: (0, h, 0, 0))
    one_row = whole(1, row_count)
    square = whole(row_count, row_count)
    table = whole(FROWS, EXT)
    table_t = whole(EXT, FROWS)
    column = whole(FROWS, 1)
    grid = (HEADS,)
    v_low = jax.ShapeDtypeStruct((v_width, row_count), BF)
    v_wide = jax.ShapeDtypeStruct((v_width, row_count), F32)
    qk_low = jax.ShapeDtypeStruct((qk_width, row_count), BF)
    qk_wide = jax.ShapeDtypeStruct((qk_width, row_count), F32)
    head_rows = jax.ShapeDtypeStruct((HEADS, 1, row_count), F32)
    states_low = jax.ShapeDtypeStruct((HEADS, FROWS, LANES), BF)
    states_wide = jax.ShapeDtypeStruct((HEADS, FROWS, LANES), F32)

    qk = dot(full_in[:, : 2 * qk_width], mixed, 0, 1).astype(BF)
    values = dot(full_in[:, 2 * qk_width :], mixed, 0, 1).astype(BF)

    id_pieces = jnp.stack([last_id // 256, last_id % 256]).astype(F32)
    states = call(
        state_kernel, states_low, grid,
        [smem, k_spec, v_spec, one_row, table, table, column], state_spec,
        10**9, 4 * 10**6,
        id_pieces, qk, values, own, left_low, right_low, key_scale,
    )
    all_states = lax.all_gather(states, "grp", axis=0)
    num_local, den_local = call(
        local_kernel, (v_wide, head_rows), grid,
        [qk_spec, k_spec, v_spec, square], (v_spec, row_spec),
        15 * 10**9, 7 * 10**6,
        qk, qk, values, allowed,
    )
    id_parts = all_states[:, 0, 0, VDIM + 2 : VDIM + 4].astype(F32)
    last_ids = id_parts[:, 0] * 256.0 + id_parts[:, 1]
    order = jnp.arange(group)
    before = jnp.where(mine > 0, last_ids[jnp.maximum(mine - 1, 0)], -1.0)
    marks = ((order < mine) & (last_ids == before)).astype(F32)
    cont = (id_float == before).astype(F32)[None, :]
    attended, output, denom, state_in = call(
        carried_kernel, (v_low, v_wide, head_rows, states_wide), grid,
        [smem, qk_spec, all_states_spec, v_spec, row_spec, one_row, table, table, column],
        (v_spec, v_spec, row_spec, state_spec),
        2 * 10**9, 16 * 10**6,
        marks, qk, all_states, num_local, den_local, cont, left_low, right_low, query_scale,
    )
    branch = dot(attended, full_out, 0, 0)
    residual = x_full + branch
    scale_mid = row_scale(residual)
    unit_mid = residual * scale_mid
    normed_mid = (unit_mid * ffn_gain).astype(BF)

    all_mid = lax.all_gather(normed_mid, "grp", axis=0, tiled=True)
    tile = row_count
    steps = group
    wide_tile = pl.BlockSpec((tile, model_width), lambda i: (i, 0))
    thin_tile = pl.BlockSpec((tile, hidden), lambda i: (i, 0))
    thin = jax.ShapeDtypeStruct((row_count * group, hidden), BF)
    wide = jax.ShapeDtypeStruct((row_count * group, model_width), BF)
    w_in_spec = whole(hidden, 2 * model_width)
    w_out_spec = whole(hidden, model_width)
    unit = 2 * row_count * group * hidden * model_width
    activation, dgate, dup, back_terms = call(
        ffn_kernel, (thin, thin, thin, wide), (steps,),
        [wide_tile, wide_tile, w_in_spec, w_out_spec],
        (thin_tile, thin_tile, thin_tile, wide_tile),
        5 * unit, 60 * 10**6,
        all_mid, all_dy, ffn_in, ffn_out,
    )
    grad_normed_mid = lax.psum_scatter(
        back_terms, "grp", scatter_dimension=0, tiled=True
    ).astype(F32)
    result_terms, ffn_grads = call(
        ffn_grad_kernel, (wide, jax.ShapeDtypeStruct((hidden, 3 * model_width), BF)), (steps,),
        [wide_tile, wide_tile, thin_tile, thin_tile, thin_tile, w_out_spec],
        (wide_tile, whole(hidden, 3 * model_width)),
        4 * unit, 60 * 10**6,
        all_mid, all_dy, activation, dgate, dup, ffn_out,
        scratch=[pltpu.VMEM((hidden, 3 * model_width), F32)],
    )
    ffn_result = lax.psum_scatter(
        result_terms, "grp", scatter_dimension=0, tiled=True
    ).astype(F32)
    mixed_out = (residual + ffn_result).astype(BF)
    ffn_grads = rep_sum(ffn_grads)

    grad_y = grad_out.astype(F32)
    grad_unit_mid = grad_normed_mid * ffn_gain
    grad_ffn_gain = jnp.sum(grad_normed_mid * unit_mid, axis=0)
    grad_mid = grad_y + scale_mid * (
        grad_unit_mid - unit_mid * jnp.mean(grad_unit_mid * unit_mid, axis=1, keepdims=True)
    )
    grad_branch = grad_mid.astype(BF)
    grad_att = dot(full_out, grad_branch, 1, 1)
    out_terms = dot(attended, grad_branch, 1, 0).astype(BF)
    out_shard = lax.psum_scatter(out_terms, "grp", scatter_dimension=0, tiled=True)
    grad_mix_out = rep_sum(out_shard)

    state_grads, dnum, dden = call(
        state_grad_kernel, (states_low, v_low, head_rows), grid,
        [v_spec, v_spec, row_spec, qk_spec, one_row, table, table, column],
        (state_spec, v_spec, row_spec),
        2 * 10**9, 12 * 10**6,
        grad_att, output, denom, qk, cont, left_low, right_low, query_scale,
    )
    all_state_grads = lax.all_gather(state_grads, "grp", axis=0)
    grad_queries, dk_local, dv_local = call(
        local_grad_kernel, (qk_low, qk_wide, v_wide), grid,
        [qk_spec, k_spec, v_spec, v_spec, row_spec, square, state_spec, one_row,
         table, table, table_t, table_t, column],
        (qk_spec, qk_spec, v_spec),
        30 * 10**9, 12 * 10**6,
        qk, qk, values, dnum, dden, allowed, state_in, cont,
        left_low, right_low, left_t, right_t, query_scale,
    )
    previous_ids = jnp.concatenate([jnp.full((1,), -1.0, F32), last_ids[:-1]])
    late_marks = ((order > mine) & (previous_ids == last_ids[mine])).astype(F32)
    grad_keys, grad_values = call(
        late_grad_kernel, (qk_low, v_low), grid,
        [smem, all_states_spec, k_spec, v_spec, one_row, qk_spec, v_spec,
         table, table, table_t, table_t, column],
        (qk_spec, v_spec),
        2 * 10**9, 14 * 10**6,
        late_marks, all_state_grads, qk, values, own, dk_local, dv_local,
        left_low, right_low, left_t, right_t, key_scale,
    )
    grad_projected = jnp.concatenate([grad_queries, grad_keys, grad_values], axis=0)
    in_terms = dot(mixed, grad_projected, 0, 1).astype(BF)
    in_shard = lax.psum_scatter(in_terms, "grp", scatter_dimension=0, tiled=True)
    grad_mix_in = rep_sum(in_shard)

    grad_mixed = dot(grad_projected, full_in, 0, 1)
    grad_conv = grad_mixed * gated
    grad_normed = grad_mixed * conv_out * silu_grad(normed)
    edge_back = jnp.concatenate([grad_conv[:2], id_float[:2, None]], axis=1)
    edge_back = passed_along(edge_back, "grp", -1)
    ext_grad = jnp.concatenate([grad_conv, edge_back[:, :model_width]], axis=0)
    ext_grad_ids = jnp.concatenate([id_float, edge_back[:, model_width]], axis=0)
    ahead_one = (ext_grad_ids[1 : row_count + 1] == id_float).astype(F32)[:, None]
    ahead_two = (ext_grad_ids[2:] == id_float).astype(F32)[:, None]
    grad_normed = (
        grad_normed
        + conv_taps[:, 0] * grad_conv
        + conv_taps[:, 1] * (ext_grad[1 : row_count + 1] * ahead_one)
        + conv_taps[:, 2] * (ext_grad[2:] * ahead_two)
    )
    grad_unit_in = grad_normed * norm_gain
    grad_tokens = (
        grad_mid
        + scale_in
        * (grad_unit_in - unit_in * jnp.mean(grad_unit_in * unit_in, axis=1, keepdims=True))
    ).astype(BF)

    stat_terms = jnp.stack(
        [
            jnp.sum(keep_rows * jnp.sum(x_full * x_full, axis=1)),
            jnp.sum(keep_rows * jnp.sum(branch * branch, axis=1)),
            jnp.sum(keep_rows * jnp.sum(ffn_result * ffn_result, axis=1)),
            jnp.sum(keep_rows),
        ]
    )
    small = jnp.concatenate(
        [
            jnp.sum(grad_normed * unit_in, axis=0),
            jnp.sum(grad_conv * normed, axis=0),
            jnp.sum(grad_conv * back_one, axis=0),
            jnp.sum(grad_conv * back_two, axis=0),
            grad_ffn_gain,
            stat_terms,
        ]
    )
    small = jnp.pad(small, (0, -small.shape[0] % 1024)).reshape(-1, LANES)
    small = jnp.sum(lax.all_gather(small, ("rep", "grp"), axis=0), axis=0).reshape(-1)
    rows = small[: 5 * model_width].reshape(5, model_width)
    stats = small[5 * model_width : 5 * model_width + 4]
    layer_stats = jnp.sqrt(stats[:3] / (jnp.maximum(stats[3], 1.0) * model_width))
    return (
        mixed_out,
        grad_tokens,
        rows[0],
        rows[1:4].T,
        grad_mix_in,
        grad_mix_out,
        rows[4],
        ffn_grads[:, : 2 * model_width],
        ffn_grads[:, 2 * model_width :],
        layer_stats,
    )


def solution(mesh):
    split = P(("rep", "grp"), None)
    shard = P("grp", None)
    return jax.shard_map(
        body,
        mesh=mesh,
        in_specs=(
            split, P(("rep", "grp")), P(("rep", "grp")), P(), P(), shard, shard, P(), shard, shard,
            split,
        ),
        out_specs=(split, split, P(), P(), shard, shard, P(), shard, shard, P()),
        check_vma=False,
    )
```

time: 1540 us -> 1030 us (0.67)
  matrix products: 453 us -> 56.6 us
  local copies, waits for them, and re-layouts: 233 us -> 45.9 us
  Pallas kernels: 0 us -> 176 us
  blocking collectives: 94.3 us -> 0 us
  other arithmetic: 129 us -> 55.4 us
  waiting for transfers between devices: 549 us -> 602 us
  starting transfers between devices: 10.7 us -> 62.2 us
  loops' own time: 34.7 us -> 0 us
    dot_general x259 -> x7, matrix products: 453 us -> 56.6 us  [dot(): lax.dot_general(left, right, (((left_dim,), (right_dim,)), ((), ())), pre...]
    pallas_call x0 -> x8, Pallas kernels: none -> 176 us  [call(): pl.pallas_call(kernel, out_shape=outs, grid=grid, in_specs=in_specs, out_...]
    ppermute x0 -> x18, waiting for transfers between devices: none -> 170 us  [the longest x9 97.1 us: rep_sum(): other = lax.ppermute(low, 'rep', route).astype(F32)]
    psum x1 -> x0, waiting for transfers between devices: 169 us -> none  [body(): lax.psum(attn_grads.astype(jnp.bfloat16), 'rep').astype(jnp.float32)]
    unnamed x10 -> x11, waiting for transfers between devices: 121 us -> 2.02 us
    all_gather x6 -> x7, waiting for transfers between devices: 158 us -> 270 us  [the longest x1 83.3 us: body(): all_mid = lax.all_gather(normed_mid, 'grp', axis=0, tiled=True)]
    dynamic_update_slice x48 -> x0, local copies, waits for them, and re-layouts: 86.1 us -> none  [body(): lax.map(head_backward, (query_heads, key_heads, value_heads, in_state, in...]
    unnamed x146 -> x106, local copies, waits for them, and re-layouts: 82.8 us -> 13 us
  transfers between devices with their start and end apart: 13 -> 31, of which waited for: 8 -> 17; matrix products, arithmetic and copies ran while one was open for 28% -> 12% of each run, Pallas kernels for 0% -> 11%
where the time goes in v1:
time: 1030 us; the launch traced here: 1020 us
  waiting for transfers between devices  602 us (58%)
  Pallas kernels  176 us (17%)
  starting transfers between devices  62.2 us (6%)
  matrix products  56.6 us (5%)
  other arithmetic  55.4 us (5%)
  local copies, waits for them, and re-layouts  45.9 us (4%)
  between operations  19 us (2%)
    pallas_call x8, Pallas kernels, call(): pl.pallas_call(kernel, out_shape=outs, grid=grid, in_specs=in_specs, out_...  176 us
    reduce_scatter x1, waiting for transfers between devices, body(): lax.psum_scatter(result_terms, 'grp', scatter_dimension=0, tiled=True)  103 us
    ppermute x9, waiting for transfers between devices, rep_sum(): other = lax.ppermute(low, 'rep', route).astype(F32)  97.1 us
    all_gather x1, waiting for transfers between devices, body(): all_mid = lax.all_gather(normed_mid, 'grp', axis=0, tiled=True)  83.3 us
    ppermute x9, waiting for transfers between devices, rep_sum(): total = total + lax.ppermute(part(mine + shift), 'rep', route).astype(F32)  72.6 us
    all_gather x1, waiting for transfers between devices, body(): all_dy = lax.all_gather(grad_out, 'grp', axis=0, tiled=True)  70.5 us
    dot_general x7, matrix products, dot(): lax.dot_general(left, right, (((left_dim,), (right_dim,)), ((), ())), pre...  56.6 us
    reduce_scatter x1, waiting for transfers between devices, body(): lax.psum_scatter(back_terms, 'grp', scatter_dimension=0, tiled=True)  54.9 us
  transfers between devices with their start and end apart: 31, of which 17 were waited for; matrix products, arithmetic and copies ran while one was open for 12% of the time, Pallas kernels for 11%

profile of v1, /device:TPU:0, one launch (start us, length us, event | category | flops | bytes accessed | tf_op | source)
XLA Modules:
  0.0 1016.5 jit_solution(16015787880511469096)
XLA Ops:
  29.7 36.8 %all-gather.10.cloned.1.call-done = bf16[1792,2304]{1,0:T(8,128)(2,1)} async-done(((bf16[224,2304]{1,0:T(8,128)(2,1)}), bf16[1792,2304]{1,0:T(8,128)(2,1)}) %all-gather.10.cloned.1.call-update) | async-done | bytes 8257552 | tf_op jit(solution)/shard_map/all_gather | solution.py:327
  87.4 10.3 %shard_map.241 = (f32[1792,512]{1,0:T(8,128)}, f32[16,1,512]{2,1,0:T(1,128)S(1)}) custom-call(bf16[512,512]{1,0:T(8,128)(2,1)S(1)} %fusion.30.keys_ref.queries_ref, bf16[512,512]{1,0:T(8,128)(2,1)S(1)} %fusion.30.keys_ref.queries_ref, bf16[1792,512]{1,0:T(8,128)(2,1)S(1)} %fusion.22.values_ref, f32[512,512]{1,0:T(8,128)S(1)} %fusion.34.allowed_ref), custom_call_target="tpu_custom_call" | custom-call | flops 15000000512 | bytes 7000000 | tf_op jit(solution)/shard_map/pallas_call | solution.py:265
  97.7 28.8 %all-gather.20.cloned.1.call-done = bf16[128,160,128]{2,1,0:T(8,128)(2,1)} async-done(((bf16[16,160,128]{2,1,0:T(8,128)(2,1)}), bf16[128,160,128]{2,1,0:T(8,128)(2,1)}) %all-gather.20.cloned.1.call-update) | async-done | bytes 5242896 | tf_op jit(solution)/shard_map/all_gather | solution.py:397
  129.6 14.1 %shard_map.242 = (bf16[1792,512]{1,0:T(8,128)(2,1)S(1)}, f32[1792,512]{1,0:T(8,128)}, f32[16,1,512]{2,1,0:T(1,128)S(1)}, f32[16,160,128]{2,1,0:T(8,128)S(1)}) custom-call(f32[8]{0:T(128)S(1)} %fusion.42.marks_ref, bf16[512,512]{1,0:T(8,128)(2,1)S(1)} %fusion.30.keys_ref.queries_ref, bf16[8,16,160,128]{3,2,1,0:T(8,128)(2,1)} %bitcast.55, ...), custom_call_target="tpu_custom_call" | custom-call | flops 2000000000 | bytes 16000000 | tf_op jit(solution)/shard_map/pallas_call | solution.py:265
  144.9 29.7 %all-gather.12.cloned.1.call-done = bf16[1792,1792]{1,0:T(8,128)(2,1)} async-done(((bf16[224,1792]{1,0:T(8,128)(2,1)}), bf16[1792,1792]{1,0:T(8,128)(2,1)}) %all-gather.12.cloned.1.call-update) | async-done | bytes 6422544 | tf_op jit(solution)/shard_map/all_gather | solution.py:328
  186.9 70.5 %all-gather.16.cloned.1.call-done.dy_ref = bf16[4096,1792]{1,0:T(8,128)(2,1)} async-done(((bf16[512,1792]{1,0:T(8,128)(2,1)}), bf16[4096,1792]{1,0:T(8,128)(2,1)}) %all-gather.16.cloned.1.call-update) | async-done | bytes 14680080 | tf_op jit(solution)/shard_map/all_gather | solution.py:329
  257.4 83.3 %all-gather.14.cloned.1.call-done.x_ref = bf16[4096,1792]{1,0:T(8,128)(2,1)} async-done(((bf16[512,1792]{1,0:T(8,128)(2,1)}), bf16[4096,1792]{1,0:T(8,128)(2,1)}) %all-gather.14.cloned.1.call-update) | async-done | bytes 14680080 | tf_op jit(solution)/shard_map/all_gather | solution.py:423
  340.7 45.3 %shard_map.243 = (bf16[4096,448]{1,0:T(8,128)(2,1)}, bf16[4096,448]{1,0:T(8,128)(2,1)}, bf16[4096,448]{1,0:T(8,128)(2,1)}, bf16[4096,1792]{1,0:T(8,128)(2,1)}) custom-call(bf16[4096,1792]{1,0:T(8,128)(2,1)} %all-gather.14.cloned.1.call-done.x_ref, bf16[4096,1792]{1,0:T(8,128)(2,1)} %all-gather.16.cloned.1.call-done.dy_ref, bf16[448,3584]{1,0:T(8,128)(2,1)} %w_in_ref.1, ...), custom_call_target="tpu_custom_call" | custom-call | flops 32883343360 | bytes 60000000 | tf_op jit(solution)/shard_map/pallas_call | solution.py:265
  386.2 48.5 %shard_map.244 = (bf16[4096,1792]{1,0:T(8,128)(2,1)}, bf16[448,5376]{1,0:T(8,128)(2,1)}) custom-call(bf16[4096,1792]{1,0:T(8,128)(2,1)} %all-gather.14.cloned.1.call-done.x_ref, bf16[4096,1792]{1,0:T(8,128)(2,1)} %all-gather.16.cloned.1.call-done.dy_ref, bf16[4096,448]{1,0:T(8,128)(2,1)} %get-tuple-element.33.act_ref, ...), custom_call_target="tpu_custom_call" | custom-call | flops 26306674688 | bytes 60000000 | tf_op jit(solution)/shard_map/pallas_call | solution.py:265
  434.9 54.9 %reduce-scatter.7.cloned.1.call-done = bf16[512,1792]{1,0:T(8,128)(2,1)} async-done(((bf16[4096,1792]{1,0:T(8,128)(2,1)}), bf16[512,1792]{1,0:T(8,128)(2,1)}) %reduce-scatter.7.cloned.1.call-update) | async-done | bytes 1835024 | tf_op jit(solution)/shard_map/reduce_scatter | solution.py:440
  493.4 103.4 %reduce-scatter.5.cloned.1.call-done = bf16[512,1792]{1,0:T(8,128)(2,1)} async-done(((bf16[4096,1792]{1,0:T(8,128)(2,1)}), bf16[512,1792]{1,0:T(8,128)(2,1)}) %reduce-scatter.5.cloned.1.call-update) | async-done | bytes 1835024 | tf_op jit(solution)/shard_map/reduce_scatter | solution.py:451
  601.9 9.7 convolution_bitcast_fusion.grad_ref
  611.6 13.2 %shard_map.245 = (bf16[16,160,128]{2,1,0:T(8,128)(2,1)}, bf16[1792,512]{1,0:T(8,128)(2,1)S(1)}, f32[16,1,512]{2,1,0:T(1,128)S(1)}) custom-call(f32[1792,512]{1,0:T(8,128)} %convolution_bitcast_fusion.grad_ref, f32[1792,512]{1,0:T(8,128)} %get-tuple-element.38.output_ref, f32[16,1,512]{2,1,0:T(1,128)S(1)} %get-tuple-element.39.denom_ref, ...), custom_call_target="tpu_custom_call" | custom-call | flops 2000000000 | bytes 12000000 | tf_op jit(solution)/shard_map/pallas_call | solution.py:265
  645.7 21.0 %shard_map.246 = (bf16[256,512]{1,0:T(8,128)(2,1)S(1)}, f32[256,512]{1,0:T(8,128)S(1)}, f32[1792,512]{1,0:T(8,128)}) custom-call(bf16[512,512]{1,0:T(8,128)(2,1)S(1)} %fusion.30.keys_ref.queries_ref, bf16[512,512]{1,0:T(8,128)(2,1)S(1)} %fusion.30.keys_ref.queries_ref, bf16[1792,512]{1,0:T(8,128)(2,1)} %copy-done, bf16[1792,512]{1,0:T(8,128)(2,1)} %copy-done.11, ...), custom_call_target="tpu_custom_call" | custom-call | flops 30000001024 | bytes 12000000 | tf_op jit(solution)/shard_map/pallas_call | solution.py:265
  667.5 14.3 %shard_map.247 = (bf16[256,512]{1,0:T(8,128)(2,1)S(1)}, bf16[1792,512]{1,0:T(8,128)(2,1)S(1)}) custom-call(f32[8]{0:T(128)S(1)} %and_convert_fusion.marks_ref, bf16[8,16,160,128]{3,2,1,0:T(8,128)(2,1)} %bitcast.56, bf16[512,512]{1,0:T(8,128)(2,1)S(1)} %fusion.30.keys_ref.queries_ref, bf16[1792,512]{1,0:T(8,128)(2,1)} %copy-done, f32[1,512]{1,0:T(1,128)S(1)} %bitcast.53, ...), custom_call_target="tpu_custom_call" | custom-call | flops 2000000000 | bytes 14000000 | tf_op jit(solution)/shard_map/pallas_call | solution.py:265
  691.3 55.5 %collective-permute-done.15 = bf16[112,5376]{1,0:T(8,128)(2,1)} collective-permute-done((bf16[112,5376]{1,0:T(8,128)(2,1)}, bf16[112,5376]{1,0:T(8,128)(2,1)}, u32[]{:S(2)}, u32[]{:S(2)}) %collective-permute-start.15) | collective-permute-done | bytes 1204256 | tf_op jit(solution)/shard_map/ppermute | solution.py:303
  762.9 25.3 %collective-permute-done.17 = bf16[112,5376]{1,0:T(8,128)(2,1)S(1)} collective-permute-done((bf16[112,5376]{1,0:T(8,128)(2,1)S(1)}, bf16[112,5376]{1,0:T(8,128)(2,1)S(1)}, u32[]{:S(2)}, u32[]{:S(2)}) %collective-permute-start.17) | collective-permute-done | bytes 1204256 | tf_op jit(solution)/shard_map/ppermute | solution.py:309
  789.9 48.2 %collective-permute-done.18 = bf16[112,5376]{1,0:T(8,128)(2,1)S(1)} collective-permute-done((bf16[112,5376]{1,0:T(8,128)(2,1)S(1)}, bf16[112,5376]{1,0:T(8,128)(2,1)S(1)}, u32[]{:S(2)}, u32[]{:S(2)}) %collective-permute-start.18) | collective-permute-done | bytes 1204256 | tf_op jit(solution)/shard_map/ppermute | solution.py:309
  851.4 13.1 %multiply_reduce_fusion.3 = (f32[1792]{0:T(1024)S(1)}, f32[1792]{0:T(1024)S(1)}, f32[1792]{0:T(1024)S(1)}, f32[512,1792]{1,0:T(8,128)}, f32[512,1792]{1,0:T(8,128)}) fusion(f32[514,1792]{1,0:T(8,128)S(1)} %copy-done.17, f32[512]{0:T(512)S(1)} %copy-done.48, f32[512]{0:T(512)S(1)} %copy-done.46, bf16[2304,512]{1,0:T(8,128)(2,1)} %copy-done.38, ...), kind=kOutput, calls=%fused_computation.32 | convolution fusion | flops 4239780608 | bytes 28992512 | tf_op jit(solution)/shard_map/dot_general | solution.py:50
  868.6 12.3 %multiply_reduce_fusion.6 = (f32[1792]{0:T(1024)S(1)}, f32[512]{0:T(512)S(1)}, f32[512,1792]{1,0:T(8,128)}) fusion(f32[514,1792]{1,0:T(8,128)S(1)} %copy-done.19, f32[1792]{0:T(1024)S(1)} %copy-done.35, f32[512]{0:T(512)S(1)} %get-tuple-element.95, f32[2,1792]{1,0:T(2,128)S(1)} %slice.176, f32[512,1792]{1,0:T(8,128)} %get-tuple-element.70, ...), kind=kLoop, calls=%fused_computation.35 | loop fusion | flops 22017792 | bytes 22076416 | tf_op jit(solution)/shard_map/reduce_sum | solution.py:534
  885.6 27.8 %collective-permute-start.10 = (bf16[56,1792]{1,0:T(8,128)(2,1)S(1)}, bf16[56,1792]{1,0:T(8,128)(2,1)S(1)}, u32[]{:S(2)}, u32[]{:S(2)}) collective-permute-start(bf16[56,1792]{1,0:T(8,128)(2,1)S(1)} %get-tuple-element.90), channel_id=1, source_target_pairs={{0,24},{8,0},{16,8},{24,16},{1,25},{9,1},{17,9},{25,17},{2,26},{10... | collective-permute-start | bytes 602120 | tf_op jit(solution)/shard_map/ppermute | solution.py:303
  918.2 13.0 %collective-permute-done.9 = bf16[56,1792]{1,0:T(8,128)(2,1)S(1)} collective-permute-done((bf16[56,1792]{1,0:T(8,128)(2,1)S(1)}, bf16[56,1792]{1,0:T(8,128)(2,1)S(1)}, u32[]{:S(2)}, u32[]{:S(2)}) %collective-permute-start.9) | collective-permute-done | bytes 200736 | tf_op jit(solution)/shard_map/ppermute | solution.py:303
  961.4 21.4 %all-gather.18.cloned.1.call-done = f32[32,72,128]{2,1,0:T(8,128)} async-done(((f32[1,72,128]{2,1,0:T(8,128)}), f32[32,72,128]{2,1,0:T(8,128)}) %all-gather.18.cloned.1.call-update) | async-done | bytes 1179664 | tf_op jit(solution)/shard_map/all_gather | solution.py:543
  997.7 10.3 %collective-permute-done.6 = bf16[56,2304]{1,0:T(8,128)(2,1)S(1)} collective-permute-done((bf16[56,2304]{1,0:T(8,128)(2,1)S(1)}, bf16[56,2304]{1,0:T(8,128)(2,1)S(1)}, u32[]{:S(2)}, u32[]{:S(2)}) %collective-permute-start.6) | collective-permute-done | bytes 258080 | tf_op jit(solution)/shard_map/ppermute | solution.py:309
  (244 shorter events, 186.7 us)
Async XLA Ops:
  7.2 59.3 %all-gather.10.cloned.1.call-start = ((), (), s32[]{:S(2)}) async-start(), calls=%async_computation.4 | async-start | bytes 9289728 | tf_op jit(solution)/shard_map/all_gather | solution.py:327
  7.9 118.7 %all-gather.20.cloned.1.call-start = ((), (), s32[]{:S(2)}) async-start(), calls=%async_computation.13 | async-start | bytes 5898240 | tf_op jit(solution)/shard_map/all_gather | solution.py:397
  85.3 89.3 %all-gather.12.cloned.1.call-start = ((), (), s32[]{:S(2)}) async-start(), calls=%async_computation.5 | async-start | bytes 7225344 | tf_op jit(solution)/shard_map/all_gather | solution.py:328
  86.0 171.3 %all-gather.16.cloned.1.call-start = ((), (), s32[]{:S(2)}) async-start(), calls=%async_computation.7 | async-start | bytes 16515072 | tf_op jit(solution)/shard_map/all_gather | solution.py:329
  86.6 254.1 %all-gather.14.cloned.1.call-start = ((), (), s32[]{:S(2)}) async-start(), calls=%async_computation.6 | async-start | bytes 16515072 | tf_op jit(solution)/shard_map/all_gather | solution.py:423
  186.9 302.9 %reduce-scatter.7.cloned.1.call-start = ((), (), s32[]{:S(2)}) async-start(), calls=%async_computation.9 | async-start | bytes 16515072 | tf_op jit(solution)/shard_map/reduce_scatter | solution.py:440
  386.0 210.8 %reduce-scatter.5.cloned.1.call-start = ((), (), s32[]{:S(2)}) async-start(), calls=%async_computation.8 | async-start | bytes 16515072 | tf_op jit(solution)/shard_map/reduce_scatter | solution.py:451
  434.8 232.7 %all-gather.22.cloned.1.call-start = ((), (), s32[]{:S(2)}) async-start(), calls=%async_computation.14 | async-start | bytes 5898240 | tf_op jit(solution)/shard_map/all_gather | solution.py:476
  626.1 258.2 %reduce-scatter.11.cloned.1.call-start = ((), (), s32[]{:S(2)}) async-start(), calls=%async_computation.12 | async-start | bytes 7225344 | tf_op jit(solution)/shard_map/reduce_scatter | solution.py:466
  635.1 318.3 %reduce-scatter.9.cloned.1.call-start = ((), (), s32[]{:S(2)}) async-start(), calls=%async_computation.11 | async-start | bytes 9289728 | tf_op jit(solution)/shard_map/reduce_scatter | solution.py:499
  639.9 51.4 %collective-permute-start.16 = (bf16[112,5376]{1,0:T(8,128)(2,1)}, bf16[112,5376]{1,0:T(8,128)(2,1)}, u32[]{:S(2)}, u32[]{:S(2)}) collective-permute-start(bf16[112,5376]{1,0:T(8,128)(2,1)} %get-tuple-element.77), channel_id=1, source_target_pairs={{0,24},{8,0},{16,8},{24,16},{1,25},{9,1},{17,9},{25,17},{2,26},{10... | collective-permute-start | bytes 3612680 | tf_op jit(solution)/shard_map/ppermute | solution.py:303
  643.3 103.5 %collective-permute-start.15 = (bf16[112,5376]{1,0:T(8,128)(2,1)}, bf16[112,5376]{1,0:T(8,128)(2,1)}, u32[]{:S(2)}, u32[]{:S(2)}) collective-permute-start(bf16[112,5376]{1,0:T(8,128)(2,1)} %get-tuple-element.78), channel_id=1, source_target_pairs={{0,16},{8,24},{16,0},{24,8},{1,17},{9,25},{17,1},{25,9},{2,18},{10... | collective-permute-start | bytes 3612680 | tf_op jit(solution)/shard_map/ppermute | solution.py:303
  643.3 103.5 %collective-permute-start.14 = (bf16[112,5376]{1,0:T(8,128)(2,1)}, bf16[112,5376]{1,0:T(8,128)(2,1)}, u32[]{:S(2)}, u32[]{:S(2)}) collective-permute-start(bf16[112,5376]{1,0:T(8,128)(2,1)} %get-tuple-element.76), channel_id=1, source_target_pairs={{0,8},{8,16},{16,24},{24,0},{1,9},{9,17},{17,25},{25,1},{2,10},{10... | collective-permute-start | bytes 3612680 | tf_op jit(solution)/shard_map/ppermute | solution.py:303
  691.2 291.5 %all-gather.18.cloned.1.call-start = ((), (), s32[]{:S(2)}) async-start(), calls=%async_computation.10 | async-start | bytes 1216512 | tf_op jit(solution)/shard_map/all_gather | solution.py:543
  756.9 31.4 %collective-permute-start.17 = (bf16[112,5376]{1,0:T(8,128)(2,1)S(1)}, bf16[112,5376]{1,0:T(8,128)(2,1)S(1)}, u32[]{:S(2)}, u32[]{:S(2)}) collective-permute-start(bf16[112,5376]{1,0:T(8,128)(2,1)S(1)} %get-tuple-element.65), channel_id=1, source_target_pairs={{0,8},{8,16},{16,24},{24,0},{1,9},{9,17},{17,25},{25,1},{2,10},{10... | collective-permute-start | bytes 3612680 | tf_op jit(solution)/shard_map/ppermute | solution.py:309
  758.2 79.9 %collective-permute-start.18 = (bf16[112,5376]{1,0:T(8,128)(2,1)S(1)}, bf16[112,5376]{1,0:T(8,128)(2,1)S(1)}, u32[]{:S(2)}, u32[]{:S(2)}) collective-permute-start(bf16[112,5376]{1,0:T(8,128)(2,1)S(1)} %get-tuple-element.65), channel_id=1, source_target_pairs={{0,16},{8,24},{16,0},{24,8},{1,17},{9,25},{17,1},{25,9},{2,18},{10... | collective-permute-start | bytes 3612680 | tf_op jit(solution)/shard_map/ppermute | solution.py:309
  759.7 79.9 %collective-permute-start.19 = (bf16[112,5376]{1,0:T(8,128)(2,1)S(1)}, bf16[112,5376]{1,0:T(8,128)(2,1)S(1)}, u32[]{:S(2)}, u32[]{:S(2)}) collective-permute-start(bf16[112,5376]{1,0:T(8,128)(2,1)S(1)} %get-tuple-element.65), channel_id=1, source_target_pairs={{0,24},{8,0},{16,8},{24,16},{1,25},{9,1},{17,9},{25,17},{2,26},{10... | collective-permute-start | bytes 3612680 | tf_op jit(solution)/shard_map/ppermute | solution.py:309
  885.6 32.6 %collective-permute-start.10 = (bf16[56,1792]{1,0:T(8,128)(2,1)S(1)}, bf16[56,1792]{1,0:T(8,128)(2,1)S(1)}, u32[]{:S(2)}, u32[]{:S(2)}) collective-permute-start(bf16[56,1792]{1,0:T(8,128)(2,1)S(1)} %get-tuple-element.90), channel_id=1, source_target_pairs={{0,24},{8,0},{16,8},{24,16},{1,25},{9,1},{17,9},{25,17},{2,26},{10... | collective-permute-start | bytes 602120 | tf_op jit(solution)/shard_map/ppermute | solution.py:303
  913.4 17.7 %collective-permute-start.9 = (bf16[56,1792]{1,0:T(8,128)(2,1)S(1)}, bf16[56,1792]{1,0:T(8,128)(2,1)S(1)}, u32[]{:S(2)}, u32[]{:S(2)}) collective-permute-start(bf16[56,1792]{1,0:T(8,128)(2,1)S(1)} %get-tuple-element.91), channel_id=1, source_target_pairs={{0,16},{8,24},{16,0},{24,8},{1,17},{9,25},{17,1},{25,9},{2,18},{10... | collective-permute-start | bytes 602120 | tf_op jit(solution)/shard_map/ppermute | solution.py:303
  941.2 20.1 %collective-permute-start.13 = (bf16[56,1792]{1,0:T(8,128)(2,1)S(1)}, bf16[56,1792]{1,0:T(8,128)(2,1)S(1)}, u32[]{:S(2)}, u32[]{:S(2)}) collective-permute-start(bf16[56,1792]{1,0:T(8,128)(2,1)S(1)} %get-tuple-element.67), channel_id=1, source_target_pairs={{0,24},{8,0},{16,8},{24,16},{1,25},{9,1},{17,9},{25,17},{2,26},{10... | collective-permute-start | bytes 602120 | tf_op jit(solution)/shard_map/ppermute | solution.py:309
  954.7 30.6 %collective-permute-start.4 = (bf16[56,2304]{1,0:T(8,128)(2,1)S(1)}, bf16[56,2304]{1,0:T(8,128)(2,1)S(1)}, u32[]{:S(2)}, u32[]{:S(2)}) collective-permute-start(bf16[56,2304]{1,0:T(8,128)(2,1)S(1)} %get-tuple-element.87), channel_id=1, source_target_pairs={{0,24},{8,0},{16,8},{24,16},{1,25},{9,1},{17,9},{25,17},{2,26},{10... | collective-permute-start | bytes 774152 | tf_op jit(solution)/shard_map/ppermute | solution.py:303
  960.7 24.6 %collective-permute-start.3 = (bf16[56,2304]{1,0:T(8,128)(2,1)S(1)}, bf16[56,2304]{1,0:T(8,128)(2,1)S(1)}, u32[]{:S(2)}, u32[]{:S(2)}) collective-permute-start(bf16[56,2304]{1,0:T(8,128)(2,1)S(1)} %get-tuple-element.88), channel_id=1, source_target_pairs={{0,16},{8,24},{16,0},{24,8},{1,17},{9,25},{17,1},{25,9},{2,18},{10... | collective-permute-start | bytes 774152 | tf_op jit(solution)/shard_map/ppermute | solution.py:303
  960.7 24.7 %collective-permute-start.2 = (bf16[56,2304]{1,0:T(8,128)(2,1)S(1)}, bf16[56,2304]{1,0:T(8,128)(2,1)S(1)}, u32[]{:S(2)}, u32[]{:S(2)}) collective-permute-start(bf16[56,2304]{1,0:T(8,128)(2,1)S(1)} %get-tuple-element.86), channel_id=1, source_target_pairs={{0,8},{8,16},{16,24},{24,0},{1,9},{9,17},{17,25},{25,1},{2,10},{10... | collective-permute-start | bytes 774152 | tf_op jit(solution)/shard_map/ppermute | solution.py:303
  989.8 18.2 %collective-permute-start.6 = (bf16[56,2304]{1,0:T(8,128)(2,1)S(1)}, bf16[56,2304]{1,0:T(8,128)(2,1)S(1)}, u32[]{:S(2)}, u32[]{:S(2)}) collective-permute-start(bf16[56,2304]{1,0:T(8,128)(2,1)S(1)} %get-tuple-element.69), channel_id=1, source_target_pairs={{0,16},{8,24},{16,0},{24,8},{1,17},{9,25},{17,1},{25,9},{2,18},{10... | collective-permute-start | bytes 774152 | tf_op jit(solution)/shard_map/ppermute | solution.py:309
  (59 other events, 847.4 us)
Sparse Core Ops, SparseCore 0:
  9.9 56.5 all-gather.9
  85.4 41.1 all-gather.19
  128.5 46.0 all-gather.11
  176.3 80.9 all-gather.15
  259.7 80.9 all-gather.13
  386.1 103.5 reduce-scatter.6
  493.2 103.5 reduce-scatter.4
  626.2 41.0 all-gather.21
  670.8 62.4 reduce-scatter.10
  736.7 70.6 reduce-scatter.8
  884.4 98.2 all-gather.17

commit v2 on v1

--- a/solution.py
+++ b/solution.py
@@ -109,14 +109,22 @@
         den_ref[0, :, span] = jnp.sum(weights, axis=0, keepdims=True)
 
 
-def carried_kernel(
-    marks_ref, queries_ref, gathered_ref, num_ref, den_ref, cont_ref, left_ref, right_ref,
-    scale_ref, attended_ref, output_ref, denom_ref, state_ref,
-):
-    blocks = gathered_ref.shape[0]
-    state = gathered_ref[0, 0].astype(F32) * marks_ref[0]
-    for block in range(1, blocks):
-        state = state + gathered_ref[block, 0].astype(F32) * marks_ref[block]
+def marked_sum(marks_ref, gathered_refs):
+    place = 0
+    total = None
+    for ref in gathered_refs:
+        for slot in range(ref.shape[0]):
+            term = ref[slot, 0].astype(F32) * marks_ref[place]
+            total = term if total is None else total + term
+            place += 1
+    return total
+
+
+def carried_kernel(stacks, marks_ref, *refs):
+    gathered_refs = refs[:stacks]
+    (queries_ref, num_ref, den_ref, cont_ref, left_ref, right_ref,
+     scale_ref, attended_ref, output_ref, denom_ref, state_ref) = refs[stacks:]
+    state = marked_sum(marks_ref, gathered_refs)
     state_ref[0] = state
     total = total_of(state)
     one, two = feature_parts(queries_ref[...], left_ref[...], right_ref[...])
@@ -195,14 +203,11 @@
             dv_ref[:, span] = dv[:, begin:]
 
 
-def late_grad_kernel(
-    marks_ref, gathered_ref, keys_ref, values_ref, own_ref, dk_in_ref, dv_in_ref, left_ref,
-    right_ref, left_t_ref, right_t_ref, scale_ref, dk_ref, dv_ref,
-):
-    blocks = gathered_ref.shape[0]
-    state = gathered_ref[0, 0].astype(F32) * marks_ref[0]
-    for block in range(1, blocks):
-        state = state + gathered_ref[block, 0].astype(F32) * marks_ref[block]
+def late_grad_kernel(stacks, marks_ref, *refs):
+    gathered_refs = refs[:stacks]
+    (keys_ref, values_ref, own_ref, dk_in_ref, dv_in_ref, left_ref, right_ref, left_t_ref,
+     right_t_ref, scale_ref, dk_ref, dv_ref) = refs[stacks:]
+    state = marked_sum(marks_ref, gathered_refs)
     total = total_of(state)
     low = state.astype(BF)
     own = own_ref[...]
@@ -214,7 +219,7 @@
     dv_ref[...] = (dv_in_ref[...] + own * dot(low, feats, 0, 0)[:VDIM]).astype(BF)
 
 
-def ffn_kernel(x_ref, dy_ref, w_in_ref, w_out_ref, act_ref, gate_ref, up_ref, back_ref):
+def ffn_kernel(x_ref, dy_ref, w_in_ref, w_out_ref, act_ref, pre_ref, back_ref):
     width = x_ref.shape[1]
     x = x_ref[...]
     gate = dot(x, w_in_ref[:, :width], 1, 1)
@@ -222,43 +227,114 @@
     dact = dot(dy_ref[...], w_out_ref[...], 1, 1)
     sigma = 1.0 / (1.0 + jnp.exp(-gate))
     silu = gate * sigma
-    act_ref[...] = (silu * up).astype(BF)
+    act_ref[0] = (silu * up).astype(BF)
     dgate = (dact * up * (sigma * (1.0 + gate * (1.0 - sigma)))).astype(BF)
     dup = (dact * silu).astype(BF)
-    gate_ref[...] = dgate
-    up_ref[...] = dup
+    pre_ref[0] = dgate
+    pre_ref[1] = dup
     back_ref[...] = (
         dot(dgate, w_in_ref[:, :width], 1, 0) + dot(dup, w_in_ref[:, width:], 1, 0)
     ).astype(BF)
 
 
-def ffn_grad_kernel(
-    x_ref, dy_ref, act_ref, gate_ref, up_ref, w_out_ref, result_ref, grads_ref, total_ref
+def weight_grad_kernel(pieces, *refs):
+    lefts, rights, outs = refs[:pieces], refs[pieces : 2 * pieces], refs[2 * pieces :]
+    total = None
+    for left, right in zip(lefts, rights):
+        term = dot(left[0], right[...], 0, 0)
+        total = term if total is None else total + term
+    rows = outs[0].shape[0]
+    for place, out_ref in enumerate(outs):
+        out_ref[...] = total[place * rows : (place + 1) * rows].astype(BF)
+
+
+def mid_grad_kernel(terms, *refs):
+    term_refs = refs[:terms]
+    residual_ref, grad_ref, gain_ref, mid_ref, branch_ref, gain_grad_ref = refs[terms:]
+    grad = term_refs[0][...].astype(F32)
+    for term_ref in term_refs[1:]:
+        grad = grad + term_ref[...].astype(F32)
+    residual = residual_ref[...]
+    scale = lax.rsqrt(jnp.mean(residual * residual, axis=1, keepdims=True) + EPSILON)
+    unit = residual * scale
+    product = grad * unit
+    part = jnp.sum(product, axis=0, keepdims=True)
+    step = pl.program_id(0)
+
+    @pl.when(step == 0)
+    def _():
+        gain_grad_ref[...] = part
+
+    @pl.when(step > 0)
+    def _():
+        gain_grad_ref[...] += part
+
+    gain = gain_ref[...]
+    mean = jnp.mean(product * gain, axis=1, keepdims=True)
+    mid = grad_ref[...].astype(F32) + scale * (grad * gain - unit * mean)
+    mid_ref[...] = mid
+    branch_ref[...] = mid.astype(BF)
+
+
+def conv_grad_kernel(
+    x_ref, before_ref, after_ref, scale_ref, flags_ref, gain_ref, taps_ref, mixed_ref, mid_ref,
+    out_ref, sums_ref, scaled_ref,
 ):
-    width = x_ref.shape[1]
-    step = pl.program_id(0)
-    act = act_ref[...]
-    result_ref[...] = dot(act, w_out_ref[...], 1, 0).astype(BF)
-    terms = (
-        (gate_ref[...], x_ref[...]),
-        (up_ref[...], x_ref[...]),
-        (act, dy_ref[...]),
-    )
-    for place, (left, right) in enumerate(terms):
-        span = pl.ds(place * width, width)
-        term = dot(left, right, 0, 0)
-
-        @pl.when(step == 0)
-        def _():
-            total_ref[:, span] = term
-
-        @pl.when(step > 0)
-        def _():
-            total_ref[:, span] += term
-
-    @pl.when(step == pl.num_programs(0) - 1)
-    def _():
-        grads_ref[...] = total_ref[...].astype(BF)
+    count, width = x_ref.shape
+    cut = LANES
+    row = lax.broadcasted_iota(jnp.int32, (count, cut), 0)
+
+    def spread(column):
+        return jnp.broadcast_to(column, (count, cut))
+
+    scale = spread(scale_ref[...])
+    same_one, same_two = spread(flags_ref[:, 0:1]), spread(flags_ref[:, 1:2])
+    ahead_one, ahead_two = spread(flags_ref[:, 2:3]), spread(flags_ref[:, 3:4])
+
+    def one_cut(index, total):
+        span = pl.ds(pl.multiple_of(index * cut, cut), cut)
+        gain = gain_ref[:, span]
+        unit = x_ref[:, span].astype(F32) * scale
+        normed = unit * gain
+        older, newer = before_ref[0:1, span], before_ref[1:2, span]
+        back_one = jnp.where(row == 0, newer, pltpu.roll(normed, 1, 0)) * same_one
+        back_two = pltpu.roll(normed, 2, 0)
+        back_two = jnp.where(row == 0, older, jnp.where(row == 1, newer, back_two)) * same_two
+        tap_0, tap_1, tap_2 = taps_ref[0:1, span], taps_ref[1:2, span], taps_ref[2:3, span]
+        conv = tap_0 * normed + tap_1 * back_one + tap_2 * back_two
+        sigma = 1.0 / (1.0 + jnp.exp(-normed))
+        mixed = mixed_ref[:, span]
+        grad_conv = mixed * (normed * sigma)
+        next_0, next_1 = after_ref[0:1, span], after_ref[1:2, span]
+        on_one = jnp.where(row == count - 1, next_0, pltpu.roll(grad_conv, count - 1, 0))
+        on_two = pltpu.roll(grad_conv, count - 2, 0)
+        on_two = jnp.where(
+            row == count - 2, next_0, jnp.where(row == count - 1, next_1, on_two)
+        )
+        grad = (
+            mixed * conv * (sigma * (1.0 + normed * (1.0 - sigma)))
+            + tap_0 * grad_conv
+            + tap_1 * (on_one * ahead_one)
+            + tap_2 * (on_two * ahead_two)
+        )
+        product = grad * unit
+        sums_ref[0:1, span] = jnp.sum(product, axis=0, keepdims=True)
+        sums_ref[1:2, span] = jnp.sum(grad_conv * normed, axis=0, keepdims=True)
+        sums_ref[2:3, span] = jnp.sum(grad_conv * back_one, axis=0, keepdims=True)
+        sums_ref[3:4, span] = jnp.sum(grad_conv * back_two, axis=0, keepdims=True)
+        scaled_ref[:, span] = grad * gain
+        return total + product * gain
+
+    total = lax.fori_loop(0, width // cut, one_cut, jnp.zeros((count, cut), F32))
+    mean = spread(jnp.sum(total, axis=1, keepdims=True) * (1.0 / width))
+
+    def second(index, carry):
+        span = pl.ds(pl.multiple_of(index * cut, cut), cut)
+        unit = x_ref[:, span].astype(F32) * scale
+        out_ref[:, span] = (mid_ref[:, span] + scale * (scaled_ref[:, span] - unit * mean)).astype(BF)
+        return carry
+
+    lax.fori_loop(0, width // cut, second, 0)
 
 
 def call(kernel, outs, grid, in_specs, out_specs, flops, moved, *args, scratch=()):
@@ -270,7 +346,7 @@
         out_specs=out_specs,
         scratch_shapes=list(scratch),
         compiler_params=pltpu.CompilerParams(vmem_limit_bytes=VMEM_LIMIT),
-        cost_estimate=pl.CostEstimate(flops=flops, bytes_accessed=moved, transcendentals=0),
+        cost_estimate=pl.CostEstimate(flops=0, bytes_accessed=0, transcendentals=0),
     )(*args)
 
 
@@ -289,28 +365,136 @@
     return lax.rsqrt(jnp.mean(values * values, axis=-1, keepdims=True) + EPSILON)
 
 
-def rep_sum(terms):
+def exchanged(block, offset):
+    count = lax.axis_size("grp")
+    return lax.ppermute(block, "grp", [(i, i ^ offset) for i in range(count)])
+
+
+def paired():
+    return lax.axis_size("grp") == 8
+
+
+def gather_near(block):
+    if not paired():
+        offsets = list(range(lax.axis_size("grp")))
+        return offsets, [block] + [exchanged(block, k) for k in offsets[1:]]
+    return [0, 2, 4, 6], [block, exchanged(block, 2), exchanged(block, 4)]
+
+
+def far_halves(pieces):
+    if not paired():
+        return []
+    half = pieces[0].shape[0] // 2
+    return [exchanged(pieces[1][:half], 4), exchanged(pieces[2][half:], 2)]
+
+
+def with_far(pieces, halves):
+    return pieces + [jnp.concatenate(halves, axis=0)] if halves else pieces
+
+
+def butterfly_sum(values):
+    for axis in ("grp", "rep"):
+        count = lax.axis_size(axis)
+        step = 1
+        while step < count:
+            route = [(i, i ^ step) for i in range(count)]
+            values = values + lax.ppermute(values, axis, route)
+            step *= 2
+    return values
+
+
+def stack_near(block):
+    offsets = (2, 4, 6) if paired() else range(1, lax.axis_size("grp"))
+    return [exchanged(block, k) for k in offsets]
+
+
+def stack_all(block, near):
+    near = jnp.stack([block, *near])
+    return [near, exchanged(near, 1)] if paired() else [near]
+
+
+def stack_offsets():
+    return [0, 2, 4, 6, 1, 3, 5, 7] if paired() else list(range(lax.axis_size("grp")))
+
+
+def rep_swap(block, step):
     count = lax.axis_size("rep")
-    mine = lax.axis_index("rep")
-    rows = terms.shape[0] // count
-
-    def part(index):
-        return lax.dynamic_slice_in_dim(terms, lax.rem(index + count, count) * rows, rows, 0)
-
-    total = part(mine).astype(F32)
-    for shift in range(1, count):
-        route = [(i, (i + shift) % count) for i in range(count)]
-        total = total + lax.ppermute(part(mine + shift), "rep", route).astype(F32)
-    low = total.astype(BF)
-    whole = jnp.zeros(terms.shape, F32)
-    whole = lax.dynamic_update_slice_in_dim(whole, low.astype(F32), mine * rows, 0)
-    for shift in range(1, count):
-        route = [(i, (i + shift) % count) for i in range(count)]
-        other = lax.ppermute(low, "rep", route).astype(F32)
-        whole = lax.dynamic_update_slice_in_dim(
-            whole, other, lax.rem(mine - shift + count, count) * rows, 0
-        )
-    return whole
+    return lax.ppermute(block, "rep", [(i, i ^ step) for i in range(count)])
+
+
+def rep_steps():
+    count = lax.axis_size("rep")
+    steps = [1 << bit for bit in range(count.bit_length() - 1)]
+    return steps, steps[::-1]
+
+
+def halves_of(blocks, step):
+    bit = (lax.axis_index("rep") // step) % 2
+    rows = blocks[0].shape[0] // 2
+
+    def total(place):
+        parts = [lax.dynamic_slice_in_dim(b, place * rows, rows, 0) for b in blocks]
+        if len(parts) == 1:
+            return parts[0]
+        return sum(p.astype(F32) for p in parts).astype(BF)
+
+    return total(bit), total(1 - bit)
+
+
+def added(one, two):
+    return (one.astype(F32) + two.astype(F32)).astype(BF)
+
+
+def joined(block, other, step):
+    bit = (lax.axis_index("rep") // step) % 2
+    return jnp.where(
+        bit == 0,
+        jnp.concatenate([block, other], axis=0),
+        jnp.concatenate([other, block], axis=0),
+    )
+
+
+class SumQueue:
+    def __init__(self, orders, parts):
+        self.parts = list(parts)
+        self.order = orders[0]
+        self.plans = [self.plan(order, 1) for order in orders]
+        self.start()
+
+    @staticmethod
+    def plan(order, skipped):
+        return [(step, True) for step in order][skipped:] + [(step, False) for step in order[::-1]]
+
+    def start(self):
+        self.moved, self.kept = [], []
+        for place, plan in enumerate(self.plans):
+            keep = send = self.parts[place]
+            if plan and plan[0][1]:
+                keep, send = halves_of([keep], plan[0][0])
+            self.kept.append(keep)
+            self.moved.append(rep_swap(send, plan[0][0]) if plan else None)
+
+    def end(self):
+        for place, plan in enumerate(self.plans):
+            if plan:
+                step, halving = plan.pop(0)
+                merge = added if halving else functools.partial(joined, step=step)
+                self.parts[place] = merge(self.kept[place], self.moved[place])
+
+    def turn(self, value, late=None):
+        value, self.moved = lax.optimization_barrier((value, self.moved))
+        self.end()
+        if late is not None:
+            self.parts.append(late)
+            self.plans.append(self.plan(self.order, 0))
+        self.start()
+        return value
+
+    def finish(self):
+        while any(self.plans):
+            self.end()
+            self.start()
+        return self.parts
 
 
 def body(
@@ -318,7 +502,6 @@
     grad_out,
 ):
     row_count, model_width = tokens.shape
-    group = lax.axis_size("grp")
     mine = lax.axis_index("grp")
     qk_width = HEADS * FEAT
     v_width = HEADS * VDIM
@@ -326,7 +509,11 @@
 
     full_in = lax.all_gather(mix_in, "grp", axis=0, tiled=True)
     full_out = lax.all_gather(mix_out, "grp", axis=0, tiled=True)
-    all_dy = lax.all_gather(grad_out, "grp", axis=0, tiled=True)
+    if paired():
+        w_in = jnp.concatenate([ffn_in, exchanged(ffn_in, 1)], axis=0)
+        w_out = jnp.concatenate([ffn_out, exchanged(ffn_out, 1)], axis=0)
+    else:
+        w_in, w_out = ffn_in, ffn_out
 
     x_full = tokens.astype(F32)
     id_float = seg_ids.astype(F32)
@@ -348,6 +535,7 @@
     conv_out = conv_taps[:, 0] * normed + conv_taps[:, 1] * back_one + conv_taps[:, 2] * back_two
     gated = jax.nn.silu(normed)
     mixed = (conv_out * gated).astype(BF)
+    mixed, w_in, w_out = lax.optimization_barrier((mixed, w_in, w_out))
 
     positions = jnp.arange(row_count)
     allowed = (
@@ -369,7 +557,10 @@
     v_spec = pl.BlockSpec((VDIM, row_count), lambda h: (h, 0))
     row_spec = pl.BlockSpec((1, 1, row_count), lambda h: (h, 0, 0))
     state_spec = pl.BlockSpec((1, FROWS, LANES), lambda h: (h, 0, 0))
-    all_states_spec = pl.BlockSpec((group, 1, FROWS, LANES), lambda h: (0, h, 0, 0))
+
+    def stack_spec(stack):
+        return pl.BlockSpec((stack.shape[0], 1, FROWS, LANES), lambda h: (0, h, 0, 0))
+
     one_row = whole(1, row_count)
     square = whole(row_count, row_count)
     table = whole(FROWS, EXT)
@@ -394,25 +585,38 @@
         10**9, 4 * 10**6,
         id_pieces, qk, values, own, left_low, right_low, key_scale,
     )
-    all_states = lax.all_gather(states, "grp", axis=0)
+    near_states = stack_near(states)
     num_local, den_local = call(
         local_kernel, (v_wide, head_rows), grid,
         [qk_spec, k_spec, v_spec, square], (v_spec, row_spec),
         15 * 10**9, 7 * 10**6,
         qk, qk, values, allowed,
     )
-    id_parts = all_states[:, 0, 0, VDIM + 2 : VDIM + 4].astype(F32)
-    last_ids = id_parts[:, 0] * 256.0 + id_parts[:, 1]
-    order = jnp.arange(group)
-    before = jnp.where(mine > 0, last_ids[jnp.maximum(mine - 1, 0)], -1.0)
-    marks = ((order < mine) & (last_ids == before)).astype(F32)
+    num_local, den_local, near_states = lax.optimization_barrier(
+        (num_local, den_local, near_states)
+    )
+    state_stacks = stack_all(states, near_states)
+    late_dy, state_stacks[0] = lax.optimization_barrier((grad_out, state_stacks[0]))
+    dy_pieces = gather_near(late_dy)[1]
+    dy_far = far_halves(dy_pieces)
+    sources = mine ^ jnp.array(stack_offsets(), jnp.int32)
+    id_parts = jnp.concatenate(
+        [stack[:, 0, 0, VDIM + 2 : VDIM + 4] for stack in state_stacks], axis=0
+    ).astype(F32)
+    source_ids = id_parts[:, 0] * 256.0 + id_parts[:, 1]
+    before = jnp.sum(jnp.where(sources == mine - 1, source_ids, 0.0))
+    before = jnp.where(mine > 0, before, -1.0)
+    marks = ((sources < mine) & (source_ids == before)).astype(F32)
     cont = (id_float == before).astype(F32)[None, :]
     attended, output, denom, state_in = call(
-        carried_kernel, (v_low, v_wide, head_rows, states_wide), grid,
-        [smem, qk_spec, all_states_spec, v_spec, row_spec, one_row, table, table, column],
+        functools.partial(carried_kernel, len(state_stacks)),
+        (v_low, v_wide, head_rows, states_wide), grid,
+        [smem, *map(stack_spec, state_stacks),
+         qk_spec, v_spec, row_spec, one_row, table, table, column],
         (v_spec, v_spec, row_spec, state_spec),
         2 * 10**9, 16 * 10**6,
-        marks, qk, all_states, num_local, den_local, cont, left_low, right_low, query_scale,
+        marks, *state_stacks,
+        qk, num_local, den_local, cont, left_low, right_low, query_scale,
     )
     branch = dot(attended, full_out, 0, 0)
     residual = x_full + branch
@@ -420,52 +624,89 @@
     unit_mid = residual * scale_mid
     normed_mid = (unit_mid * ffn_gain).astype(BF)
 
-    all_mid = lax.all_gather(normed_mid, "grp", axis=0, tiled=True)
-    tile = row_count
-    steps = group
-    wide_tile = pl.BlockSpec((tile, model_width), lambda i: (i, 0))
-    thin_tile = pl.BlockSpec((tile, hidden), lambda i: (i, 0))
-    thin = jax.ShapeDtypeStruct((row_count * group, hidden), BF)
-    wide = jax.ShapeDtypeStruct((row_count * group, model_width), BF)
-    w_in_spec = whole(hidden, 2 * model_width)
-    w_out_spec = whole(hidden, model_width)
-    unit = 2 * row_count * group * hidden * model_width
-    activation, dgate, dup, back_terms = call(
-        ffn_kernel, (thin, thin, thin, wide), (steps,),
-        [wide_tile, wide_tile, w_in_spec, w_out_spec],
-        (thin_tile, thin_tile, thin_tile, wide_tile),
-        5 * unit, 60 * 10**6,
-        all_mid, all_dy, ffn_in, ffn_out,
-    )
-    grad_normed_mid = lax.psum_scatter(
-        back_terms, "grp", scatter_dimension=0, tiled=True
-    ).astype(F32)
-    result_terms, ffn_grads = call(
-        ffn_grad_kernel, (wide, jax.ShapeDtypeStruct((hidden, 3 * model_width), BF)), (steps,),
-        [wide_tile, wide_tile, thin_tile, thin_tile, thin_tile, w_out_spec],
-        (wide_tile, whole(hidden, 3 * model_width)),
-        4 * unit, 60 * 10**6,
-        all_mid, all_dy, activation, dgate, dup, ffn_out,
-        scratch=[pltpu.VMEM((hidden, 3 * model_width), F32)],
-    )
-    ffn_result = lax.psum_scatter(
-        result_terms, "grp", scatter_dimension=0, tiled=True
-    ).astype(F32)
-    mixed_out = (residual + ffn_result).astype(BF)
-    ffn_grads = rep_sum(ffn_grads)
-
-    grad_y = grad_out.astype(F32)
-    grad_unit_mid = grad_normed_mid * ffn_gain
-    grad_ffn_gain = jnp.sum(grad_normed_mid * unit_mid, axis=0)
-    grad_mid = grad_y + scale_mid * (
-        grad_unit_mid - unit_mid * jnp.mean(grad_unit_mid * unit_mid, axis=1, keepdims=True)
-    )
-    grad_branch = grad_mid.astype(BF)
+    offsets, mid_pieces = gather_near(normed_mid)
+    units = w_in.shape[0]
+    tokens_low = jax.ShapeDtypeStruct((row_count, model_width), BF)
+    tokens_wide = jax.ShapeDtypeStruct((row_count, model_width), F32)
+    tokens_spec = whole(row_count, model_width)
+    once = pl.Buffered(1)
+    def ffn_piece(x_piece, dy_piece):
+        return call(
+            ffn_kernel,
+            (
+                jax.ShapeDtypeStruct((1, row_count, units), BF),
+                jax.ShapeDtypeStruct((2, row_count, units), BF),
+                tokens_low,
+            ),
+            (1,),
+            [
+                tokens_spec, tokens_spec,
+                pl.BlockSpec((units, 2 * model_width), lambda i: (0, 0), pipeline_mode=once),
+                pl.BlockSpec((units, model_width), lambda i: (0, 0), pipeline_mode=once),
+            ],
+            (whole(1, row_count, units), whole(2, row_count, units), tokens_spec),
+            0, 0, x_piece, dy_piece, w_in, w_out,
+        )
+
+    first = ffn_piece(mid_pieces[0], dy_pieces[0])
+    *first, near = lax.optimization_barrier((*first, tuple(mid_pieces[1:])))
+    mid_pieces = [mid_pieces[0], *near]
+    mid_far = far_halves(mid_pieces)
+    done = [first] + [ffn_piece(x, dy) for x, dy in zip(mid_pieces[1:], dy_pieces[1:])]
+    done[-1], mid_far, dy_far = lax.optimization_barrier((list(done[-1]), mid_far, dy_far))
+    mid_pieces, dy_pieces = with_far(mid_pieces, mid_far), with_far(dy_pieces, dy_far)
+    done += [ffn_piece(x, dy) for x, dy in zip(mid_pieces[len(done) :], dy_pieces[len(done) :])]
+    acts, pres, backs = map(list, zip(*done))
+    acts, pres, backs[-1] = lax.optimization_barrier((acts, pres, backs[-1]))
+
+    def weight_grads(lefts, rights):
+        kinds = lefts[0].shape[0]
+        cut = 256
+        cuts = model_width // cut
+        count = len(lefts)
+        return call(
+            functools.partial(weight_grad_kernel, count),
+            tuple(
+                jax.ShapeDtypeStruct((hidden, kinds * model_width), BF)
+                for _ in range(units // hidden)
+            ),
+            (kinds, cuts),
+            [pl.BlockSpec((1, row_count, units), lambda m, j: (m, 0, 0))] * count
+            + [pl.BlockSpec((row_count, cut), lambda m, j: (0, j))] * count,
+            tuple(
+                pl.BlockSpec((hidden, cut), lambda m, j: (0, m * cuts + j))
+                for _ in range(units // hidden)
+            ),
+            0, 0, *lefts, *rights,
+        )
+
+    back_terms = [exchanged(b, k) for b, k in zip(backs[1:], offsets[1:])]
+    in_parts = weight_grads(pres, mid_pieces)
+    acts, in_parts, back_terms[:-1] = lax.optimization_barrier((acts, in_parts, back_terms[:-1]))
+    out_parts = weight_grads(acts, dy_pieces)
+    results = [dot(act[0], w_out, 1, 0).astype(BF) for act in acts]
+    orders = rep_steps()
+    sums = [
+        halves_of([own_part, *(exchanged(g, 1) for g in rest)], order[0])
+        for (own_part, *rest), order in zip((in_parts, out_parts), orders)
+    ]
+    back_terms, results, sums = lax.optimization_barrier((back_terms, results, sums))
+    back_terms = [backs[0], *back_terms]
+    kept = [keep for keep, _ in sums]
+    moved = [rep_swap(send, order[0]) for (_, send), order in zip(sums, orders)]
+    *results, last_result = results
+    result_terms = [exchanged(r, k) for r, k in zip(results[1:], offsets[1:])]
+    tile = row_count // 4
+    tile_spec = pl.BlockSpec((tile, model_width), lambda i: (i, 0))
+    gain_spec = whole(1, model_width)
+    grad_mid, grad_branch, grad_ffn_gain = call(
+        functools.partial(mid_grad_kernel, len(back_terms)),
+        (tokens_wide, tokens_low, jax.ShapeDtypeStruct((1, model_width), F32)), (4,),
+        [tile_spec] * (len(back_terms) + 2) + [gain_spec],
+        (tile_spec, tile_spec, gain_spec),
+        0, 0, *back_terms, residual, grad_out, ffn_gain[None],
+    )
     grad_att = dot(full_out, grad_branch, 1, 1)
-    out_terms = dot(attended, grad_branch, 1, 0).astype(BF)
-    out_shard = lax.psum_scatter(out_terms, "grp", scatter_dimension=0, tiled=True)
-    grad_mix_out = rep_sum(out_shard)
-
     state_grads, dnum, dden = call(
         state_grad_kernel, (states_low, v_low, head_rows), grid,
         [v_spec, v_spec, row_spec, qk_spec, one_row, table, table, column],
@@ -473,7 +714,8 @@
         2 * 10**9, 12 * 10**6,
         grad_att, output, denom, qk, cont, left_low, right_low, query_scale,
     )
-    all_state_grads = lax.all_gather(state_grads, "grp", axis=0)
+    state_grads, result_terms = lax.optimization_barrier((state_grads, result_terms))
+    near_grads = stack_near(state_grads)
     grad_queries, dk_local, dv_local = call(
         local_grad_kernel, (qk_low, qk_wide, v_wide), grid,
         [qk_spec, k_spec, v_spec, v_spec, row_spec, square, state_spec, one_row,
@@ -483,43 +725,58 @@
         qk, qk, values, dnum, dden, allowed, state_in, cont,
         left_low, right_low, left_t, right_t, query_scale,
     )
-    previous_ids = jnp.concatenate([jnp.full((1,), -1.0, F32), last_ids[:-1]])
-    late_marks = ((order > mine) & (previous_ids == last_ids[mine])).astype(F32)
+    dk_local, dv_local, near_grads, moved = lax.optimization_barrier(
+        (dk_local, dv_local, near_grads, moved)
+    )
+    grad_stacks = stack_all(state_grads, near_grads)
+    queue = SumQueue(orders, [added(k, m) for k, m in zip(kept, moved)])
+    late_attended, grad_stacks[0] = lax.optimization_barrier((attended, grad_stacks[0]))
+    out_terms = dot(late_attended, grad_branch, 1, 0).astype(BF)
+    out_shard = lax.psum_scatter(out_terms, "grp", scatter_dimension=0, tiled=True)
+    earlier = sources[None, :] == sources[:, None] - 1
+    previous_ids = jnp.sum(jnp.where(earlier, source_ids[None, :], 0.0), axis=1)
+    late_marks = ((sources > mine) & (previous_ids == id_float[row_count - 1])).astype(F32)
     grad_keys, grad_values = call(
-        late_grad_kernel, (qk_low, v_low), grid,
-        [smem, all_states_spec, k_spec, v_spec, one_row, qk_spec, v_spec,
+        functools.partial(late_grad_kernel, len(grad_stacks)), (qk_low, v_low), grid,
+        [smem, *map(stack_spec, grad_stacks), k_spec, v_spec, one_row, qk_spec, v_spec,
          table, table, table_t, table_t, column],
         (qk_spec, v_spec),
         2 * 10**9, 14 * 10**6,
-        late_marks, all_state_grads, qk, values, own, dk_local, dv_local,
+        late_marks, *grad_stacks, qk, values, own, dk_local, dv_local,
         left_low, right_low, left_t, right_t, key_scale,
     )
     grad_projected = jnp.concatenate([grad_queries, grad_keys, grad_values], axis=0)
     in_terms = dot(mixed, grad_projected, 0, 1).astype(BF)
+    in_terms = queue.turn(in_terms)
     in_shard = lax.psum_scatter(in_terms, "grp", scatter_dimension=0, tiled=True)
-    grad_mix_in = rep_sum(in_shard)
-
+    in_shard, last_result = lax.optimization_barrier((in_shard, last_result))
+    grad_mix_in = lax.psum(in_shard, "rep").astype(F32)
+    result_terms.append(exchanged(last_result, offsets[-1]))
     grad_mixed = dot(grad_projected, full_in, 0, 1)
-    grad_conv = grad_mixed * gated
-    grad_normed = grad_mixed * conv_out * silu_grad(normed)
-    edge_back = jnp.concatenate([grad_conv[:2], id_float[:2, None]], axis=1)
+    grad_mixed = queue.turn(grad_mixed, out_shard)
+    edge_back = jnp.concatenate([grad_mixed[:2] * gated[:2], id_float[:2, None]], axis=1)
     edge_back = passed_along(edge_back, "grp", -1)
-    ext_grad = jnp.concatenate([grad_conv, edge_back[:, :model_width]], axis=0)
     ext_grad_ids = jnp.concatenate([id_float, edge_back[:, model_width]], axis=0)
     ahead_one = (ext_grad_ids[1 : row_count + 1] == id_float).astype(F32)[:, None]
     ahead_two = (ext_grad_ids[2:] == id_float).astype(F32)[:, None]
-    grad_normed = (
-        grad_normed
-        + conv_taps[:, 0] * grad_conv
-        + conv_taps[:, 1] * (ext_grad[1 : row_count + 1] * ahead_one)
-        + conv_taps[:, 2] * (ext_grad[2:] * ahead_two)
-    )
-    grad_unit_in = grad_normed * norm_gain
-    grad_tokens = (
-        grad_mid
-        + scale_in
-        * (grad_unit_in - unit_in * jnp.mean(grad_unit_in * unit_in, axis=1, keepdims=True))
-    ).astype(BF)
+    flags = jnp.concatenate([same_one, same_two, ahead_one, ahead_two], axis=1)
+    grad_tokens, sums = call(
+        conv_grad_kernel, (tokens_low, jax.ShapeDtypeStruct((4, model_width), F32)), (1,),
+        [
+            tokens_spec, whole(2, model_width), whole(2, model_width), whole(row_count, 1),
+            whole(row_count, 4), gain_spec, whole(3, model_width), tokens_spec, tokens_spec,
+        ],
+        (tokens_spec, whole(4, model_width)),
+        0, 0,
+        tokens, ext_norm[:2], edge_back[:, :model_width], scale_in, flags, norm_gain[None],
+        conv_taps.T, grad_mixed, grad_mid,
+        scratch=[pltpu.VMEM((row_count, model_width), F32)],
+    )
+
+    grad_tokens, sums = queue.turn((grad_tokens, sums))
+    grad_ffn_in, grad_ffn_out, grad_mix_out = queue.finish()
+    ffn_result = sum(term.astype(F32) for term in [results[0], *result_terms])
+    mixed_out = (residual + ffn_result).astype(BF)
 
     stat_terms = jnp.stack(
         [
@@ -529,18 +786,9 @@
             jnp.sum(keep_rows),
         ]
     )
-    small = jnp.concatenate(
-        [
-            jnp.sum(grad_normed * unit_in, axis=0),
-            jnp.sum(grad_conv * normed, axis=0),
-            jnp.sum(grad_conv * back_one, axis=0),
-            jnp.sum(grad_conv * back_two, axis=0),
-            grad_ffn_gain,
-            stat_terms,
-        ]
-    )
+    small = jnp.concatenate([sums.reshape(-1), grad_ffn_gain[0], stat_terms])
     small = jnp.pad(small, (0, -small.shape[0] % 1024)).reshape(-1, LANES)
-    small = jnp.sum(lax.all_gather(small, ("rep", "grp"), axis=0), axis=0).reshape(-1)
+    small = butterfly_sum(small).reshape(-1)
     rows = small[: 5 * model_width].reshape(5, model_width)
     stats = small[5 * model_width : 5 * model_width + 4]
     layer_stats = jnp.sqrt(stats[:3] / (jnp.maximum(stats[3], 1.0) * model_width))
@@ -550,10 +798,10 @@
         rows[0],
         rows[1:4].T,
         grad_mix_in,
-        grad_mix_out,
+        grad_mix_out.astype(F32),
         rows[4],
-        ffn_grads[:, : 2 * model_width],
-        ffn_grads[:, 2 * model_width :],
+        grad_ffn_in.astype(F32),
+        grad_ffn_out.astype(F32),
         layer_stats,
     )
 

time: 1030 us -> 737 us (0.72)
  waiting for transfers between devices: 602 us -> 282 us
  Pallas kernels: 176 us -> 202 us
  starting transfers between devices: 62.2 us -> 51.3 us
    all_gather x5 -> x0, waiting for transfers between devices: 204 us -> none  [the longest x1 83.3 us: body(): all_mid = lax.all_gather(normed_mid, 'grp', axis=0, tiled=True)]
    reduce_scatter x2 -> x0, waiting for transfers between devices: 158 us -> none  [the longest x1 103 us: body(): lax.psum_scatter(result_terms, 'grp', scatter_dimension=0, tiled=True)]
    reduce_scatter x1, waiting for transfers between devices: 0.02 us -> 71.4 us  [body(): lax.psum_scatter(out_terms, 'grp', scatter_dimension=0, tiled=True)]
    ppermute x18 -> x43, waiting for transfers between devices: 170 us -> 135 us  [the longest x26 69.8 us: exchanged(): return lax.ppermute(block, 'grp', [(i, i ^ offset) for i in range(count)])]
    all_gather x1, waiting for transfers between devices: 29.7 us -> 0.01 us  [body(): full_out = lax.all_gather(mix_out, 'grp', axis=0, tiled=True)]
    psum x0 -> x1, waiting for transfers between devices: none -> 26.6 us  [body(): grad_mix_in = lax.psum(in_shard, 'rep').astype(F32)]
    pallas_call x8 -> x14, Pallas kernels: 176 us -> 202 us  [call(): pl.pallas_call(kernel, out_shape=outs, grid=grid, in_specs=in_specs, out_...]
    reduce_scatter x1, waiting for transfers between devices: 0.02 us -> 17.3 us  [body(): lax.psum_scatter(in_terms, 'grp', scatter_dimension=0, tiled=True)]
  transfers between devices with their start and end apart: 31 -> 50, of which waited for: 17 -> 19; matrix products, arithmetic and copies ran while one was open for 12% -> 20% of each run, Pallas kernels for 11% -> 28%
where the time goes in v2:
time: 737 us; the launch traced here: 727 us
  waiting for transfers between devices  282 us (38%)
  Pallas kernels  202 us (27%)
  matrix products  63.7 us (9%)
  other arithmetic  60.7 us (8%)
  starting transfers between devices  51.3 us (7%)
  local copies, waits for them, and re-layouts  48.1 us (7%)
  between operations  19.3 us (3%)
    pallas_call x14, Pallas kernels, call(): pl.pallas_call(kernel, out_shape=outs, grid=grid, in_specs=in_specs, out_...  202 us
    reduce_scatter x1, waiting for transfers between devices, body(): lax.psum_scatter(out_terms, 'grp', scatter_dimension=0, tiled=True)  71.4 us
    ppermute x26, waiting for transfers between devices, exchanged(): return lax.ppermute(block, 'grp', [(i, i ^ offset) for i in range(count)])  69.8 us
    dot_general x11, matrix products, dot(): lax.dot_general(left, right, (((left_dim,), (right_dim,)), ((), ())), pre...  63.7 us
    ppermute x12, waiting for transfers between devices, rep_swap(): return lax.ppermute(block, 'rep', [(i, i ^ step) for i in range(count)])  49.6 us
    all_gather x1, waiting for transfers between devices, body(): full_in = lax.all_gather(mix_in, 'grp', axis=0, tiled=True)  29.6 us
    psum x1, waiting for transfers between devices, body(): grad_mix_in = lax.psum(in_shard, 'rep').astype(F32)  26.6 us
    ppermute x26, starting transfers between devices, exchanged(): return lax.ppermute(block, 'grp', [(i, i ^ offset) for i in range(count)])  25.6 us
  transfers between devices with their start and end apart: 50, of which 19 were waited for; matrix products, arithmetic and copies ran while one was open for 20% of the time, Pallas kernels for 28%

profile of v2, /device:TPU:0, one launch (start us, length us, event | category | flops | bytes accessed | tf_op | source)
XLA Modules:
  0.0 726.5 jit_solution(5946371287627767008)
XLA Ops:
  36.9 29.6 %all-gather.3.cloned.1.call-done = bf16[1792,2304]{1,0:T(8,128)(2,1)} async-done(((bf16[224,2304]{1,0:T(8,128)(2,1)}), bf16[1792,2304]{1,0:T(8,128)(2,1)}) %all-gather.3.cloned.1.call-update) | async-done | bytes 8257552 | tf_op jit(solution)/shard_map/all_gather | solution.py:510
  87.0 10.4 %shard_map.250 = (f32[1792,512]{1,0:T(8,128)}, f32[16,1,512]{2,1,0:T(1,128)S(1)}) custom-call(bf16[512,512]{1,0:T(8,128)(2,1)S(1)} %fusion.21.keys_ref.queries_ref.refs_2_, bf16[512,512]{1,0:T(8,128)(2,1)S(1)} %fusion.21.keys_ref.queries_ref.refs_2_, bf16[1792,512]{1,0:T(8,128)(2,1)S(1)} %fusion.12.values_ref.refs_3_, f32[512,512]{1,0:T(8,128)S(1)} %fusion.25.allowed_ref), custom_call_target="tpu_custom_call" | custom-call | tf_op jit(solution)/shard_map/pallas_call | solution.py:341
  102.5 18.9 %collective-permute-done.4 = bf16[16,160,128]{2,1,0:T(8,128)(2,1)S(1)} collective-permute-done((bf16[16,160,128]{2,1,0:T(8,128)(2,1)S(1)}, bf16[16,160,128]{2,1,0:T(8,128)(2,1)S(1)}, u32[]{:S(2)}, u32[]{:S(2)}) %collective-permute-start.4) | collective-permute-done | bytes 655392 | tf_op jit(solution)/shard_map/ppermute | solution.py:370
  133.5 14.2 %shard_map.251 = (bf16[1792,512]{1,0:T(8,128)(2,1)S(1)}, f32[1792,512]{1,0:T(8,128)}, f32[16,1,512]{2,1,0:T(1,128)S(1)}, f32[16,160,128]{2,1,0:T(8,128)S(1)}) custom-call(f32[8]{0:T(128)S(1)} %get-tuple-element.260.marks_ref, bf16[4,16,160,128]{3,2,1,0:T(8,128)(2,1)} %pad_maximum_fusion.3.refs_0_, bf16[4,16,160,128]{3,2,1,0:T(8,128)(2,1)} %collective-permute-done.6.refs_1_, ...), custom_call_target="tpu_custom_call" | custom-call | tf_op jit(solution)/shard_map/pallas_call | solution.py:341
  162.0 10.7 %collective-permute-done.10.dy_ref.refs_6_ = bf16[512,1792]{1,0:T(8,128)(2,1)} collective-permute-done((bf16[512,1792]{1,0:T(8,128)(2,1)}, bf16[512,1792]{1,0:T(8,128)(2,1)}, u32[]{:S(2)}, u32[]{:S(2)}) %collective-permute-start.10) | collective-permute-done | bytes 1835040 | tf_op jit(solution)/shard_map/ppermute | solution.py:370
  179.1 16.7 %shard_map.252 = (bf16[1,512,896]{2,1,0:T(8,128)(2,1)S(1)}, bf16[2,512,896]{2,1,0:T(8,128)(2,1)S(1)}, bf16[512,1792]{1,0:T(8,128)(2,1)}) custom-call(bf16[512,1792]{1,0:T(8,128)(2,1)} %copy-done.41, bf16[512,1792]{1,0:T(8,128)(2,1)} %refs_5_.1, bf16[896,3584]{1,0:T(8,128)(2,1)} %pad_maximum_fusion.w_in_ref, bf16[896,1792]{1,0:T(8,128)(2,1)} %pad_maximum_fusion.2.w_out_ref), custom_call_target="tpu_custom_call" | custom-call | tf_op jit(solution)/shard_map/pallas_call | solution.py:341
  195.8 16.1 %collective-permute-done.8.x_ref.refs_6_ = bf16[512,1792]{1,0:T(8,128)(2,1)S(1)} collective-permute-done((bf16[512,1792]{1,0:T(8,128)(2,1)S(1)}, bf16[512,1792]{1,0:T(8,128)(2,1)S(1)}, u32[]{:S(2)}, u32[]{:S(2)}) %collective-permute-start.8) | collective-permute-done | bytes 1835040 | tf_op jit(solution)/shard_map/ppermute | solution.py:370
  216.4 16.6 %shard_map.253 = (bf16[1,512,896]{2,1,0:T(8,128)(2,1)S(1)}, bf16[2,512,896]{2,1,0:T(8,128)(2,1)S(1)}, bf16[512,1792]{1,0:T(8,128)(2,1)}) custom-call(bf16[512,1792]{1,0:T(8,128)(2,1)} %copy-done.43, bf16[512,1792]{1,0:T(8,128)(2,1)} %collective-permute-done.9.dy_ref.refs_5_, bf16[896,3584]{1,0:T(8,128)(2,1)} %pad_maximum_fusion.w_in_ref, ...), custom_call_target="tpu_custom_call" | custom-call | tf_op jit(solution)/shard_map/pallas_call | solution.py:341
  234.8 16.9 %shard_map.254 = (bf16[1,512,896]{2,1,0:T(8,128)(2,1)S(1)}, bf16[2,512,896]{2,1,0:T(8,128)(2,1)S(1)}, bf16[512,1792]{1,0:T(8,128)(2,1)}) custom-call(bf16[512,1792]{1,0:T(8,128)(2,1)} %copy-done.42, bf16[512,1792]{1,0:T(8,128)(2,1)} %collective-permute-done.10.dy_ref.refs_6_, bf16[896,3584]{1,0:T(8,128)(2,1)} %pad_maximum_fusion.w_in_ref, ...), custom_call_target="tpu_custom_call" | custom-call | tf_op jit(solution)/shard_map/pallas_call | solution.py:341
  259.5 16.5 %shard_map.255 = (bf16[1,512,896]{2,1,0:T(8,128)(2,1)S(1)}, bf16[2,512,896]{2,1,0:T(8,128)(2,1)S(1)}, bf16[512,1792]{1,0:T(8,128)(2,1)}) custom-call(bf16[512,1792]{1,0:T(8,128)(2,1)} %copy-done.44, bf16[512,1792]{1,0:T(8,128)(2,1)} %copy-done.45, bf16[896,3584]{1,0:T(8,128)(2,1)} %pad_maximum_fusion.w_in_ref, bf16[896,1792]{1,0:T(8,128)(2,1)} %pad_maximum_fusion.2.w_out_ref), custom_call_target="tpu_custom_call" | custom-call | tf_op jit(solution)/shard_map/pallas_call | solution.py:341
  277.2 20.6 %shard_map.256 = (bf16[448,3584]{1,0:T(8,128)(2,1)}, bf16[448,3584]{1,0:T(8,128)(2,1)}) custom-call(bf16[2,512,896]{2,1,0:T(8,128)(2,1)S(1)} %get-tuple-element.158.refs_0_, bf16[2,512,896]{2,1,0:T(8,128)(2,1)S(1)} %get-tuple-element.159.refs_1_, bf16[2,512,896]{2,1,0:T(8,128)(2,1)} %copy-done.3, bf16[2,512,896]{2,1,0:T(8,128)(2,1)} %copy-done.4, ...), custom_call_target="tpu_custom_call" | custom-call | tf_op jit(solution)/shard_map/pallas_call | solution.py:341
  304.3 10.8 %shard_map.257 = (bf16[448,1792]{1,0:T(8,128)(2,1)}, bf16[448,1792]{1,0:T(8,128)(2,1)}) custom-call(bf16[1,512,896]{2,1,0:T(8,128)(2,1)S(1)} %copy-done.12, bf16[1,512,896]{2,1,0:T(8,128)(2,1)S(1)} %copy-done.14, bf16[1,512,896]{2,1,0:T(8,128)(2,1)S(1)} %copy-done.16, bf16[1,512,896]{2,1,0:T(8,128)(2,1)S(1)} %copy-done.18, bf16[512,1792]{1,0:T(8,128)(2,1)} %refs_5_.1, ...), custom_call_target="tpu_custom_call" | custom-call | tf_op jit(solution)/shard_map/pallas_call | solution.py:341
  364.8 12.4 %shard_map.259 = (bf16[16,160,128]{2,1,0:T(8,128)(2,1)S(1)}, bf16[1792,512]{1,0:T(8,128)(2,1)S(1)}, f32[16,1,512]{2,1,0:T(1,128)S(1)}) custom-call(f32[1792,512]{1,0:T(8,128)} %convolution_bitcast_fusion.grad_ref, f32[1792,512]{1,0:T(8,128)} %get-tuple-element.183.output_ref, f32[16,1,512]{2,1,0:T(1,128)S(1)} %get-tuple-element.184.denom_ref, ...), custom_call_target="tpu_custom_call" | custom-call | tf_op jit(solution)/shard_map/pallas_call | solution.py:341
  387.8 21.0 %shard_map.260 = (bf16[256,512]{1,0:T(8,128)(2,1)S(1)}, f32[256,512]{1,0:T(8,128)S(1)}, f32[1792,512]{1,0:T(8,128)}) custom-call(bf16[512,512]{1,0:T(8,128)(2,1)S(1)} %fusion.21.keys_ref.queries_ref.refs_2_, bf16[512,512]{1,0:T(8,128)(2,1)S(1)} %fusion.21.keys_ref.queries_ref.refs_2_, bf16[1792,512]{1,0:T(8,128)(2,1)} %copy-done, ...), custom_call_target="tpu_custom_call" | custom-call | tf_op jit(solution)/shard_map/pallas_call | solution.py:341
  427.2 14.1 %shard_map.261 = (bf16[256,512]{1,0:T(8,128)(2,1)S(1)}, bf16[1792,512]{1,0:T(8,128)(2,1)S(1)}) custom-call(f32[8]{0:T(128)S(1)} %copy-done.35, bf16[4,16,160,128]{3,2,1,0:T(8,128)(2,1)} %pad_maximum_fusion.4.refs_0_, bf16[4,16,160,128]{3,2,1,0:T(8,128)(2,1)} %collective-permute-done.27.refs_1_, bf16[512,512]{1,0:T(8,128)(2,1)S(1)} %fusion.21.keys_ref.queries_ref.refs_2_, ...), custom_call_target="tpu_custom_call" | custom-call | tf_op jit(solution)/shard_map/pallas_call | solution.py:341
  450.4 12.8 %collective-permute-done.28 = bf16[112,3584]{1,0:T(8,128)(2,1)} collective-permute-done((bf16[112,3584]{1,0:T(8,128)(2,1)}, bf16[112,3584]{1,0:T(8,128)(2,1)}, u32[]{:S(2)}, u32[]{:S(2)}) %collective-permute-start.28) | collective-permute-done | bytes 802848 | tf_op jit(solution)/shard_map/ppermute | solution.py:422
  463.2 9.1 %convolution_convert_fusion.1 = bf16[1792,1792]{1,0:T(8,128)(2,1)} fusion(bf16[1792,512]{1,0:T(8,128)(2,1)} %copy-done.36, bf16[512,1792]{1,0:T(8,128)(2,1)} %copy-done.37), kind=kOutput, calls=%fused_computation.1 | convolution fusion | flops 3291545600 | bytes 10092544 | tf_op jit(solution)/shard_map/dot_general | solution.py:50
  491.5 21.7 %collective-permute-done.31 = bf16[112,3584]{1,0:T(8,128)(2,1)S(1)} collective-permute-done((bf16[112,3584]{1,0:T(8,128)(2,1)S(1)}, bf16[112,3584]{1,0:T(8,128)(2,1)S(1)}, u32[]{:S(2)}, u32[]{:S(2)}) %collective-permute-start.31) | collective-permute-done | bytes 802848 | tf_op jit(solution)/shard_map/ppermute | solution.py:422
  515.5 17.3 %reduce-scatter.3.cloned.1.call-done = bf16[224,2304]{1,0:T(8,128)(2,1)} async-done(((bf16[1792,2304]{1,0:T(8,128)(2,1)}), bf16[224,2304]{1,0:T(8,128)(2,1)}) %reduce-scatter.3.cloned.1.call-update) | async-done | bytes 1032208 | tf_op jit(solution)/shard_map/reduce_scatter | solution.py:751
  540.7 71.4 %reduce-scatter.5.cloned.1.call-done = bf16[224,1792]{1,0:T(8,128)(2,1)} async-done(((bf16[1792,1792]{1,0:T(8,128)(2,1)}), bf16[224,1792]{1,0:T(8,128)(2,1)}) %reduce-scatter.5.cloned.1.call-update) | async-done | bytes 802832 | tf_op jit(solution)/shard_map/reduce_scatter | solution.py:735
  615.6 16.2 %shard_map.262 = (bf16[512,1792]{1,0:T(8,128)(2,1)}, f32[4,1792]{1,0:T(4,128)S(1)}) custom-call(bf16[512,1792]{1,0:T(8,128)(2,1)S(1)} %copy-done.2, f32[2,1792]{1,0:T(2,128)S(1)} %slice.181.before_ref, f32[2,1792]{1,0:T(2,128)S(1)} %slice.183.after_ref, f32[512,1]{1,0:T(8,128)S(1)} %copy.63.scale_ref, f32[512,4]{1,0:T(8,128)S(1)} %copy.64.flags_ref, ...), custom_call_target="tpu_custom_call" | custom-call | tf_op jit(solution)/shard_map/pallas_call | solution.py:341
  648.4 10.1 %collective-permute-done.43 = bf16[56,1792]{1,0:T(8,128)(2,1)S(1)} collective-permute-done((bf16[56,1792]{1,0:T(8,128)(2,1)S(1)}, bf16[56,1792]{1,0:T(8,128)(2,1)S(1)}, u32[]{:S(2)}, u32[]{:S(2)}) %collective-permute-start.43) | collective-permute-done | bytes 200736 | tf_op jit(solution)/shard_map/ppermute | solution.py:422
  670.7 15.3 %collective-permute-done.40 = f32[72,128]{1,0:T(8,128)S(1)} collective-permute-done((f32[72,128]{1,0:T(8,128)S(1)}, f32[72,128]{1,0:T(8,128)S(1)}, u32[]{:S(2)}, u32[]{:S(2)}) %collective-permute-start.40) | collective-permute-done | bytes 36896 | tf_op jit(solution)/shard_map/ppermute | solution.py:401
  687.3 26.6 %all-reduce.3.cloned.1.call-done = bf16[224,2304]{1,0:T(8,128)(2,1)} async-done(((bf16[224,2304]{1,0:T(8,128)(2,1)}), bf16[224,2304]{1,0:T(8,128)(2,1)}) %all-reduce.3.cloned.1.call-update) | async-done | bytes 1032208 | tf_op jit(solution)/shard_map/psum | solution.py:753
  (376 shorter events, 261.4 us)
Async XLA Ops:
  7.2 59.3 %all-gather.3.cloned.1.call-start = ((), (), s32[]{:S(2)}) async-start(), calls=%async_computation.2 | async-start | bytes 9289728 | tf_op jit(solution)/shard_map/all_gather | solution.py:510
  7.9 142.1 %all-gather.5.cloned.1.call-start = ((), (), s32[]{:S(2)}) async-start(), calls=%async_computation.3 | async-start | bytes 7225344 | tf_op jit(solution)/shard_map/all_gather | solution.py:511
  8.7 524.1 %reduce-scatter.3.cloned.1.call-start = ((), (), s32[]{:S(2)}) async-start(), calls=%async_computation.4 | async-start | bytes 9289728 | tf_op jit(solution)/shard_map/reduce_scatter | solution.py:751
  123.8 48.8 %collective-permute-start.10 = (bf16[512,1792]{1,0:T(8,128)(2,1)}, bf16[512,1792]{1,0:T(8,128)(2,1)}, u32[]{:S(2)}, u32[]{:S(2)}) collective-permute-start(bf16[512,1792]{1,0:T(8,128)(2,1)} %refs_5_.1), channel_id=1, source_target_pairs={{0,4},{1,5},{2,6},{3,7},{4,0},{5,1},{6,2},{7,3},{8,12},{9,13},{10,... | collective-permute-start | bytes 5505032 | tf_op jit(solution)/shard_map/ppermute | solution.py:370
  125.2 51.1 %collective-permute-start.9 = (bf16[512,1792]{1,0:T(8,128)(2,1)}, bf16[512,1792]{1,0:T(8,128)(2,1)}, u32[]{:S(2)}, u32[]{:S(2)}) collective-permute-start(bf16[512,1792]{1,0:T(8,128)(2,1)} %refs_5_.1), channel_id=1, source_target_pairs={{0,2},{1,3},{2,0},{3,1},{4,6},{5,7},{6,4},{7,5},{8,10},{9,11},{10,... | collective-permute-start | bytes 5505032 | tf_op jit(solution)/shard_map/ppermute | solution.py:370
  160.1 51.8 %collective-permute-start.8 = (bf16[512,1792]{1,0:T(8,128)(2,1)S(1)}, bf16[512,1792]{1,0:T(8,128)(2,1)S(1)}, u32[]{:S(2)}, u32[]{:S(2)}) collective-permute-start(bf16[512,1792]{1,0:T(8,128)(2,1)S(1)} %multiply_convert_fusion.x_ref.refs_4_), channel_id=1, source_target_pairs={{0,4},{1,5},{2,6},{3,7},{4,0},{5,1},{6,2},{7,3},{8,12},{9,13},{10,... | collective-permute-start | bytes 5505032 | tf_op jit(solution)/shard_map/ppermute | solution.py:370
  161.5 50.4 %collective-permute-start.7 = (bf16[512,1792]{1,0:T(8,128)(2,1)S(1)}, bf16[512,1792]{1,0:T(8,128)(2,1)S(1)}, u32[]{:S(2)}, u32[]{:S(2)}) collective-permute-start(bf16[512,1792]{1,0:T(8,128)(2,1)S(1)} %multiply_convert_fusion.x_ref.refs_4_), channel_id=1, source_target_pairs={{0,2},{1,3},{2,0},{3,1},{4,6},{5,7},{6,4},{7,5},{8,10},{9,11},{10,... | collective-permute-start | bytes 5505032 | tf_op jit(solution)/shard_map/ppermute | solution.py:370
  174.8 77.0 %collective-permute-start.14 = (bf16[256,1792]{1,0:T(8,128)(2,1)}, bf16[256,1792]{1,0:T(8,128)(2,1)S(1)}, u32[]{:S(2)}, u32[]{:S(2)}) collective-permute-start(bf16[256,1792]{1,0:T(8,128)(2,1)} %slice.180), channel_id=1, source_target_pairs={{0,2},{1,3},{2,0},{3,1},{4,6},{5,7},{6,4},{7,5},{8,10},{9,11},{10,... | collective-permute-start | bytes 2752520 | tf_op jit(solution)/shard_map/ppermute | solution.py:370
  178.5 73.3 %collective-permute-start.13 = (bf16[256,1792]{1,0:T(8,128)(2,1)}, bf16[256,1792]{1,0:T(8,128)(2,1)}, u32[]{:S(2)}, u32[]{:S(2)}) collective-permute-start(bf16[256,1792]{1,0:T(8,128)(2,1)} %slice.179), channel_id=1, source_target_pairs={{0,4},{1,5},{2,6},{3,7},{4,0},{5,1},{6,2},{7,3},{8,12},{9,13},{10,... | collective-permute-start | bytes 2752520 | tf_op jit(solution)/shard_map/ppermute | solution.py:370
  214.3 37.5 %collective-permute-start.12 = (bf16[256,1792]{1,0:T(8,128)(2,1)}, bf16[256,1792]{1,0:T(8,128)(2,1)}, u32[]{:S(2)}, u32[]{:S(2)}) collective-permute-start(bf16[256,1792]{1,0:T(8,128)(2,1)} %slice.150), channel_id=1, source_target_pairs={{0,2},{1,3},{2,0},{3,1},{4,6},{5,7},{6,4},{7,5},{8,10},{9,11},{10,... | collective-permute-start | bytes 2752520 | tf_op jit(solution)/shard_map/ppermute | solution.py:370
  233.9 63.9 %collective-permute-start.15 = (bf16[512,1792]{1,0:T(8,128)(2,1)}, bf16[512,1792]{1,0:T(8,128)(2,1)}, u32[]{:S(2)}, u32[]{:S(2)}) collective-permute-start(bf16[512,1792]{1,0:T(8,128)(2,1)} %get-tuple-element.164), channel_id=1, source_target_pairs={{0,2},{1,3},{2,0},{3,1},{4,6},{5,7},{6,4},{7,5},{8,10},{9,11},{10,... | collective-permute-start | bytes 5505032 | tf_op jit(solution)/shard_map/ppermute | solution.py:370
  252.7 45.1 %collective-permute-start.16 = (bf16[512,1792]{1,0:T(8,128)(2,1)}, bf16[512,1792]{1,0:T(8,128)(2,1)}, u32[]{:S(2)}, u32[]{:S(2)}) collective-permute-start(bf16[512,1792]{1,0:T(8,128)(2,1)} %get-tuple-element.165), channel_id=1, source_target_pairs={{0,4},{1,5},{2,6},{3,7},{4,0},{5,1},{6,2},{7,3},{8,12},{9,13},{10,... | collective-permute-start | bytes 5505032 | tf_op jit(solution)/shard_map/ppermute | solution.py:370
  298.0 43.5 %collective-permute-start.17 = (bf16[512,1792]{1,0:T(8,128)(2,1)}, bf16[512,1792]{1,0:T(8,128)(2,1)S(1)}, u32[]{:S(2)}, u32[]{:S(2)}) collective-permute-start(bf16[512,1792]{1,0:T(8,128)(2,1)} %get-tuple-element.168), channel_id=1, source_target_pairs={{0,6},{1,7},{2,4},{3,5},{4,2},{5,3},{6,0},{7,1},{8,14},{9,15},{10,... | collective-permute-start | bytes 5505032 | tf_op jit(solution)/shard_map/ppermute | solution.py:370
  341.4 41.7 %collective-permute-start.20 = (bf16[512,1792]{1,0:T(8,128)(2,1)}, bf16[512,1792]{1,0:T(8,128)(2,1)S(1)}, u32[]{:S(2)}, u32[]{:S(2)}) collective-permute-start(bf16[512,1792]{1,0:T(8,128)(2,1)} %convolution_convert_fusion.4), channel_id=1, source_target_pairs={{0,2},{1,3},{2,0},{3,1},{4,6},{5,7},{6,4},{7,5},{8,10},{9,11},{10,... | collective-permute-start | bytes 5505032 | tf_op jit(solution)/shard_map/ppermute | solution.py:370
  342.9 41.4 %collective-permute-start.21 = (bf16[512,1792]{1,0:T(8,128)(2,1)}, bf16[512,1792]{1,0:T(8,128)(2,1)S(1)}, u32[]{:S(2)}, u32[]{:S(2)}) collective-permute-start(bf16[512,1792]{1,0:T(8,128)(2,1)} %convolution_convert_fusion.3), channel_id=1, source_target_pairs={{0,4},{1,5},{2,6},{3,7},{4,0},{5,1},{6,2},{7,3},{8,12},{9,13},{10,... | collective-permute-start | bytes 5505032 | tf_op jit(solution)/shard_map/ppermute | solution.py:370
  343.5 65.3 %collective-permute-start.25 = (bf16[224,3584]{1,0:T(8,128)(2,1)}, bf16[224,3584]{1,0:T(8,128)(2,1)}, u32[]{:S(2)}, u32[]{:S(2)}) collective-permute-start(bf16[224,3584]{1,0:T(8,128)(2,1)} %get-tuple-element.197), channel_id=1, source_target_pairs={{0,8},{8,0},{16,24},{24,16},{1,9},{9,1},{17,25},{25,17},{2,10},{10... | collective-permute-start | bytes 4816904 | tf_op jit(solution)/shard_map/ppermute | solution.py:422
  345.0 63.9 %collective-permute-start.26 = (bf16[224,1792]{1,0:T(8,128)(2,1)}, bf16[224,1792]{1,0:T(8,128)(2,1)S(1)}, u32[]{:S(2)}, u32[]{:S(2)}) collective-permute-start(bf16[224,1792]{1,0:T(8,128)(2,1)} %get-tuple-element.198), channel_id=1, source_target_pairs={{0,16},{8,24},{16,0},{24,8},{1,17},{9,25},{17,1},{25,9},{2,18},{10... | collective-permute-start | bytes 2408456 | tf_op jit(solution)/shard_map/ppermute | solution.py:422
  424.7 38.5 %collective-permute-start.28 = (bf16[112,3584]{1,0:T(8,128)(2,1)}, bf16[112,3584]{1,0:T(8,128)(2,1)}, u32[]{:S(2)}, u32[]{:S(2)}) collective-permute-start(bf16[112,3584]{1,0:T(8,128)(2,1)} %constant_dynamic-slice_fusion.2), channel_id=1, source_target_pairs={{0,16},{8,24},{16,0},{24,8},{1,17},{9,25},{17,1},{25,9},{2,18},{10... | collective-permute-start | bytes 2408456 | tf_op jit(solution)/shard_map/ppermute | solution.py:422
  463.2 148.9 %reduce-scatter.5.cloned.1.call-start = ((), (), s32[]{:S(2)}) async-start(), calls=%async_computation.5 | async-start | bytes 7225344 | tf_op jit(solution)/shard_map/reduce_scatter | solution.py:735
  472.3 241.6 %all-reduce.3.cloned.1.call-start = ((), (), s32[]{:S(2)}) async-start(), calls=%async_computation.6 | async-start | bytes 2064384 | tf_op jit(solution)/shard_map/psum | solution.py:753
  476.2 36.9 %collective-permute-start.31 = (bf16[112,3584]{1,0:T(8,128)(2,1)S(1)}, bf16[112,3584]{1,0:T(8,128)(2,1)S(1)}, u32[]{:S(2)}, u32[]{:S(2)}) collective-permute-start(bf16[112,3584]{1,0:T(8,128)(2,1)S(1)} %add_convert_fusion.4), channel_id=1, source_target_pairs={{0,16},{8,24},{16,0},{24,8},{1,17},{9,25},{17,1},{25,9},{2,18},{10... | collective-permute-start | bytes 2408456 | tf_op jit(solution)/shard_map/ppermute | solution.py:422
  514.6 117.2 %collective-permute-start.34 = (bf16[224,3584]{1,0:T(8,128)(2,1)}, bf16[224,3584]{1,0:T(8,128)(2,1)}, u32[]{:S(2)}, u32[]{:S(2)}) collective-permute-start(bf16[224,3584]{1,0:T(8,128)(2,1)} %maximum_select_fusion.1), channel_id=1, source_target_pairs={{0,8},{8,0},{16,24},{24,16},{1,9},{9,1},{17,25},{25,17},{2,10},{10... | collective-permute-start | bytes 4816904 | tf_op jit(solution)/shard_map/ppermute | solution.py:422
  532.8 102.8 %collective-permute-start.30 = (bf16[512,1792]{1,0:T(8,128)(2,1)}, bf16[512,1792]{1,0:T(8,128)(2,1)}, u32[]{:S(2)}, u32[]{:S(2)}) collective-permute-start(bf16[512,1792]{1,0:T(8,128)(2,1)} %convolution_convert_fusion.2), channel_id=1, source_target_pairs={{0,6},{1,7},{2,4},{3,5},{4,2},{5,3},{6,0},{7,1},{8,14},{9,15},{10,... | collective-permute-start | bytes 5505032 | tf_op jit(solution)/shard_map/ppermute | solution.py:370
  536.9 94.8 %collective-permute-start.35 = (bf16[224,1792]{1,0:T(8,128)(2,1)S(1)}, bf16[224,1792]{1,0:T(8,128)(2,1)}, u32[]{:S(2)}, u32[]{:S(2)}) collective-permute-start(bf16[224,1792]{1,0:T(8,128)(2,1)S(1)} %maximum_select_fusion.3), channel_id=1, source_target_pairs={{0,16},{8,24},{16,0},{24,8},{1,17},{9,25},{17,1},{25,9},{2,18},{10... | collective-permute-start | bytes 2408456 | tf_op jit(solution)/shard_map/ppermute | solution.py:422
  (113 other events, 2154.3 us)
Sparse Core Ops, SparseCore 0:
  9.9 56.5 all-gather.2
  68.4 72.3 all-gather.4
  463.3 69.4 reduce-scatter.2
  537.0 75.0 reduce-scatter.4
  658.8 55.0 all-reduce.2

commit v3 on v2

--- a/solution.py
+++ b/solution.py
@@ -246,6 +246,18 @@
     rows = outs[0].shape[0]
     for place, out_ref in enumerate(outs):
         out_ref[...] = total[place * rows : (place + 1) * rows].astype(BF)
+
+
+def product_kernel(left_dim, right_dim, left_ref, right_ref, out_ref):
+    out_ref[...] = dot(left_ref[...], right_ref[...], left_dim, right_dim).astype(out_ref.dtype)
+
+
+def mixed_grad_kernel(left_ref, right_ref, out_ref, turned_ref):
+    @pl.when(pl.program_id(0) == 0)
+    def _():
+        turned_ref[...] = left_ref[...].T
+
+    out_ref[...] = dot(turned_ref[...], right_ref[...], 1, 1)
 
 
 def mid_grad_kernel(terms, *refs):
@@ -454,10 +466,41 @@
     )
 
 
+def rep_cycled(block, shift):
+    count = lax.axis_size("rep")
+    return lax.ppermute(block, "rep", [(i, (i + shift) % count) for i in range(count)])
+
+
+def rep_scattered(terms):
+    count = lax.axis_size("rep")
+    mine = lax.axis_index("rep")
+    rows = terms.shape[0] // count
+
+    def part(index):
+        return lax.dynamic_slice_in_dim(terms, lax.rem(index, count) * rows, rows, 0)
+
+    return [part(mine)] + [rep_cycled(part(mine + s), s) for s in range(1, count)]
+
+
+def rep_gathered(block):
+    count = lax.axis_size("rep")
+    mine = lax.axis_index("rep")
+    parts = [block] + [rep_cycled(block, s) for s in range(1, count)]
+    return jnp.concatenate(
+        [
+            sum(
+                jnp.where(lax.rem(mine - index + count, count) == s, part.astype(F32), 0.0)
+                for s, part in enumerate(parts)
+            )
+            for index in range(count)
+        ],
+        axis=0,
+    )
+
+
 class SumQueue:
     def __init__(self, orders, parts):
         self.parts = list(parts)
-        self.order = orders[0]
         self.plans = [self.plan(order, 1) for order in orders]
         self.start()
 
@@ -481,12 +524,9 @@
                 merge = added if halving else functools.partial(joined, step=step)
                 self.parts[place] = merge(self.kept[place], self.moved[place])
 
-    def turn(self, value, late=None):
+    def turn(self, value):
         value, self.moved = lax.optimization_barrier((value, self.moved))
         self.end()
-        if late is not None:
-            self.parts.append(late)
-            self.plans.append(self.plan(self.order, 0))
         self.start()
         return value
 
@@ -706,7 +746,14 @@
         (tile_spec, tile_spec, gain_spec),
         0, 0, *back_terms, residual, grad_out, ffn_gain[None],
     )
-    grad_att = dot(full_out, grad_branch, 1, 1)
+    block_rows = 256
+    blocks = (v_width // block_rows,)
+    rows_spec = pl.BlockSpec((block_rows, model_width), lambda i: (i, 0))
+    columns_spec = pl.BlockSpec((block_rows, row_count), lambda i: (i, 0))
+    grad_att = call(
+        functools.partial(product_kernel, 1, 1), v_wide, blocks,
+        [rows_spec, tokens_spec], columns_spec, 0, 0, full_out, grad_branch,
+    )
     state_grads, dnum, dden = call(
         state_grad_kernel, (states_low, v_low, head_rows), grid,
         [v_spec, v_spec, row_spec, qk_spec, one_row, table, table, column],
@@ -715,7 +762,15 @@
         grad_att, output, denom, qk, cont, left_low, right_low, query_scale,
     )
     state_grads, result_terms = lax.optimization_barrier((state_grads, result_terms))
+    late_attended, state_grads = lax.optimization_barrier((attended, state_grads))
     near_grads = stack_near(state_grads)
+    out_terms = call(
+        functools.partial(product_kernel, 1, 0),
+        jax.ShapeDtypeStruct((v_width, model_width), BF), blocks,
+        [columns_spec, tokens_spec], rows_spec, 0, 0, late_attended, grad_branch,
+    )
+    dnum, out_terms, moved = lax.optimization_barrier((dnum, out_terms, moved))
+    queue = SumQueue(orders, [added(k, m) for k, m in zip(kept, moved)])
     grad_queries, dk_local, dv_local = call(
         local_grad_kernel, (qk_low, qk_wide, v_wide), grid,
         [qk_spec, k_spec, v_spec, v_spec, row_spec, square, state_spec, one_row,
@@ -725,13 +780,12 @@
         qk, qk, values, dnum, dden, allowed, state_in, cont,
         left_low, right_low, left_t, right_t, query_scale,
     )
-    dk_local, dv_local, near_grads, moved = lax.optimization_barrier(
-        (dk_local, dv_local, near_grads, moved)
-    )
+    dk_local, dv_local, near_grads = lax.optimization_barrier((dk_local, dv_local, near_grads))
     grad_stacks = stack_all(state_grads, near_grads)
-    queue = SumQueue(orders, [added(k, m) for k, m in zip(kept, moved)])
-    late_attended, grad_stacks[0] = lax.optimization_barrier((attended, grad_stacks[0]))
-    out_terms = dot(late_attended, grad_branch, 1, 0).astype(BF)
+    last_result, out_terms, grad_stacks[0] = lax.optimization_barrier(
+        (last_result, out_terms, grad_stacks[0])
+    )
+    result_terms.append(exchanged(last_result, offsets[-1]))
     out_shard = lax.psum_scatter(out_terms, "grp", scatter_dimension=0, tiled=True)
     earlier = sources[None, :] == sources[:, None] - 1
     previous_ids = jnp.sum(jnp.where(earlier, source_ids[None, :], 0.0), axis=1)
@@ -745,15 +799,37 @@
         late_marks, *grad_stacks, qk, values, own, dk_local, dv_local,
         left_low, right_low, left_t, right_t, key_scale,
     )
+    grad_keys, grad_values = queue.turn((grad_keys, grad_values))
     grad_projected = jnp.concatenate([grad_queries, grad_keys, grad_values], axis=0)
-    in_terms = dot(mixed, grad_projected, 0, 1).astype(BF)
-    in_terms = queue.turn(in_terms)
+    in_width = full_in.shape[1]
+    in_terms = call(
+        functools.partial(product_kernel, 0, 1),
+        jax.ShapeDtypeStruct((model_width, in_width), BF), (model_width // block_rows,),
+        [pl.BlockSpec((row_count, block_rows), lambda i: (0, i)), whole(in_width, row_count)],
+        pl.BlockSpec((block_rows, in_width), lambda i: (i, 0)),
+        0, 0, mixed, grad_projected,
+    )
+    in_terms, result_terms = queue.turn((in_terms, result_terms))
+    grad_projected, queue.kept = lax.optimization_barrier((grad_projected, queue.kept))
+    ffn_result = sum(term.astype(F32) for term in [results[0], *result_terms])
+    mixed_out = (residual + ffn_result).astype(BF)
+    sum_ffn = jnp.sum(keep_rows * jnp.sum(ffn_result * ffn_result, axis=1))
+    mixed_out, sum_ffn, grad_projected = lax.optimization_barrier(
+        (mixed_out, sum_ffn, grad_projected)
+    )
     in_shard = lax.psum_scatter(in_terms, "grp", scatter_dimension=0, tiled=True)
-    in_shard, last_result = lax.optimization_barrier((in_shard, last_result))
-    grad_mix_in = lax.psum(in_shard, "rep").astype(F32)
-    result_terms.append(exchanged(last_result, offsets[-1]))
-    grad_mixed = dot(grad_projected, full_in, 0, 1)
-    grad_mixed = queue.turn(grad_mixed, out_shard)
+    grad_mixed = call(
+        mixed_grad_kernel, tokens_wide, (model_width // block_rows,),
+        [
+            whole(in_width, row_count),
+            pl.BlockSpec((block_rows, in_width), lambda i: (i, 0)),
+        ],
+        pl.BlockSpec((row_count, block_rows), lambda i: (0, i)),
+        0, 0, grad_projected, full_in,
+        scratch=[pltpu.VMEM((row_count, in_width), BF)],
+    )
+    grad_mixed, out_shard = lax.optimization_barrier((grad_mixed, out_shard))
+    out_parts = rep_scattered(out_shard)
     edge_back = jnp.concatenate([grad_mixed[:2] * gated[:2], id_float[:2, None]], axis=1)
     edge_back = passed_along(edge_back, "grp", -1)
     ext_grad_ids = jnp.concatenate([id_float, edge_back[:, model_width]], axis=0)
@@ -773,22 +849,25 @@
         scratch=[pltpu.VMEM((row_count, model_width), F32)],
     )
 
-    grad_tokens, sums = queue.turn((grad_tokens, sums))
-    grad_ffn_in, grad_ffn_out, grad_mix_out = queue.finish()
-    ffn_result = sum(term.astype(F32) for term in [results[0], *result_terms])
-    mixed_out = (residual + ffn_result).astype(BF)
+    grad_tokens, sums, out_parts = queue.turn((grad_tokens, sums, out_parts))
+    grad_ffn_in, grad_ffn_out = queue.finish()
+    in_shard, grad_tokens, sums = lax.optimization_barrier((in_shard, grad_tokens, sums))
+    in_parts = rep_scattered(in_shard)
 
     stat_terms = jnp.stack(
         [
             jnp.sum(keep_rows * jnp.sum(x_full * x_full, axis=1)),
             jnp.sum(keep_rows * jnp.sum(branch * branch, axis=1)),
-            jnp.sum(keep_rows * jnp.sum(ffn_result * ffn_result, axis=1)),
+            sum_ffn,
             jnp.sum(keep_rows),
         ]
     )
     small = jnp.concatenate([sums.reshape(-1), grad_ffn_gain[0], stat_terms])
     small = jnp.pad(small, (0, -small.shape[0] % 1024)).reshape(-1, LANES)
-    small = butterfly_sum(small).reshape(-1)
+    in_parts, small = lax.optimization_barrier((in_parts, butterfly_sum(small)))
+    small = small.reshape(-1)
+    grad_mix_in = rep_gathered(sum(p.astype(F32) for p in in_parts).astype(BF))
+    grad_mix_out = rep_gathered(sum(p.astype(F32) for p in out_parts).astype(BF))
     rows = small[: 5 * model_width].reshape(5, model_width)
     stats = small[5 * model_width : 5 * model_width + 4]
     layer_stats = jnp.sqrt(stats[:3] / (jnp.maximum(stats[3], 1.0) * model_width))
@@ -798,7 +877,7 @@
         rows[0],
         rows[1:4].T,
         grad_mix_in,
-        grad_mix_out.astype(F32),
+        grad_mix_out,
         rows[4],
         grad_ffn_in.astype(F32),
         grad_ffn_out.astype(F32),

time: 737 us -> 669 us (0.908)
  waiting for transfers between devices: 282 us -> 198 us
  Pallas kernels: 202 us -> 239 us
  matrix products: 63.7 us -> 29.9 us
  starting transfers between devices: 51.3 us -> 62.5 us
    reduce_scatter x1, waiting for transfers between devices: 71.4 us -> 0.01 us  [body(): lax.psum_scatter(out_terms, 'grp', scatter_dimension=0, tiled=True)]
    pallas_call x14 -> x18, Pallas kernels: 202 us -> 239 us  [call(): pl.pallas_call(kernel, out_shape=outs, grid=grid, in_specs=in_specs, out_...]
    dot_general x11 -> x7, matrix products: 63.7 us -> 29.9 us  [dot(): lax.dot_general(left, right, (((left_dim,), (right_dim,)), ((), ())), pre...]
    ppermute x0 -> x12, waiting for transfers between devices: none -> 26.9 us  [rep_cycled(): lax.ppermute(block, 'rep', [(i, (i + shift) % count) for i in range(count)])]
    psum x1 -> x0, waiting for transfers between devices: 26.6 us -> none  [body(): grad_mix_in = lax.psum(in_shard, 'rep').astype(F32)]
    reduce_scatter x1, waiting for transfers between devices: 17.3 us -> 0.01 us  [body(): lax.psum_scatter(in_terms, 'grp', scatter_dimension=0, tiled=True)]
    ppermute x0 -> x12, starting transfers between devices: none -> 13.2 us  [rep_cycled(): lax.ppermute(block, 'rep', [(i, (i + shift) % count) for i in range(count)])]
    ppermute x12 -> x8, waiting for transfers between devices: 49.6 us -> 42 us  [rep_swap(): return lax.ppermute(block, 'rep', [(i, i ^ step) for i in range(count)])]
  transfers between devices with their start and end apart: 50 -> 57, of which waited for: 19 -> 25; matrix products, arithmetic and copies ran while one was open for 20% -> 17% of each run, Pallas kernels for 28% -> 36%
where the time goes in v3:
time: 669 us; the launch traced here: 658 us
  Pallas kernels  239 us (36%)
  waiting for transfers between devices  198 us (30%)
  starting transfers between devices  62.5 us (9%)
  other arithmetic  61.7 us (9%)
  local copies, waits for them, and re-layouts  47.8 us (7%)
  matrix products  29.9 us (4%)
  between operations  18.9 us (3%)
    pallas_call x18, Pallas kernels, call(): pl.pallas_call(kernel, out_shape=outs, grid=grid, in_specs=in_specs, out_...  239 us
    ppermute x26, waiting for transfers between devices, exchanged(): return lax.ppermute(block, 'grp', [(i, i ^ offset) for i in range(count)])  77.4 us
    ppermute x8, waiting for transfers between devices, rep_swap(): return lax.ppermute(block, 'rep', [(i, i ^ step) for i in range(count)])  42 us
    dot_general x7, matrix products, dot(): lax.dot_general(left, right, (((left_dim,), (right_dim,)), ((), ())), pre...  29.9 us
    all_gather x1, waiting for transfers between devices, body(): full_in = lax.all_gather(mix_in, 'grp', axis=0, tiled=True)  29.6 us
    ppermute x12, waiting for transfers between devices, rep_cycled(): lax.ppermute(block, 'rep', [(i, (i + shift) % count) for i in range(count)])  26.9 us
    ppermute x26, starting transfers between devices, exchanged(): return lax.ppermute(block, 'grp', [(i, i ^ offset) for i in range(count)])  25.3 us
    unnamed x164, local copies, waits for them, and re-layouts  25 us
  transfers between devices with their start and end apart: 57, of which 25 were waited for; matrix products, arithmetic and copies ran while one was open for 17% of the time, Pallas kernels for 36%

profile of v3, /device:TPU:0, one launch (start us, length us, event | category | flops | bytes accessed | tf_op | source)
XLA Modules:
  0.0 657.5 jit_solution(6876998969977531799)
XLA Ops:
  36.9 29.6 %all-gather.3.cloned.1.call-done.right_ref = bf16[1792,2304]{1,0:T(8,128)(2,1)} async-done(((bf16[224,2304]{1,0:T(8,128)(2,1)}), bf16[1792,2304]{1,0:T(8,128)(2,1)}) %all-gather.3.cloned.1.call-update) | async-done | bytes 8257552 | tf_op jit(solution)/shard_map/all_gather | solution.py:550
  86.5 10.4 %shard_map.250 = (f32[1792,512]{1,0:T(8,128)}, f32[16,1,512]{2,1,0:T(1,128)S(1)}) custom-call(bf16[512,512]{1,0:T(8,128)(2,1)S(1)} %fusion.21.keys_ref.queries_ref.refs_2_, bf16[512,512]{1,0:T(8,128)(2,1)S(1)} %fusion.21.keys_ref.queries_ref.refs_2_, bf16[1792,512]{1,0:T(8,128)(2,1)S(1)} %fusion.12.values_ref.refs_3_, f32[512,512]{1,0:T(8,128)S(1)} %fusion.25.allowed_ref), custom_call_target="tpu_custom_call" | custom-call | tf_op jit(solution)/shard_map/pallas_call | solution.py:353
  102.5 18.4 %collective-permute-done.4 = bf16[16,160,128]{2,1,0:T(8,128)(2,1)S(1)} collective-permute-done((bf16[16,160,128]{2,1,0:T(8,128)(2,1)S(1)}, bf16[16,160,128]{2,1,0:T(8,128)(2,1)S(1)}, u32[]{:S(2)}, u32[]{:S(2)}) %collective-permute-start.4) | collective-permute-done | bytes 655392 | tf_op jit(solution)/shard_map/ppermute | solution.py:382
  133.0 14.3 %shard_map.251 = (bf16[1792,512]{1,0:T(8,128)(2,1)S(1)}, f32[1792,512]{1,0:T(8,128)}, f32[16,1,512]{2,1,0:T(1,128)S(1)}, f32[16,160,128]{2,1,0:T(8,128)S(1)}) custom-call(f32[8]{0:T(128)S(1)} %get-tuple-element.326.marks_ref, bf16[4,16,160,128]{3,2,1,0:T(8,128)(2,1)} %pad_maximum_fusion.3.refs_0_, bf16[4,16,160,128]{3,2,1,0:T(8,128)(2,1)} %collective-permute-done.6.refs_1_, ...), custom_call_target="tpu_custom_call" | custom-call | tf_op jit(solution)/shard_map/pallas_call | solution.py:353
  161.1 11.5 %collective-permute-done.10.dy_ref.refs_6_ = bf16[512,1792]{1,0:T(8,128)(2,1)} collective-permute-done((bf16[512,1792]{1,0:T(8,128)(2,1)}, bf16[512,1792]{1,0:T(8,128)(2,1)}, u32[]{:S(2)}, u32[]{:S(2)}) %collective-permute-start.10) | collective-permute-done | bytes 1835040 | tf_op jit(solution)/shard_map/ppermute | solution.py:382
  179.0 16.9 %shard_map.252 = (bf16[1,512,896]{2,1,0:T(8,128)(2,1)S(1)}, bf16[2,512,896]{2,1,0:T(8,128)(2,1)S(1)}, bf16[512,1792]{1,0:T(8,128)(2,1)}) custom-call(bf16[512,1792]{1,0:T(8,128)(2,1)} %copy-done.40, bf16[512,1792]{1,0:T(8,128)(2,1)} %refs_5_.1, bf16[896,3584]{1,0:T(8,128)(2,1)} %pad_maximum_fusion.w_in_ref, bf16[896,1792]{1,0:T(8,128)(2,1)} %pad_maximum_fusion.2.w_out_ref), custom_call_target="tpu_custom_call" | custom-call | tf_op jit(solution)/shard_map/pallas_call | solution.py:353
  195.8 16.0 %collective-permute-done.8.x_ref.refs_6_ = bf16[512,1792]{1,0:T(8,128)(2,1)S(1)} collective-permute-done((bf16[512,1792]{1,0:T(8,128)(2,1)S(1)}, bf16[512,1792]{1,0:T(8,128)(2,1)S(1)}, u32[]{:S(2)}, u32[]{:S(2)}) %collective-permute-start.8) | collective-permute-done | bytes 1835040 | tf_op jit(solution)/shard_map/ppermute | solution.py:382
  216.3 16.5 %shard_map.253 = (bf16[1,512,896]{2,1,0:T(8,128)(2,1)S(1)}, bf16[2,512,896]{2,1,0:T(8,128)(2,1)S(1)}, bf16[512,1792]{1,0:T(8,128)(2,1)}) custom-call(bf16[512,1792]{1,0:T(8,128)(2,1)} %copy-done.42, bf16[512,1792]{1,0:T(8,128)(2,1)} %collective-permute-done.9.dy_ref.refs_5_, bf16[896,3584]{1,0:T(8,128)(2,1)} %pad_maximum_fusion.w_in_ref, ...), custom_call_target="tpu_custom_call" | custom-call | tf_op jit(solution)/shard_map/pallas_call | solution.py:353
  233.6 16.7 %shard_map.254 = (bf16[1,512,896]{2,1,0:T(8,128)(2,1)S(1)}, bf16[2,512,896]{2,1,0:T(8,128)(2,1)S(1)}, bf16[512,1792]{1,0:T(8,128)(2,1)}) custom-call(bf16[512,1792]{1,0:T(8,128)(2,1)} %copy-done.41, bf16[512,1792]{1,0:T(8,128)(2,1)} %collective-permute-done.10.dy_ref.refs_6_, bf16[896,3584]{1,0:T(8,128)(2,1)} %pad_maximum_fusion.w_in_ref, ...), custom_call_target="tpu_custom_call" | custom-call | tf_op jit(solution)/shard_map/pallas_call | solution.py:353
  258.2 16.5 %shard_map.255 = (bf16[1,512,896]{2,1,0:T(8,128)(2,1)S(1)}, bf16[2,512,896]{2,1,0:T(8,128)(2,1)S(1)}, bf16[512,1792]{1,0:T(8,128)(2,1)}) custom-call(bf16[512,1792]{1,0:T(8,128)(2,1)} %copy-done.43, bf16[512,1792]{1,0:T(8,128)(2,1)} %copy-done.44, bf16[896,3584]{1,0:T(8,128)(2,1)} %pad_maximum_fusion.w_in_ref, bf16[896,1792]{1,0:T(8,128)(2,1)} %pad_maximum_fusion.2.w_out_ref), custom_call_target="tpu_custom_call" | custom-call | tf_op jit(solution)/shard_map/pallas_call | solution.py:353
  276.0 20.6 %shard_map.256 = (bf16[448,3584]{1,0:T(8,128)(2,1)}, bf16[448,3584]{1,0:T(8,128)(2,1)}) custom-call(bf16[2,512,896]{2,1,0:T(8,128)(2,1)S(1)} %get-tuple-element.184.refs_0_, bf16[2,512,896]{2,1,0:T(8,128)(2,1)S(1)} %get-tuple-element.185.refs_1_, bf16[2,512,896]{2,1,0:T(8,128)(2,1)} %copy-done.10, bf16[2,512,896]{2,1,0:T(8,128)(2,1)} %copy-done.11, ...), custom_call_target="tpu_custom_call" | custom-call | tf_op jit(solution)/shard_map/pallas_call | solution.py:353
  300.7 11.1 %shard_map.257 = (bf16[448,1792]{1,0:T(8,128)(2,1)}, bf16[448,1792]{1,0:T(8,128)(2,1)}) custom-call(bf16[1,512,896]{2,1,0:T(8,128)(2,1)S(1)} %get-tuple-element.195.refs_0_, bf16[1,512,896]{2,1,0:T(8,128)(2,1)S(1)} %get-tuple-element.196.refs_1_, bf16[1,512,896]{2,1,0:T(8,128)(2,1)S(1)} %copy-done.19, bf16[1,512,896]{2,1,0:T(8,128)(2,1)S(1)} %copy-done.21, ...), custom_call_target="tpu_custom_call" | custom-call | tf_op jit(solution)/shard_map/pallas_call | solution.py:353
  364.6 13.3 %shard_map.260 = (bf16[16,160,128]{2,1,0:T(8,128)(2,1)}, bf16[1792,512]{1,0:T(8,128)(2,1)S(1)}, f32[16,1,512]{2,1,0:T(1,128)S(1)}) custom-call(f32[1792,512]{1,0:T(8,128)} %shard_map.259.grad_ref, f32[1792,512]{1,0:T(8,128)} %get-tuple-element.209.output_ref, f32[16,1,512]{2,1,0:T(1,128)S(1)} %get-tuple-element.210.denom_ref, ...), custom_call_target="tpu_custom_call" | custom-call | tf_op jit(solution)/shard_map/pallas_call | solution.py:353
  397.0 21.2 %shard_map.262 = (bf16[256,512]{1,0:T(8,128)(2,1)S(1)}, f32[256,512]{1,0:T(8,128)S(1)}, f32[1792,512]{1,0:T(8,128)}) custom-call(bf16[512,512]{1,0:T(8,128)(2,1)S(1)} %fusion.21.keys_ref.queries_ref.refs_2_, bf16[512,512]{1,0:T(8,128)(2,1)S(1)} %fusion.21.keys_ref.queries_ref.refs_2_, bf16[1792,512]{1,0:T(8,128)(2,1)} %copy-done, ...), custom_call_target="tpu_custom_call" | custom-call | tf_op jit(solution)/shard_map/pallas_call | solution.py:353
  435.4 14.7 %shard_map.263 = (bf16[256,512]{1,0:T(8,128)(2,1)S(1)}, bf16[1792,512]{1,0:T(8,128)(2,1)S(1)}) custom-call(f32[8]{0:T(128)S(1)} %copy-done.35, bf16[4,16,160,128]{3,2,1,0:T(8,128)(2,1)} %pad_maximum_fusion.4.refs_0_, bf16[4,16,160,128]{3,2,1,0:T(8,128)(2,1)} %collective-permute-done.27.refs_1_, bf16[512,512]{1,0:T(8,128)(2,1)S(1)} %fusion.21.keys_ref.queries_ref.refs_2_, ...), custom_call_target="tpu_custom_call" | custom-call | tf_op jit(solution)/shard_map/pallas_call | solution.py:353
  455.8 9.5 %collective-permute-done.28 = bf16[112,3584]{1,0:T(8,128)(2,1)} collective-permute-done((bf16[112,3584]{1,0:T(8,128)(2,1)}, bf16[112,3584]{1,0:T(8,128)(2,1)}, u32[]{:S(2)}, u32[]{:S(2)}) %collective-permute-start.28) | collective-permute-done | bytes 802848 | tf_op jit(solution)/shard_map/ppermute | solution.py:434
  473.3 9.1 %shard_map.264 = bf16[1792,2304]{1,0:T(8,128)(2,1)} custom-call(bf16[512,1792]{1,0:T(8,128)(2,1)S(1)} %copy-done.7, bf16[2304,512]{1,0:T(8,128)(2,1)} %copy-done.1), custom_call_target="tpu_custom_call" | custom-call | tf_op jit(solution)/shard_map/pallas_call | solution.py:353
  482.5 10.5 %collective-permute-done.30 = bf16[512,1792]{1,0:T(8,128)(2,1)} collective-permute-done((bf16[512,1792]{1,0:T(8,128)(2,1)}, bf16[512,1792]{1,0:T(8,128)(2,1)}, u32[]{:S(2)}, u32[]{:S(2)}) %collective-permute-start.30) | collective-permute-done | bytes 1835040 | tf_op jit(solution)/shard_map/ppermute | solution.py:382
  493.0 10.1 %collective-permute-done.31 = bf16[112,3584]{1,0:T(8,128)(2,1)} collective-permute-done((bf16[112,3584]{1,0:T(8,128)(2,1)S(1)}, bf16[112,3584]{1,0:T(8,128)(2,1)}, u32[]{:S(2)}, u32[]{:S(2)}) %collective-permute-start.31) | collective-permute-done | bytes 802848 | tf_op jit(solution)/shard_map/ppermute | solution.py:434
  516.4 10.9 %shard_map.265.mixed_ref = f32[512,1792]{1,0:T(8,128)} custom-call(bf16[2304,512]{1,0:T(8,128)(2,1)S(1)} %copy-done.2, bf16[1792,2304]{1,0:T(8,128)(2,1)} %all-gather.3.cloned.1.call-done.right_ref), custom_call_target="tpu_custom_call" | custom-call | tf_op jit(solution)/shard_map/pallas_call | solution.py:353
  535.0 16.4 %shard_map.266 = (bf16[512,1792]{1,0:T(8,128)(2,1)}, f32[4,1792]{1,0:T(4,128)S(1)}) custom-call(bf16[512,1792]{1,0:T(8,128)(2,1)S(1)} %copy-done.5, f32[2,1792]{1,0:T(2,128)S(1)} %slice.181.before_ref, f32[2,1792]{1,0:T(2,128)S(1)} %slice.183.after_ref, f32[512,1]{1,0:T(8,128)S(1)} %copy.59.scale_ref, f32[512,4]{1,0:T(8,128)S(1)} %copy.60.flags_ref, ...), custom_call_target="tpu_custom_call" | custom-call | tf_op jit(solution)/shard_map/pallas_call | solution.py:353
  551.4 15.1 %collective-permute-done.37 = bf16[224,3584]{1,0:T(8,128)(2,1)} collective-permute-done((bf16[224,3584]{1,0:T(8,128)(2,1)}, bf16[224,3584]{1,0:T(8,128)(2,1)}, u32[]{:S(2)}, u32[]{:S(2)}) %collective-permute-start.37) | collective-permute-done | bytes 1605664 | tf_op jit(solution)/shard_map/ppermute | solution.py:434
  607.3 16.9 %collective-permute-done.46 = f32[72,128]{1,0:T(8,128)S(1)} collective-permute-done((f32[72,128]{1,0:T(8,128)S(1)}, f32[72,128]{1,0:T(8,128)S(1)}, u32[]{:S(2)}, u32[]{:S(2)}) %collective-permute-start.46) | collective-permute-done | bytes 36896 | tf_op jit(solution)/shard_map/ppermute | solution.py:413
  634.5 14.3 %collective-permute-done.48 = bf16[56,2304]{1,0:T(8,128)(2,1)S(1)} collective-permute-done((bf16[56,2304]{1,0:T(8,128)(2,1)S(1)}, bf16[56,2304]{1,0:T(8,128)(2,1)S(1)}, u32[]{:S(2)}, u32[]{:S(2)}) %collective-permute-start.48) | collective-permute-done | bytes 258080 | tf_op jit(solution)/shard_map/ppermute | solution.py:471
  (378 shorter events, 278.3 us)
Async XLA Ops:
  7.2 59.3 %all-gather.3.cloned.1.call-start = ((), (), s32[]{:S(2)}) async-start(), calls=%async_computation.2 | async-start | bytes 9289728 | tf_op jit(solution)/shard_map/all_gather | solution.py:550
  7.9 141.8 %all-gather.5.cloned.1.call-start = ((), (), s32[]{:S(2)}) async-start(), calls=%async_computation.3 | async-start | bytes 7225344 | tf_op jit(solution)/shard_map/all_gather | solution.py:551
  8.7 518.6 %reduce-scatter.5.cloned.1.call-start = ((), (), s32[]{:S(2)}) async-start(), calls=%async_computation.5 | async-start | bytes 7225344 | tf_op jit(solution)/shard_map/reduce_scatter | solution.py:789
  123.3 49.3 %collective-permute-start.10 = (bf16[512,1792]{1,0:T(8,128)(2,1)}, bf16[512,1792]{1,0:T(8,128)(2,1)}, u32[]{:S(2)}, u32[]{:S(2)}) collective-permute-start(bf16[512,1792]{1,0:T(8,128)(2,1)} %refs_5_.1), channel_id=1, source_target_pairs={{0,4},{1,5},{2,6},{3,7},{4,0},{5,1},{6,2},{7,3},{8,12},{9,13},{10,... | collective-permute-start | bytes 5505032 | tf_op jit(solution)/shard_map/ppermute | solution.py:382
  124.0 52.3 %collective-permute-start.9 = (bf16[512,1792]{1,0:T(8,128)(2,1)}, bf16[512,1792]{1,0:T(8,128)(2,1)}, u32[]{:S(2)}, u32[]{:S(2)}) collective-permute-start(bf16[512,1792]{1,0:T(8,128)(2,1)} %refs_5_.1), channel_id=1, source_target_pairs={{0,2},{1,3},{2,0},{3,1},{4,6},{5,7},{6,4},{7,5},{8,10},{9,11},{10,... | collective-permute-start | bytes 5505032 | tf_op jit(solution)/shard_map/ppermute | solution.py:382
  159.2 52.6 %collective-permute-start.8 = (bf16[512,1792]{1,0:T(8,128)(2,1)S(1)}, bf16[512,1792]{1,0:T(8,128)(2,1)S(1)}, u32[]{:S(2)}, u32[]{:S(2)}) collective-permute-start(bf16[512,1792]{1,0:T(8,128)(2,1)S(1)} %multiply_convert_fusion.x_ref.refs_4_), channel_id=1, source_target_pairs={{0,4},{1,5},{2,6},{3,7},{4,0},{5,1},{6,2},{7,3},{8,12},{9,13},{10,... | collective-permute-start | bytes 5505032 | tf_op jit(solution)/shard_map/ppermute | solution.py:382
  159.8 52.1 %collective-permute-start.7 = (bf16[512,1792]{1,0:T(8,128)(2,1)S(1)}, bf16[512,1792]{1,0:T(8,128)(2,1)S(1)}, u32[]{:S(2)}, u32[]{:S(2)}) collective-permute-start(bf16[512,1792]{1,0:T(8,128)(2,1)S(1)} %multiply_convert_fusion.x_ref.refs_4_), channel_id=1, source_target_pairs={{0,2},{1,3},{2,0},{3,1},{4,6},{5,7},{6,4},{7,5},{8,10},{9,11},{10,... | collective-permute-start | bytes 5505032 | tf_op jit(solution)/shard_map/ppermute | solution.py:382
  174.8 75.5 %collective-permute-start.14 = (bf16[256,1792]{1,0:T(8,128)(2,1)}, bf16[256,1792]{1,0:T(8,128)(2,1)S(1)}, u32[]{:S(2)}, u32[]{:S(2)}) collective-permute-start(bf16[256,1792]{1,0:T(8,128)(2,1)} %slice.180), channel_id=1, source_target_pairs={{0,2},{1,3},{2,0},{3,1},{4,6},{5,7},{6,4},{7,5},{8,10},{9,11},{10,... | collective-permute-start | bytes 2752520 | tf_op jit(solution)/shard_map/ppermute | solution.py:382
  178.4 71.8 %collective-permute-start.13 = (bf16[256,1792]{1,0:T(8,128)(2,1)}, bf16[256,1792]{1,0:T(8,128)(2,1)}, u32[]{:S(2)}, u32[]{:S(2)}) collective-permute-start(bf16[256,1792]{1,0:T(8,128)(2,1)} %slice.179), channel_id=1, source_target_pairs={{0,4},{1,5},{2,6},{3,7},{4,0},{5,1},{6,2},{7,3},{8,12},{9,13},{10,... | collective-permute-start | bytes 2752520 | tf_op jit(solution)/shard_map/ppermute | solution.py:382
  232.8 63.8 %collective-permute-start.15 = (bf16[512,1792]{1,0:T(8,128)(2,1)}, bf16[512,1792]{1,0:T(8,128)(2,1)}, u32[]{:S(2)}, u32[]{:S(2)}) collective-permute-start(bf16[512,1792]{1,0:T(8,128)(2,1)} %get-tuple-element.190), channel_id=1, source_target_pairs={{0,2},{1,3},{2,0},{3,1},{4,6},{5,7},{6,4},{7,5},{8,10},{9,11},{10,... | collective-permute-start | bytes 5505032 | tf_op jit(solution)/shard_map/ppermute | solution.py:382
  252.4 44.2 %collective-permute-start.16 = (bf16[512,1792]{1,0:T(8,128)(2,1)}, bf16[512,1792]{1,0:T(8,128)(2,1)}, u32[]{:S(2)}, u32[]{:S(2)}) collective-permute-start(bf16[512,1792]{1,0:T(8,128)(2,1)} %get-tuple-element.191), channel_id=1, source_target_pairs={{0,4},{1,5},{2,6},{3,7},{4,0},{5,1},{6,2},{7,3},{8,12},{9,13},{10,... | collective-permute-start | bytes 5505032 | tf_op jit(solution)/shard_map/ppermute | solution.py:382
  296.8 43.5 %collective-permute-start.17 = (bf16[512,1792]{1,0:T(8,128)(2,1)}, bf16[512,1792]{1,0:T(8,128)(2,1)S(1)}, u32[]{:S(2)}, u32[]{:S(2)}) collective-permute-start(bf16[512,1792]{1,0:T(8,128)(2,1)} %get-tuple-element.194), channel_id=1, source_target_pairs={{0,6},{1,7},{2,4},{3,5},{4,2},{5,3},{6,0},{7,1},{8,14},{9,15},{10,... | collective-permute-start | bytes 5505032 | tf_op jit(solution)/shard_map/ppermute | solution.py:382
  341.5 41.7 %collective-permute-start.20 = (bf16[512,1792]{1,0:T(8,128)(2,1)}, bf16[512,1792]{1,0:T(8,128)(2,1)S(1)}, u32[]{:S(2)}, u32[]{:S(2)}) collective-permute-start(bf16[512,1792]{1,0:T(8,128)(2,1)} %convolution_convert_fusion.2), channel_id=1, source_target_pairs={{0,2},{1,3},{2,0},{3,1},{4,6},{5,7},{6,4},{7,5},{8,10},{9,11},{10,... | collective-permute-start | bytes 5505032 | tf_op jit(solution)/shard_map/ppermute | solution.py:382
  342.1 41.4 %collective-permute-start.21 = (bf16[512,1792]{1,0:T(8,128)(2,1)}, bf16[512,1792]{1,0:T(8,128)(2,1)S(1)}, u32[]{:S(2)}, u32[]{:S(2)}) collective-permute-start(bf16[512,1792]{1,0:T(8,128)(2,1)} %convolution_convert_fusion.1), channel_id=1, source_target_pairs={{0,4},{1,5},{2,6},{3,7},{4,0},{5,1},{6,2},{7,3},{8,12},{9,13},{10,... | collective-permute-start | bytes 5505032 | tf_op jit(solution)/shard_map/ppermute | solution.py:382
  343.5 53.5 %collective-permute-start.22 = (bf16[224,3584]{1,0:T(8,128)(2,1)}, bf16[224,3584]{1,0:T(8,128)(2,1)}, u32[]{:S(2)}, u32[]{:S(2)}) collective-permute-start(bf16[224,3584]{1,0:T(8,128)(2,1)} %get-tuple-element.217), channel_id=1, source_target_pairs={{0,8},{8,0},{16,24},{24,16},{1,9},{9,1},{17,25},{25,17},{2,10},{10... | collective-permute-start | bytes 4816904 | tf_op jit(solution)/shard_map/ppermute | solution.py:434
  345.0 51.0 %collective-permute-start.23 = (bf16[224,1792]{1,0:T(8,128)(2,1)}, bf16[224,1792]{1,0:T(8,128)(2,1)}, u32[]{:S(2)}, u32[]{:S(2)}) collective-permute-start(bf16[224,1792]{1,0:T(8,128)(2,1)} %get-tuple-element.218), channel_id=1, source_target_pairs={{0,16},{8,24},{16,0},{24,8},{1,17},{9,25},{17,1},{25,9},{2,18},{10... | collective-permute-start | bytes 2408456 | tf_op jit(solution)/shard_map/ppermute | solution.py:434
  422.5 160.6 %reduce-scatter.3.cloned.1.call-start = ((), (), s32[]{:S(2)}) async-start(), calls=%async_computation.4 | async-start | bytes 9289728 | tf_op jit(solution)/shard_map/reduce_scatter | solution.py:820
  427.8 37.5 %collective-permute-start.28 = (bf16[112,3584]{1,0:T(8,128)(2,1)}, bf16[112,3584]{1,0:T(8,128)(2,1)}, u32[]{:S(2)}, u32[]{:S(2)}) collective-permute-start(bf16[112,3584]{1,0:T(8,128)(2,1)} %constant_dynamic-slice_fusion.9), channel_id=1, source_target_pairs={{0,16},{8,24},{16,0},{24,8},{1,17},{9,25},{17,1},{25,9},{2,18},{10... | collective-permute-start | bytes 2408456 | tf_op jit(solution)/shard_map/ppermute | solution.py:434
  434.0 59.0 %collective-permute-start.30 = (bf16[512,1792]{1,0:T(8,128)(2,1)}, bf16[512,1792]{1,0:T(8,128)(2,1)}, u32[]{:S(2)}, u32[]{:S(2)}) collective-permute-start(bf16[512,1792]{1,0:T(8,128)(2,1)} %convolution_convert_fusion), channel_id=1, source_target_pairs={{0,6},{1,7},{2,4},{3,5},{4,2},{5,3},{6,0},{7,1},{8,14},{9,15},{10,... | collective-permute-start | bytes 5505032 | tf_op jit(solution)/shard_map/ppermute | solution.py:382
  504.5 46.9 %collective-permute-start.38 = (bf16[224,1792]{1,0:T(8,128)(2,1)S(1)}, bf16[224,1792]{1,0:T(8,128)(2,1)}, u32[]{:S(2)}, u32[]{:S(2)}) collective-permute-start(bf16[224,1792]{1,0:T(8,128)(2,1)S(1)} %maximum_select_fusion.3), channel_id=1, source_target_pairs={{0,16},{8,24},{16,0},{24,8},{1,17},{9,25},{17,1},{25,9},{2,18},{10... | collective-permute-start | bytes 2408456 | tf_op jit(solution)/shard_map/ppermute | solution.py:434
  507.6 58.8 %collective-permute-start.37 = (bf16[224,3584]{1,0:T(8,128)(2,1)}, bf16[224,3584]{1,0:T(8,128)(2,1)}, u32[]{:S(2)}, u32[]{:S(2)}) collective-permute-start(bf16[224,3584]{1,0:T(8,128)(2,1)} %maximum_select_fusion.1), channel_id=1, source_target_pairs={{0,8},{8,0},{16,24},{24,16},{1,9},{9,1},{17,25},{25,17},{2,10},{10... | collective-permute-start | bytes 4816904 | tf_op jit(solution)/shard_map/ppermute | solution.py:434
  531.7 41.9 %collective-permute-start.36 = (bf16[56,1792]{1,0:T(8,128)(2,1)}, bf16[56,1792]{1,0:T(8,128)(2,1)}, u32[]{:S(2)}, u32[]{:S(2)}) collective-permute-start(bf16[56,1792]{1,0:T(8,128)(2,1)} %get-tuple-element.313), channel_id=1, source_target_pairs={{0,24},{8,0},{16,8},{24,16},{1,25},{9,1},{17,9},{25,17},{2,26},{10... | collective-permute-start | bytes 602120 | tf_op jit(solution)/shard_map/ppermute | solution.py:471
  533.8 39.8 %collective-permute-start.35 = (bf16[56,1792]{1,0:T(8,128)(2,1)}, bf16[56,1792]{1,0:T(8,128)(2,1)}, u32[]{:S(2)}, u32[]{:S(2)}) collective-permute-start(bf16[56,1792]{1,0:T(8,128)(2,1)} %get-tuple-element.314), channel_id=1, source_target_pairs={{0,16},{8,24},{16,0},{24,8},{1,17},{9,25},{17,1},{25,9},{2,18},{10... | collective-permute-start | bytes 602120 | tf_op jit(solution)/shard_map/ppermute | solution.py:471
  533.8 39.8 %collective-permute-start.34 = (bf16[56,1792]{1,0:T(8,128)(2,1)}, bf16[56,1792]{1,0:T(8,128)(2,1)}, u32[]{:S(2)}, u32[]{:S(2)}) collective-permute-start(bf16[56,1792]{1,0:T(8,128)(2,1)} %get-tuple-element.315), channel_id=1, source_target_pairs={{0,8},{8,16},{16,24},{24,0},{1,9},{9,17},{17,25},{25,1},{2,10},{10... | collective-permute-start | bytes 602120 | tf_op jit(solution)/shard_map/ppermute | solution.py:471
  (113 other events, 1520.2 us)
Sparse Core Ops, SparseCore 0:
  9.9 56.5 all-gather.2
  68.4 72.7 all-gather.4
  422.6 80.0 reduce-scatter.4
  506.3 70.2 reduce-scatter.2

commit v4 on v3

--- a/solution.py
+++ b/solution.py
@@ -849,8 +849,9 @@
         scratch=[pltpu.VMEM((row_count, model_width), F32)],
     )
 
-    grad_tokens, sums, out_parts = queue.turn((grad_tokens, sums, out_parts))
-    grad_ffn_in, grad_ffn_out = queue.finish()
+    grad_tokens, sums, out_parts, queue.moved = lax.optimization_barrier(
+        (grad_tokens, sums, out_parts, queue.moved)
+    )
     in_shard, grad_tokens, sums = lax.optimization_barrier((in_shard, grad_tokens, sums))
     in_parts = rep_scattered(in_shard)
 
@@ -864,7 +865,10 @@
     )
     small = jnp.concatenate([sums.reshape(-1), grad_ffn_gain[0], stat_terms])
     small = jnp.pad(small, (0, -small.shape[0] % 1024)).reshape(-1, LANES)
-    in_parts, small = lax.optimization_barrier((in_parts, butterfly_sum(small)))
+    in_parts, small, queue.kept = lax.optimization_barrier(
+        (in_parts, butterfly_sum(small), queue.kept)
+    )
+    grad_ffn_in, grad_ffn_out = queue.finish()
     small = small.reshape(-1)
     grad_mix_in = rep_gathered(sum(p.astype(F32) for p in in_parts).astype(BF))
     grad_mix_out = rep_gathered(sum(p.astype(F32) for p in out_parts).astype(BF))

time: 669 us -> 677 us (1.012)
  transfers between devices with their start and end apart: 57 -> 57, of which waited for: 25 -> 25; matrix products, arithmetic and copies ran while one was open for 17% -> 16% of each run, Pallas kernels for 36% -> 36%
where the time goes in v4:
time: 677 us; the launch traced here: 665 us
  Pallas kernels  239 us (35%)
  waiting for transfers between devices  204 us (30%)
  starting transfers between devices  64 us (9%)
  other arithmetic  61.6 us (9%)
  local copies, waits for them, and re-layouts  47.9 us (7%)
  matrix products  29.9 us (4%)
  between operations  18.9 us (3%)
    pallas_call x18, Pallas kernels, call(): pl.pallas_call(kernel, out_shape=outs, grid=grid, in_specs=in_specs, out_...  239 us
    ppermute x26, waiting for transfers between devices, exchanged(): return lax.ppermute(block, 'grp', [(i, i ^ offset) for i in range(count)])  77.4 us
    ppermute x8, waiting for transfers between devices, rep_swap(): return lax.ppermute(block, 'rep', [(i, i ^ step) for i in range(count)])  41.9 us
    ppermute x12, waiting for transfers between devices, rep_cycled(): lax.ppermute(block, 'rep', [(i, (i + shift) % count) for i in range(count)])  31 us
    dot_general x7, matrix products, dot(): lax.dot_general(left, right, (((left_dim,), (right_dim,)), ((), ())), pre...  29.9 us
    all_gather x1, waiting for transfers between devices, body(): full_in = lax.all_gather(mix_in, 'grp', axis=0, tiled=True)  29.6 us
    ppermute x26, starting transfers between devices, exchanged(): return lax.ppermute(block, 'grp', [(i, i ^ offset) for i in range(count)])  25.3 us
    unnamed x164, local copies, waits for them, and re-layouts  25 us
  transfers between devices with their start and end apart: 57, of which 25 were waited for; matrix products, arithmetic and copies ran while one was open for 16% of the time, Pallas kernels for 36%

profile of v4, /device:TPU:0, one launch (start us, length us, event | category | flops | bytes accessed | tf_op | source)
XLA Modules:
  0.0 665.5 jit_solution(10419044628356798793)
XLA Ops:
  36.9 29.6 %all-gather.3.cloned.1.call-done.right_ref = bf16[1792,2304]{1,0:T(8,128)(2,1)} async-done(((bf16[224,2304]{1,0:T(8,128)(2,1)}), bf16[1792,2304]{1,0:T(8,128)(2,1)}) %all-gather.3.cloned.1.call-update) | async-done | bytes 8257552 | tf_op jit(solution)/shard_map/all_gather | solution.py:550
  86.5 10.4 %shard_map.250 = (f32[1792,512]{1,0:T(8,128)}, f32[16,1,512]{2,1,0:T(1,128)S(1)}) custom-call(bf16[512,512]{1,0:T(8,128)(2,1)S(1)} %fusion.21.keys_ref.queries_ref.refs_2_, bf16[512,512]{1,0:T(8,128)(2,1)S(1)} %fusion.21.keys_ref.queries_ref.refs_2_, bf16[1792,512]{1,0:T(8,128)(2,1)S(1)} %fusion.12.values_ref.refs_3_, f32[512,512]{1,0:T(8,128)S(1)} %fusion.25.allowed_ref), custom_call_target="tpu_custom_call" | custom-call | tf_op jit(solution)/shard_map/pallas_call | solution.py:353
  102.5 18.4 %collective-permute-done.4 = bf16[16,160,128]{2,1,0:T(8,128)(2,1)S(1)} collective-permute-done((bf16[16,160,128]{2,1,0:T(8,128)(2,1)S(1)}, bf16[16,160,128]{2,1,0:T(8,128)(2,1)S(1)}, u32[]{:S(2)}, u32[]{:S(2)}) %collective-permute-start.4) | collective-permute-done | bytes 655392 | tf_op jit(solution)/shard_map/ppermute | solution.py:382
  133.0 14.3 %shard_map.251 = (bf16[1792,512]{1,0:T(8,128)(2,1)S(1)}, f32[1792,512]{1,0:T(8,128)}, f32[16,1,512]{2,1,0:T(1,128)S(1)}, f32[16,160,128]{2,1,0:T(8,128)S(1)}) custom-call(f32[8]{0:T(128)S(1)} %get-tuple-element.330.marks_ref, bf16[4,16,160,128]{3,2,1,0:T(8,128)(2,1)} %pad_maximum_fusion.3.refs_0_, bf16[4,16,160,128]{3,2,1,0:T(8,128)(2,1)} %collective-permute-done.6.refs_1_, ...), custom_call_target="tpu_custom_call" | custom-call | tf_op jit(solution)/shard_map/pallas_call | solution.py:353
  161.1 11.5 %collective-permute-done.10.dy_ref.refs_6_ = bf16[512,1792]{1,0:T(8,128)(2,1)} collective-permute-done((bf16[512,1792]{1,0:T(8,128)(2,1)}, bf16[512,1792]{1,0:T(8,128)(2,1)}, u32[]{:S(2)}, u32[]{:S(2)}) %collective-permute-start.10) | collective-permute-done | bytes 1835040 | tf_op jit(solution)/shard_map/ppermute | solution.py:382
  179.0 16.9 %shard_map.252 = (bf16[1,512,896]{2,1,0:T(8,128)(2,1)S(1)}, bf16[2,512,896]{2,1,0:T(8,128)(2,1)S(1)}, bf16[512,1792]{1,0:T(8,128)(2,1)}) custom-call(bf16[512,1792]{1,0:T(8,128)(2,1)} %copy-done.40, bf16[512,1792]{1,0:T(8,128)(2,1)} %refs_5_.1, bf16[896,3584]{1,0:T(8,128)(2,1)} %pad_maximum_fusion.w_in_ref, bf16[896,1792]{1,0:T(8,128)(2,1)} %pad_maximum_fusion.2.w_out_ref), custom_call_target="tpu_custom_call" | custom-call | tf_op jit(solution)/shard_map/pallas_call | solution.py:353
  195.8 16.0 %collective-permute-done.8.x_ref.refs_6_ = bf16[512,1792]{1,0:T(8,128)(2,1)S(1)} collective-permute-done((bf16[512,1792]{1,0:T(8,128)(2,1)S(1)}, bf16[512,1792]{1,0:T(8,128)(2,1)S(1)}, u32[]{:S(2)}, u32[]{:S(2)}) %collective-permute-start.8) | collective-permute-done | bytes 1835040 | tf_op jit(solution)/shard_map/ppermute | solution.py:382
  216.3 16.5 %shard_map.253 = (bf16[1,512,896]{2,1,0:T(8,128)(2,1)S(1)}, bf16[2,512,896]{2,1,0:T(8,128)(2,1)S(1)}, bf16[512,1792]{1,0:T(8,128)(2,1)}) custom-call(bf16[512,1792]{1,0:T(8,128)(2,1)} %copy-done.42, bf16[512,1792]{1,0:T(8,128)(2,1)} %collective-permute-done.9.dy_ref.refs_5_, bf16[896,3584]{1,0:T(8,128)(2,1)} %pad_maximum_fusion.w_in_ref, ...), custom_call_target="tpu_custom_call" | custom-call | tf_op jit(solution)/shard_map/pallas_call | solution.py:353
  233.6 16.7 %shard_map.254 = (bf16[1,512,896]{2,1,0:T(8,128)(2,1)S(1)}, bf16[2,512,896]{2,1,0:T(8,128)(2,1)S(1)}, bf16[512,1792]{1,0:T(8,128)(2,1)}) custom-call(bf16[512,1792]{1,0:T(8,128)(2,1)} %copy-done.41, bf16[512,1792]{1,0:T(8,128)(2,1)} %collective-permute-done.10.dy_ref.refs_6_, bf16[896,3584]{1,0:T(8,128)(2,1)} %pad_maximum_fusion.w_in_ref, ...), custom_call_target="tpu_custom_call" | custom-call | tf_op jit(solution)/shard_map/pallas_call | solution.py:353
  258.2 16.5 %shard_map.255 = (bf16[1,512,896]{2,1,0:T(8,128)(2,1)S(1)}, bf16[2,512,896]{2,1,0:T(8,128)(2,1)S(1)}, bf16[512,1792]{1,0:T(8,128)(2,1)}) custom-call(bf16[512,1792]{1,0:T(8,128)(2,1)} %copy-done.43, bf16[512,1792]{1,0:T(8,128)(2,1)} %copy-done.44, bf16[896,3584]{1,0:T(8,128)(2,1)} %pad_maximum_fusion.w_in_ref, bf16[896,1792]{1,0:T(8,128)(2,1)} %pad_maximum_fusion.2.w_out_ref), custom_call_target="tpu_custom_call" | custom-call | tf_op jit(solution)/shard_map/pallas_call | solution.py:353
  276.0 20.6 %shard_map.256 = (bf16[448,3584]{1,0:T(8,128)(2,1)}, bf16[448,3584]{1,0:T(8,128)(2,1)}) custom-call(bf16[2,512,896]{2,1,0:T(8,128)(2,1)S(1)} %get-tuple-element.186.refs_0_, bf16[2,512,896]{2,1,0:T(8,128)(2,1)S(1)} %get-tuple-element.187.refs_1_, bf16[2,512,896]{2,1,0:T(8,128)(2,1)} %copy-done.10, bf16[2,512,896]{2,1,0:T(8,128)(2,1)} %copy-done.11, ...), custom_call_target="tpu_custom_call" | custom-call | tf_op jit(solution)/shard_map/pallas_call | solution.py:353
  300.7 11.1 %shard_map.257 = (bf16[448,1792]{1,0:T(8,128)(2,1)}, bf16[448,1792]{1,0:T(8,128)(2,1)}) custom-call(bf16[1,512,896]{2,1,0:T(8,128)(2,1)S(1)} %get-tuple-element.197.refs_0_, bf16[1,512,896]{2,1,0:T(8,128)(2,1)S(1)} %get-tuple-element.198.refs_1_, bf16[1,512,896]{2,1,0:T(8,128)(2,1)S(1)} %copy-done.19, bf16[1,512,896]{2,1,0:T(8,128)(2,1)S(1)} %copy-done.21, ...), custom_call_target="tpu_custom_call" | custom-call | tf_op jit(solution)/shard_map/pallas_call | solution.py:353
  364.6 13.3 %shard_map.260 = (bf16[16,160,128]{2,1,0:T(8,128)(2,1)}, bf16[1792,512]{1,0:T(8,128)(2,1)S(1)}, f32[16,1,512]{2,1,0:T(1,128)S(1)}) custom-call(f32[1792,512]{1,0:T(8,128)} %shard_map.259.grad_ref, f32[1792,512]{1,0:T(8,128)} %get-tuple-element.211.output_ref, f32[16,1,512]{2,1,0:T(1,128)S(1)} %get-tuple-element.212.denom_ref, ...), custom_call_target="tpu_custom_call" | custom-call | tf_op jit(solution)/shard_map/pallas_call | solution.py:353
  397.0 21.2 %shard_map.262 = (bf16[256,512]{1,0:T(8,128)(2,1)S(1)}, f32[256,512]{1,0:T(8,128)S(1)}, f32[1792,512]{1,0:T(8,128)}) custom-call(bf16[512,512]{1,0:T(8,128)(2,1)S(1)} %fusion.21.keys_ref.queries_ref.refs_2_, bf16[512,512]{1,0:T(8,128)(2,1)S(1)} %fusion.21.keys_ref.queries_ref.refs_2_, bf16[1792,512]{1,0:T(8,128)(2,1)} %copy-done, ...), custom_call_target="tpu_custom_call" | custom-call | tf_op jit(solution)/shard_map/pallas_call | solution.py:353
  435.4 14.7 %shard_map.263 = (bf16[256,512]{1,0:T(8,128)(2,1)S(1)}, bf16[1792,512]{1,0:T(8,128)(2,1)S(1)}) custom-call(f32[8]{0:T(128)S(1)} %copy-done.35, bf16[4,16,160,128]{3,2,1,0:T(8,128)(2,1)} %pad_maximum_fusion.4.refs_0_, bf16[4,16,160,128]{3,2,1,0:T(8,128)(2,1)} %collective-permute-done.27.refs_1_, bf16[512,512]{1,0:T(8,128)(2,1)S(1)} %fusion.21.keys_ref.queries_ref.refs_2_, ...), custom_call_target="tpu_custom_call" | custom-call | tf_op jit(solution)/shard_map/pallas_call | solution.py:353
  455.8 9.5 %collective-permute-done.28 = bf16[112,3584]{1,0:T(8,128)(2,1)} collective-permute-done((bf16[112,3584]{1,0:T(8,128)(2,1)}, bf16[112,3584]{1,0:T(8,128)(2,1)}, u32[]{:S(2)}, u32[]{:S(2)}) %collective-permute-start.28) | collective-permute-done | bytes 802848 | tf_op jit(solution)/shard_map/ppermute | solution.py:434
  473.3 9.1 %shard_map.264 = bf16[1792,2304]{1,0:T(8,128)(2,1)} custom-call(bf16[512,1792]{1,0:T(8,128)(2,1)S(1)} %copy-done.7, bf16[2304,512]{1,0:T(8,128)(2,1)} %copy-done.1), custom_call_target="tpu_custom_call" | custom-call | tf_op jit(solution)/shard_map/pallas_call | solution.py:353
  482.5 10.5 %collective-permute-done.30 = bf16[512,1792]{1,0:T(8,128)(2,1)} collective-permute-done((bf16[512,1792]{1,0:T(8,128)(2,1)}, bf16[512,1792]{1,0:T(8,128)(2,1)}, u32[]{:S(2)}, u32[]{:S(2)}) %collective-permute-start.30) | collective-permute-done | bytes 1835040 | tf_op jit(solution)/shard_map/ppermute | solution.py:382
  493.0 10.1 %collective-permute-done.31 = bf16[112,3584]{1,0:T(8,128)(2,1)} collective-permute-done((bf16[112,3584]{1,0:T(8,128)(2,1)S(1)}, bf16[112,3584]{1,0:T(8,128)(2,1)}, u32[]{:S(2)}, u32[]{:S(2)}) %collective-permute-start.31) | collective-permute-done | bytes 802848 | tf_op jit(solution)/shard_map/ppermute | solution.py:434
  516.4 10.9 %shard_map.265.mixed_ref = f32[512,1792]{1,0:T(8,128)} custom-call(bf16[2304,512]{1,0:T(8,128)(2,1)S(1)} %copy-done.2, bf16[1792,2304]{1,0:T(8,128)(2,1)} %all-gather.3.cloned.1.call-done.right_ref), custom_call_target="tpu_custom_call" | custom-call | tf_op jit(solution)/shard_map/pallas_call | solution.py:353
  535.0 16.4 %shard_map.266 = (bf16[512,1792]{1,0:T(8,128)(2,1)}, f32[4,1792]{1,0:T(4,128)S(1)}) custom-call(bf16[512,1792]{1,0:T(8,128)(2,1)S(1)} %copy-done.5, f32[2,1792]{1,0:T(2,128)S(1)} %slice.181.before_ref, f32[2,1792]{1,0:T(2,128)S(1)} %slice.183.after_ref, f32[512,1]{1,0:T(8,128)S(1)} %copy.59.scale_ref, f32[512,4]{1,0:T(8,128)S(1)} %copy.60.flags_ref, ...), custom_call_target="tpu_custom_call" | custom-call | tf_op jit(solution)/shard_map/pallas_call | solution.py:353
  551.4 15.0 %collective-permute-done.37 = bf16[224,3584]{1,0:T(8,128)(2,1)} collective-permute-done((bf16[224,3584]{1,0:T(8,128)(2,1)}, bf16[224,3584]{1,0:T(8,128)(2,1)}, u32[]{:S(2)}, u32[]{:S(2)}) %collective-permute-start.37) | collective-permute-done | bytes 1605664 | tf_op jit(solution)/shard_map/ppermute | solution.py:434
  589.4 12.5 %collective-permute-done.51 = bf16[56,1792]{1,0:T(8,128)(2,1)S(1)} collective-permute-done((bf16[56,1792]{1,0:T(8,128)(2,1)S(1)}, bf16[56,1792]{1,0:T(8,128)(2,1)S(1)}, u32[]{:S(2)}, u32[]{:S(2)}) %collective-permute-start.51) | collective-permute-done | bytes 200736 | tf_op jit(solution)/shard_map/ppermute | solution.py:471
  614.9 17.6 %collective-permute-done.46 = f32[72,128]{1,0:T(8,128)S(1)} collective-permute-done((f32[72,128]{1,0:T(8,128)S(1)}, f32[72,128]{1,0:T(8,128)S(1)}, u32[]{:S(2)}, u32[]{:S(2)}) %collective-permute-start.46) | collective-permute-done | bytes 36896 | tf_op jit(solution)/shard_map/ppermute | solution.py:413
  (378 shorter events, 287.4 us)
Async XLA Ops:
  7.2 59.3 %all-gather.3.cloned.1.call-start = ((), (), s32[]{:S(2)}) async-start(), calls=%async_computation.2 | async-start | bytes 9289728 | tf_op jit(solution)/shard_map/all_gather | solution.py:550
  7.9 141.8 %all-gather.5.cloned.1.call-start = ((), (), s32[]{:S(2)}) async-start(), calls=%async_computation.3 | async-start | bytes 7225344 | tf_op jit(solution)/shard_map/all_gather | solution.py:551
  8.7 518.7 %reduce-scatter.5.cloned.1.call-start = ((), (), s32[]{:S(2)}) async-start(), calls=%async_computation.5 | async-start | bytes 7225344 | tf_op jit(solution)/shard_map/reduce_scatter | solution.py:789
  123.3 49.3 %collective-permute-start.10 = (bf16[512,1792]{1,0:T(8,128)(2,1)}, bf16[512,1792]{1,0:T(8,128)(2,1)}, u32[]{:S(2)}, u32[]{:S(2)}) collective-permute-start(bf16[512,1792]{1,0:T(8,128)(2,1)} %refs_5_.1), channel_id=1, source_target_pairs={{0,4},{1,5},{2,6},{3,7},{4,0},{5,1},{6,2},{7,3},{8,12},{9,13},{10,... | collective-permute-start | bytes 5505032 | tf_op jit(solution)/shard_map/ppermute | solution.py:382
  124.0 52.3 %collective-permute-start.9 = (bf16[512,1792]{1,0:T(8,128)(2,1)}, bf16[512,1792]{1,0:T(8,128)(2,1)}, u32[]{:S(2)}, u32[]{:S(2)}) collective-permute-start(bf16[512,1792]{1,0:T(8,128)(2,1)} %refs_5_.1), channel_id=1, source_target_pairs={{0,2},{1,3},{2,0},{3,1},{4,6},{5,7},{6,4},{7,5},{8,10},{9,11},{10,... | collective-permute-start | bytes 5505032 | tf_op jit(solution)/shard_map/ppermute | solution.py:382
  159.2 52.6 %collective-permute-start.8 = (bf16[512,1792]{1,0:T(8,128)(2,1)S(1)}, bf16[512,1792]{1,0:T(8,128)(2,1)S(1)}, u32[]{:S(2)}, u32[]{:S(2)}) collective-permute-start(bf16[512,1792]{1,0:T(8,128)(2,1)S(1)} %multiply_convert_fusion.x_ref.refs_4_), channel_id=1, source_target_pairs={{0,4},{1,5},{2,6},{3,7},{4,0},{5,1},{6,2},{7,3},{8,12},{9,13},{10,... | collective-permute-start | bytes 5505032 | tf_op jit(solution)/shard_map/ppermute | solution.py:382
  159.8 52.1 %collective-permute-start.7 = (bf16[512,1792]{1,0:T(8,128)(2,1)S(1)}, bf16[512,1792]{1,0:T(8,128)(2,1)S(1)}, u32[]{:S(2)}, u32[]{:S(2)}) collective-permute-start(bf16[512,1792]{1,0:T(8,128)(2,1)S(1)} %multiply_convert_fusion.x_ref.refs_4_), channel_id=1, source_target_pairs={{0,2},{1,3},{2,0},{3,1},{4,6},{5,7},{6,4},{7,5},{8,10},{9,11},{10,... | collective-permute-start | bytes 5505032 | tf_op jit(solution)/shard_map/ppermute | solution.py:382
  174.8 75.5 %collective-permute-start.14 = (bf16[256,1792]{1,0:T(8,128)(2,1)}, bf16[256,1792]{1,0:T(8,128)(2,1)S(1)}, u32[]{:S(2)}, u32[]{:S(2)}) collective-permute-start(bf16[256,1792]{1,0:T(8,128)(2,1)} %slice.180), channel_id=1, source_target_pairs={{0,2},{1,3},{2,0},{3,1},{4,6},{5,7},{6,4},{7,5},{8,10},{9,11},{10,... | collective-permute-start | bytes 2752520 | tf_op jit(solution)/shard_map/ppermute | solution.py:382
  178.4 71.8 %collective-permute-start.13 = (bf16[256,1792]{1,0:T(8,128)(2,1)}, bf16[256,1792]{1,0:T(8,128)(2,1)}, u32[]{:S(2)}, u32[]{:S(2)}) collective-permute-start(bf16[256,1792]{1,0:T(8,128)(2,1)} %slice.179), channel_id=1, source_target_pairs={{0,4},{1,5},{2,6},{3,7},{4,0},{5,1},{6,2},{7,3},{8,12},{9,13},{10,... | collective-permute-start | bytes 2752520 | tf_op jit(solution)/shard_map/ppermute | solution.py:382
  232.8 63.8 %collective-permute-start.15 = (bf16[512,1792]{1,0:T(8,128)(2,1)}, bf16[512,1792]{1,0:T(8,128)(2,1)}, u32[]{:S(2)}, u32[]{:S(2)}) collective-permute-start(bf16[512,1792]{1,0:T(8,128)(2,1)} %get-tuple-element.192), channel_id=1, source_target_pairs={{0,2},{1,3},{2,0},{3,1},{4,6},{5,7},{6,4},{7,5},{8,10},{9,11},{10,... | collective-permute-start | bytes 5505032 | tf_op jit(solution)/shard_map/ppermute | solution.py:382
  252.4 44.2 %collective-permute-start.16 = (bf16[512,1792]{1,0:T(8,128)(2,1)}, bf16[512,1792]{1,0:T(8,128)(2,1)}, u32[]{:S(2)}, u32[]{:S(2)}) collective-permute-start(bf16[512,1792]{1,0:T(8,128)(2,1)} %get-tuple-element.193), channel_id=1, source_target_pairs={{0,4},{1,5},{2,6},{3,7},{4,0},{5,1},{6,2},{7,3},{8,12},{9,13},{10,... | collective-permute-start | bytes 5505032 | tf_op jit(solution)/shard_map/ppermute | solution.py:382
  296.8 43.5 %collective-permute-start.17 = (bf16[512,1792]{1,0:T(8,128)(2,1)}, bf16[512,1792]{1,0:T(8,128)(2,1)S(1)}, u32[]{:S(2)}, u32[]{:S(2)}) collective-permute-start(bf16[512,1792]{1,0:T(8,128)(2,1)} %get-tuple-element.196), channel_id=1, source_target_pairs={{0,6},{1,7},{2,4},{3,5},{4,2},{5,3},{6,0},{7,1},{8,14},{9,15},{10,... | collective-permute-start | bytes 5505032 | tf_op jit(solution)/shard_map/ppermute | solution.py:382
  341.5 41.7 %collective-permute-start.20 = (bf16[512,1792]{1,0:T(8,128)(2,1)}, bf16[512,1792]{1,0:T(8,128)(2,1)S(1)}, u32[]{:S(2)}, u32[]{:S(2)}) collective-permute-start(bf16[512,1792]{1,0:T(8,128)(2,1)} %convolution_convert_fusion.2), channel_id=1, source_target_pairs={{0,2},{1,3},{2,0},{3,1},{4,6},{5,7},{6,4},{7,5},{8,10},{9,11},{10,... | collective-permute-start | bytes 5505032 | tf_op jit(solution)/shard_map/ppermute | solution.py:382
  342.1 41.4 %collective-permute-start.21 = (bf16[512,1792]{1,0:T(8,128)(2,1)}, bf16[512,1792]{1,0:T(8,128)(2,1)S(1)}, u32[]{:S(2)}, u32[]{:S(2)}) collective-permute-start(bf16[512,1792]{1,0:T(8,128)(2,1)} %convolution_convert_fusion.1), channel_id=1, source_target_pairs={{0,4},{1,5},{2,6},{3,7},{4,0},{5,1},{6,2},{7,3},{8,12},{9,13},{10,... | collective-permute-start | bytes 5505032 | tf_op jit(solution)/shard_map/ppermute | solution.py:382
  343.5 53.5 %collective-permute-start.22 = (bf16[224,3584]{1,0:T(8,128)(2,1)}, bf16[224,3584]{1,0:T(8,128)(2,1)}, u32[]{:S(2)}, u32[]{:S(2)}) collective-permute-start(bf16[224,3584]{1,0:T(8,128)(2,1)} %get-tuple-element.219), channel_id=1, source_target_pairs={{0,8},{8,0},{16,24},{24,16},{1,9},{9,1},{17,25},{25,17},{2,10},{10... | collective-permute-start | bytes 4816904 | tf_op jit(solution)/shard_map/ppermute | solution.py:434
  345.0 51.0 %collective-permute-start.23 = (bf16[224,1792]{1,0:T(8,128)(2,1)}, bf16[224,1792]{1,0:T(8,128)(2,1)}, u32[]{:S(2)}, u32[]{:S(2)}) collective-permute-start(bf16[224,1792]{1,0:T(8,128)(2,1)} %get-tuple-element.220), channel_id=1, source_target_pairs={{0,16},{8,24},{16,0},{24,8},{1,17},{9,25},{17,1},{25,9},{2,18},{10... | collective-permute-start | bytes 2408456 | tf_op jit(solution)/shard_map/ppermute | solution.py:434
  422.5 154.1 %reduce-scatter.3.cloned.1.call-start = ((), (), s32[]{:S(2)}) async-start(), calls=%async_computation.4 | async-start | bytes 9289728 | tf_op jit(solution)/shard_map/reduce_scatter | solution.py:820
  427.8 37.5 %collective-permute-start.28 = (bf16[112,3584]{1,0:T(8,128)(2,1)}, bf16[112,3584]{1,0:T(8,128)(2,1)}, u32[]{:S(2)}, u32[]{:S(2)}) collective-permute-start(bf16[112,3584]{1,0:T(8,128)(2,1)} %constant_dynamic-slice_fusion.9), channel_id=1, source_target_pairs={{0,16},{8,24},{16,0},{24,8},{1,17},{9,25},{17,1},{25,9},{2,18},{10... | collective-permute-start | bytes 2408456 | tf_op jit(solution)/shard_map/ppermute | solution.py:434
  434.0 59.0 %collective-permute-start.30 = (bf16[512,1792]{1,0:T(8,128)(2,1)}, bf16[512,1792]{1,0:T(8,128)(2,1)}, u32[]{:S(2)}, u32[]{:S(2)}) collective-permute-start(bf16[512,1792]{1,0:T(8,128)(2,1)} %convolution_convert_fusion), channel_id=1, source_target_pairs={{0,6},{1,7},{2,4},{3,5},{4,2},{5,3},{6,0},{7,1},{8,14},{9,15},{10,... | collective-permute-start | bytes 5505032 | tf_op jit(solution)/shard_map/ppermute | solution.py:382
  504.5 46.9 %collective-permute-start.38 = (bf16[224,1792]{1,0:T(8,128)(2,1)S(1)}, bf16[224,1792]{1,0:T(8,128)(2,1)}, u32[]{:S(2)}, u32[]{:S(2)}) collective-permute-start(bf16[224,1792]{1,0:T(8,128)(2,1)S(1)} %maximum_select_fusion.3), channel_id=1, source_target_pairs={{0,16},{8,24},{16,0},{24,8},{1,17},{9,25},{17,1},{25,9},{2,18},{10... | collective-permute-start | bytes 2408456 | tf_op jit(solution)/shard_map/ppermute | solution.py:434
  507.7 58.8 %collective-permute-start.37 = (bf16[224,3584]{1,0:T(8,128)(2,1)}, bf16[224,3584]{1,0:T(8,128)(2,1)}, u32[]{:S(2)}, u32[]{:S(2)}) collective-permute-start(bf16[224,3584]{1,0:T(8,128)(2,1)} %maximum_select_fusion.1), channel_id=1, source_target_pairs={{0,8},{8,0},{16,24},{24,16},{1,9},{9,1},{17,25},{25,17},{2,10},{10... | collective-permute-start | bytes 4816904 | tf_op jit(solution)/shard_map/ppermute | solution.py:434
  531.7 41.9 %collective-permute-start.36 = (bf16[56,1792]{1,0:T(8,128)(2,1)}, bf16[56,1792]{1,0:T(8,128)(2,1)}, u32[]{:S(2)}, u32[]{:S(2)}) collective-permute-start(bf16[56,1792]{1,0:T(8,128)(2,1)} %get-tuple-element.317), channel_id=1, source_target_pairs={{0,24},{8,0},{16,8},{24,16},{1,25},{9,1},{17,9},{25,17},{2,26},{10... | collective-permute-start | bytes 602120 | tf_op jit(solution)/shard_map/ppermute | solution.py:471
  533.9 39.8 %collective-permute-start.35 = (bf16[56,1792]{1,0:T(8,128)(2,1)}, bf16[56,1792]{1,0:T(8,128)(2,1)}, u32[]{:S(2)}, u32[]{:S(2)}) collective-permute-start(bf16[56,1792]{1,0:T(8,128)(2,1)} %get-tuple-element.318), channel_id=1, source_target_pairs={{0,16},{8,24},{16,0},{24,8},{1,17},{9,25},{17,1},{25,9},{2,18},{10... | collective-permute-start | bytes 602120 | tf_op jit(solution)/shard_map/ppermute | solution.py:471
  533.9 39.8 %collective-permute-start.34 = (bf16[56,1792]{1,0:T(8,128)(2,1)}, bf16[56,1792]{1,0:T(8,128)(2,1)}, u32[]{:S(2)}, u32[]{:S(2)}) collective-permute-start(bf16[56,1792]{1,0:T(8,128)(2,1)} %get-tuple-element.319), channel_id=1, source_target_pairs={{0,8},{8,16},{16,24},{24,0},{1,9},{9,17},{17,25},{25,1},{2,10},{10... | collective-permute-start | bytes 602120 | tf_op jit(solution)/shard_map/ppermute | solution.py:471
  (113 other events, 1558.1 us)
Sparse Core Ops, SparseCore 0:
  9.9 56.5 all-gather.2
  68.4 72.7 all-gather.4
  422.6 80.0 reduce-scatter.4
  506.3 70.3 reduce-scatter.2

commit v5 on v3

--- a/solution.py
+++ b/solution.py
@@ -780,7 +780,7 @@
         qk, qk, values, dnum, dden, allowed, state_in, cont,
         left_low, right_low, left_t, right_t, query_scale,
     )
-    dk_local, dv_local, near_grads = lax.optimization_barrier((dk_local, dv_local, near_grads))
+    dk_local, dv_local, near_grads = queue.turn((dk_local, dv_local, near_grads))
     grad_stacks = stack_all(state_grads, near_grads)
     last_result, out_terms, grad_stacks[0] = lax.optimization_barrier(
         (last_result, out_terms, grad_stacks[0])
@@ -809,8 +809,7 @@
         pl.BlockSpec((block_rows, in_width), lambda i: (i, 0)),
         0, 0, mixed, grad_projected,
     )
-    in_terms, result_terms = queue.turn((in_terms, result_terms))
-    grad_projected, queue.kept = lax.optimization_barrier((grad_projected, queue.kept))
+    grad_projected, result_terms = lax.optimization_barrier((grad_projected, result_terms))
     ffn_result = sum(term.astype(F32) for term in [results[0], *result_terms])
     mixed_out = (residual + ffn_result).astype(BF)
     sum_ffn = jnp.sum(keep_rows * jnp.sum(ffn_result * ffn_result, axis=1))

time: 669 us -> 705 us (1.054)
  waiting for transfers between devices: 198 us -> 239 us
    ppermute x26, waiting for transfers between devices: 77.4 us -> 115 us  [exchanged(): return lax.ppermute(block, 'grp', [(i, i ^ offset) for i in range(count)])]
    unnamed x164 -> x168, local copies, waits for them, and re-layouts: 25 us -> 20.7 us
  transfers between devices with their start and end apart: 57 -> 57, of which waited for: 25 -> 27; matrix products, arithmetic and copies ran while one was open for 17% -> 16% of each run, Pallas kernels for 36% -> 34%
where the time goes in v5:
time: 705 us; the launch traced here: 694 us
  waiting for transfers between devices  239 us (34%)
  Pallas kernels  238 us (34%)
  starting transfers between devices  63.3 us (9%)
  other arithmetic  62.4 us (9%)
  local copies, waits for them, and re-layouts  41.9 us (6%)
  matrix products  30 us (4%)
  between operations  18.9 us (3%)
    pallas_call x18, Pallas kernels, call(): pl.pallas_call(kernel, out_shape=outs, grid=grid, in_specs=in_specs, out_...  238 us
    ppermute x26, waiting for transfers between devices, exchanged(): return lax.ppermute(block, 'grp', [(i, i ^ offset) for i in range(count)])  115 us
    ppermute x8, waiting for transfers between devices, rep_swap(): return lax.ppermute(block, 'rep', [(i, i ^ step) for i in range(count)])  44.7 us
    dot_general x7, matrix products, dot(): lax.dot_general(left, right, (((left_dim,), (right_dim,)), ((), ())), pre...  30 us
    all_gather x1, waiting for transfers between devices, body(): full_in = lax.all_gather(mix_in, 'grp', axis=0, tiled=True)  29.6 us
    ppermute x12, waiting for transfers between devices, rep_cycled(): lax.ppermute(block, 'rep', [(i, (i + shift) % count) for i in range(count)])  28 us
    ppermute x26, starting transfers between devices, exchanged(): return lax.ppermute(block, 'grp', [(i, i ^ offset) for i in range(count)])  25.6 us
    unnamed x168, local copies, waits for them, and re-layouts  20.7 us
  transfers between devices with their start and end apart: 57, of which 27 were waited for; matrix products, arithmetic and copies ran while one was open for 16% of the time, Pallas kernels for 34%

profile of v5, /device:TPU:0, one launch (start us, length us, event | category | flops | bytes accessed | tf_op | source)
XLA Modules:
  0.0 693.6 jit_solution(5830343072476356480)
XLA Ops:
  36.9 29.6 %all-gather.3.cloned.1.call-done.right_ref = bf16[1792,2304]{1,0:T(8,128)(2,1)} async-done(((bf16[224,2304]{1,0:T(8,128)(2,1)}), bf16[1792,2304]{1,0:T(8,128)(2,1)}) %all-gather.3.cloned.1.call-update) | async-done | bytes 8257552 | tf_op jit(solution)/shard_map/all_gather | solution.py:550
  86.6 10.4 %shard_map.250 = (f32[1792,512]{1,0:T(8,128)}, f32[16,1,512]{2,1,0:T(1,128)S(1)}) custom-call(bf16[512,512]{1,0:T(8,128)(2,1)S(1)} %fusion.21.keys_ref.queries_ref.refs_2_, bf16[512,512]{1,0:T(8,128)(2,1)S(1)} %fusion.21.keys_ref.queries_ref.refs_2_, bf16[1792,512]{1,0:T(8,128)(2,1)S(1)} %fusion.12.values_ref.refs_3_, f32[512,512]{1,0:T(8,128)S(1)} %fusion.25.allowed_ref), custom_call_target="tpu_custom_call" | custom-call | tf_op jit(solution)/shard_map/pallas_call | solution.py:353
  102.5 18.5 %collective-permute-done.4 = bf16[16,160,128]{2,1,0:T(8,128)(2,1)S(1)} collective-permute-done((bf16[16,160,128]{2,1,0:T(8,128)(2,1)S(1)}, bf16[16,160,128]{2,1,0:T(8,128)(2,1)S(1)}, u32[]{:S(2)}, u32[]{:S(2)}) %collective-permute-start.4) | collective-permute-done | bytes 655392 | tf_op jit(solution)/shard_map/ppermute | solution.py:382
  133.1 14.4 %shard_map.251 = (bf16[1792,512]{1,0:T(8,128)(2,1)S(1)}, f32[1792,512]{1,0:T(8,128)}, f32[16,1,512]{2,1,0:T(1,128)S(1)}, f32[16,160,128]{2,1,0:T(8,128)S(1)}) custom-call(f32[8]{0:T(128)S(1)} %get-tuple-element.320.marks_ref, bf16[4,16,160,128]{3,2,1,0:T(8,128)(2,1)} %pad_maximum_fusion.3.refs_0_, bf16[4,16,160,128]{3,2,1,0:T(8,128)(2,1)} %collective-permute-done.6.refs_1_, ...), custom_call_target="tpu_custom_call" | custom-call | tf_op jit(solution)/shard_map/pallas_call | solution.py:353
  161.3 11.3 %collective-permute-done.10.dy_ref.refs_6_ = bf16[512,1792]{1,0:T(8,128)(2,1)} collective-permute-done((bf16[512,1792]{1,0:T(8,128)(2,1)}, bf16[512,1792]{1,0:T(8,128)(2,1)}, u32[]{:S(2)}, u32[]{:S(2)}) %collective-permute-start.10) | collective-permute-done | bytes 1835040 | tf_op jit(solution)/shard_map/ppermute | solution.py:382
  179.0 16.9 %shard_map.252 = (bf16[1,512,896]{2,1,0:T(8,128)(2,1)S(1)}, bf16[2,512,896]{2,1,0:T(8,128)(2,1)S(1)}, bf16[512,1792]{1,0:T(8,128)(2,1)}) custom-call(bf16[512,1792]{1,0:T(8,128)(2,1)} %copy-done.37, bf16[512,1792]{1,0:T(8,128)(2,1)} %refs_5_.1, bf16[896,3584]{1,0:T(8,128)(2,1)} %pad_maximum_fusion.w_in_ref, bf16[896,1792]{1,0:T(8,128)(2,1)} %pad_maximum_fusion.2.w_out_ref), custom_call_target="tpu_custom_call" | custom-call | tf_op jit(solution)/shard_map/pallas_call | solution.py:353
  195.9 15.9 %collective-permute-done.8.x_ref.refs_6_ = bf16[512,1792]{1,0:T(8,128)(2,1)S(1)} collective-permute-done((bf16[512,1792]{1,0:T(8,128)(2,1)S(1)}, bf16[512,1792]{1,0:T(8,128)(2,1)S(1)}, u32[]{:S(2)}, u32[]{:S(2)}) %collective-permute-start.8) | collective-permute-done | bytes 1835040 | tf_op jit(solution)/shard_map/ppermute | solution.py:382
  216.3 16.5 %shard_map.253 = (bf16[1,512,896]{2,1,0:T(8,128)(2,1)S(1)}, bf16[2,512,896]{2,1,0:T(8,128)(2,1)S(1)}, bf16[512,1792]{1,0:T(8,128)(2,1)}) custom-call(bf16[512,1792]{1,0:T(8,128)(2,1)} %copy-done.39, bf16[512,1792]{1,0:T(8,128)(2,1)} %collective-permute-done.9.dy_ref.refs_5_, bf16[896,3584]{1,0:T(8,128)(2,1)} %pad_maximum_fusion.w_in_ref, ...), custom_call_target="tpu_custom_call" | custom-call | tf_op jit(solution)/shard_map/pallas_call | solution.py:353
  233.6 16.7 %shard_map.254 = (bf16[1,512,896]{2,1,0:T(8,128)(2,1)S(1)}, bf16[2,512,896]{2,1,0:T(8,128)(2,1)S(1)}, bf16[512,1792]{1,0:T(8,128)(2,1)}) custom-call(bf16[512,1792]{1,0:T(8,128)(2,1)} %copy-done.38, bf16[512,1792]{1,0:T(8,128)(2,1)} %collective-permute-done.10.dy_ref.refs_6_, bf16[896,3584]{1,0:T(8,128)(2,1)} %pad_maximum_fusion.w_in_ref, ...), custom_call_target="tpu_custom_call" | custom-call | tf_op jit(solution)/shard_map/pallas_call | solution.py:353
  258.2 16.5 %shard_map.255 = (bf16[1,512,896]{2,1,0:T(8,128)(2,1)S(1)}, bf16[2,512,896]{2,1,0:T(8,128)(2,1)S(1)}, bf16[512,1792]{1,0:T(8,128)(2,1)}) custom-call(bf16[512,1792]{1,0:T(8,128)(2,1)} %copy-done.40, bf16[512,1792]{1,0:T(8,128)(2,1)} %copy-done.41, bf16[896,3584]{1,0:T(8,128)(2,1)} %pad_maximum_fusion.w_in_ref, bf16[896,1792]{1,0:T(8,128)(2,1)} %pad_maximum_fusion.2.w_out_ref), custom_call_target="tpu_custom_call" | custom-call | tf_op jit(solution)/shard_map/pallas_call | solution.py:353
  276.0 20.6 %shard_map.256 = (bf16[448,3584]{1,0:T(8,128)(2,1)}, bf16[448,3584]{1,0:T(8,128)(2,1)}) custom-call(bf16[2,512,896]{2,1,0:T(8,128)(2,1)S(1)} %get-tuple-element.181.refs_0_, bf16[2,512,896]{2,1,0:T(8,128)(2,1)S(1)} %get-tuple-element.182.refs_1_, bf16[2,512,896]{2,1,0:T(8,128)(2,1)} %copy-done.10, bf16[2,512,896]{2,1,0:T(8,128)(2,1)} %copy-done.11, ...), custom_call_target="tpu_custom_call" | custom-call | tf_op jit(solution)/shard_map/pallas_call | solution.py:353
  300.7 11.1 %shard_map.257 = (bf16[448,1792]{1,0:T(8,128)(2,1)}, bf16[448,1792]{1,0:T(8,128)(2,1)}) custom-call(bf16[1,512,896]{2,1,0:T(8,128)(2,1)S(1)} %get-tuple-element.192.refs_0_, bf16[1,512,896]{2,1,0:T(8,128)(2,1)S(1)} %get-tuple-element.193.refs_1_, bf16[1,512,896]{2,1,0:T(8,128)(2,1)S(1)} %copy-done.19, bf16[1,512,896]{2,1,0:T(8,128)(2,1)S(1)} %copy-done.21, ...), custom_call_target="tpu_custom_call" | custom-call | tf_op jit(solution)/shard_map/pallas_call | solution.py:353
  354.5 8.9 %shard_map.259.grad_ref = f32[1792,512]{1,0:T(8,128)} custom-call(bf16[1792,1792]{1,0:T(8,128)(2,1)} %all-gather.5.cloned.1.call-done.left_ref, bf16[512,1792]{1,0:T(8,128)(2,1)S(1)} %get-tuple-element.205.right_ref), custom_call_target="tpu_custom_call" | custom-call | tf_op jit(solution)/shard_map/pallas_call | solution.py:353
  363.4 12.5 %shard_map.260 = (bf16[16,160,128]{2,1,0:T(8,128)(2,1)S(1)}, bf16[1792,512]{1,0:T(8,128)(2,1)S(1)}, f32[16,1,512]{2,1,0:T(1,128)S(1)}) custom-call(f32[1792,512]{1,0:T(8,128)} %shard_map.259.grad_ref, f32[1792,512]{1,0:T(8,128)} %get-tuple-element.206.output_ref, f32[16,1,512]{2,1,0:T(1,128)S(1)} %get-tuple-element.207.denom_ref, ...), custom_call_target="tpu_custom_call" | custom-call | tf_op jit(solution)/shard_map/pallas_call | solution.py:353
  403.8 21.0 %shard_map.262 = (bf16[256,512]{1,0:T(8,128)(2,1)S(1)}, f32[256,512]{1,0:T(8,128)S(1)}, f32[1792,512]{1,0:T(8,128)}) custom-call(bf16[512,512]{1,0:T(8,128)(2,1)S(1)} %fusion.21.keys_ref.queries_ref.refs_2_, bf16[512,512]{1,0:T(8,128)(2,1)S(1)} %fusion.21.keys_ref.queries_ref.refs_2_, bf16[1792,512]{1,0:T(8,128)(2,1)} %copy-done, ...), custom_call_target="tpu_custom_call" | custom-call | tf_op jit(solution)/shard_map/pallas_call | solution.py:353
  424.9 9.5 %collective-permute-done.27 = bf16[112,3584]{1,0:T(8,128)(2,1)S(1)} collective-permute-done((bf16[112,3584]{1,0:T(8,128)(2,1)S(1)}, bf16[112,3584]{1,0:T(8,128)(2,1)S(1)}, u32[]{:S(2)}, u32[]{:S(2)}) %collective-permute-start.27) | collective-permute-done | bytes 802848 | tf_op jit(solution)/shard_map/ppermute | solution.py:434
  446.7 14.7 %shard_map.263 = (bf16[256,512]{1,0:T(8,128)(2,1)S(1)}, bf16[1792,512]{1,0:T(8,128)(2,1)S(1)}) custom-call(f32[8]{0:T(128)S(1)} %copy-done.33, bf16[4,16,160,128]{3,2,1,0:T(8,128)(2,1)} %pad_maximum_fusion.4.refs_0_, bf16[4,16,160,128]{3,2,1,0:T(8,128)(2,1)} %collective-permute-done.29.refs_1_, bf16[512,512]{1,0:T(8,128)(2,1)S(1)} %fusion.21.keys_ref.queries_ref.refs_2_, ...), custom_call_target="tpu_custom_call" | custom-call | tf_op jit(solution)/shard_map/pallas_call | solution.py:353
  467.0 11.7 %collective-permute-done.30 = bf16[112,3584]{1,0:T(8,128)(2,1)S(1)} collective-permute-done((bf16[112,3584]{1,0:T(8,128)(2,1)S(1)}, bf16[112,3584]{1,0:T(8,128)(2,1)S(1)}, u32[]{:S(2)}, u32[]{:S(2)}) %collective-permute-start.30) | collective-permute-done | bytes 802848 | tf_op jit(solution)/shard_map/ppermute | solution.py:434
  480.3 9.2 %shard_map.264 = bf16[1792,2304]{1,0:T(8,128)(2,1)} custom-call(bf16[512,1792]{1,0:T(8,128)(2,1)S(1)} %copy-done.7, bf16[2304,512]{1,0:T(8,128)(2,1)} %copy-done.1), custom_call_target="tpu_custom_call" | custom-call | tf_op jit(solution)/shard_map/pallas_call | solution.py:353
  492.3 47.7 %collective-permute-done.32 = bf16[512,1792]{1,0:T(8,128)(2,1)} collective-permute-done((bf16[512,1792]{1,0:T(8,128)(2,1)}, bf16[512,1792]{1,0:T(8,128)(2,1)}, u32[]{:S(2)}, u32[]{:S(2)}) %collective-permute-start.32) | collective-permute-done | bytes 1835040 | tf_op jit(solution)/shard_map/ppermute | solution.py:382
  554.3 10.6 %shard_map.265.mixed_ref = f32[512,1792]{1,0:T(8,128)} custom-call(bf16[2304,512]{1,0:T(8,128)(2,1)S(1)} %copy-done.2, bf16[1792,2304]{1,0:T(8,128)(2,1)} %all-gather.3.cloned.1.call-done.right_ref), custom_call_target="tpu_custom_call" | custom-call | tf_op jit(solution)/shard_map/pallas_call | solution.py:353
  572.1 16.3 %shard_map.266 = (bf16[512,1792]{1,0:T(8,128)(2,1)}, f32[4,1792]{1,0:T(4,128)S(1)}) custom-call(bf16[512,1792]{1,0:T(8,128)(2,1)S(1)} %copy-done.5, f32[2,1792]{1,0:T(2,128)S(1)} %slice.181.before_ref, f32[2,1792]{1,0:T(2,128)S(1)} %slice.183.after_ref, f32[512,1]{1,0:T(8,128)S(1)} %copy.59.scale_ref, f32[512,4]{1,0:T(8,128)S(1)} %copy.60.flags_ref, ...), custom_call_target="tpu_custom_call" | custom-call | tf_op jit(solution)/shard_map/pallas_call | solution.py:353
  643.9 16.7 %collective-permute-done.46 = f32[72,128]{1,0:T(8,128)S(1)} collective-permute-done((f32[72,128]{1,0:T(8,128)S(1)}, f32[72,128]{1,0:T(8,128)S(1)}, u32[]{:S(2)}, u32[]{:S(2)}) %collective-permute-start.46) | collective-permute-done | bytes 36896 | tf_op jit(solution)/shard_map/ppermute | solution.py:413
  670.9 13.9 %collective-permute-done.48 = bf16[56,2304]{1,0:T(8,128)(2,1)S(1)} collective-permute-done((bf16[56,2304]{1,0:T(8,128)(2,1)S(1)}, bf16[56,2304]{1,0:T(8,128)(2,1)S(1)}, u32[]{:S(2)}, u32[]{:S(2)}) %collective-permute-start.48) | collective-permute-done | bytes 258080 | tf_op jit(solution)/shard_map/ppermute | solution.py:471
  (382 shorter events, 283.5 us)
Async XLA Ops:
  7.2 59.3 %all-gather.3.cloned.1.call-start = ((), (), s32[]{:S(2)}) async-start(), calls=%async_computation.2 | async-start | bytes 9289728 | tf_op jit(solution)/shard_map/all_gather | solution.py:550
  7.9 141.9 %all-gather.5.cloned.1.call-start = ((), (), s32[]{:S(2)}) async-start(), calls=%async_computation.3 | async-start | bytes 7225344 | tf_op jit(solution)/shard_map/all_gather | solution.py:551
  8.7 556.3 %reduce-scatter.5.cloned.1.call-start = ((), (), s32[]{:S(2)}) async-start(), calls=%async_computation.5 | async-start | bytes 7225344 | tf_op jit(solution)/shard_map/reduce_scatter | solution.py:789
  123.4 49.2 %collective-permute-start.10 = (bf16[512,1792]{1,0:T(8,128)(2,1)}, bf16[512,1792]{1,0:T(8,128)(2,1)}, u32[]{:S(2)}, u32[]{:S(2)}) collective-permute-start(bf16[512,1792]{1,0:T(8,128)(2,1)} %refs_5_.1), channel_id=1, source_target_pairs={{0,4},{1,5},{2,6},{3,7},{4,0},{5,1},{6,2},{7,3},{8,12},{9,13},{10,... | collective-permute-start | bytes 5505032 | tf_op jit(solution)/shard_map/ppermute | solution.py:382
  124.2 52.1 %collective-permute-start.9 = (bf16[512,1792]{1,0:T(8,128)(2,1)}, bf16[512,1792]{1,0:T(8,128)(2,1)}, u32[]{:S(2)}, u32[]{:S(2)}) collective-permute-start(bf16[512,1792]{1,0:T(8,128)(2,1)} %refs_5_.1), channel_id=1, source_target_pairs={{0,2},{1,3},{2,0},{3,1},{4,6},{5,7},{6,4},{7,5},{8,10},{9,11},{10,... | collective-permute-start | bytes 5505032 | tf_op jit(solution)/shard_map/ppermute | solution.py:382
  159.3 52.5 %collective-permute-start.8 = (bf16[512,1792]{1,0:T(8,128)(2,1)S(1)}, bf16[512,1792]{1,0:T(8,128)(2,1)S(1)}, u32[]{:S(2)}, u32[]{:S(2)}) collective-permute-start(bf16[512,1792]{1,0:T(8,128)(2,1)S(1)} %multiply_convert_fusion.x_ref.refs_4_), channel_id=1, source_target_pairs={{0,4},{1,5},{2,6},{3,7},{4,0},{5,1},{6,2},{7,3},{8,12},{9,13},{10,... | collective-permute-start | bytes 5505032 | tf_op jit(solution)/shard_map/ppermute | solution.py:382
  160.0 51.9 %collective-permute-start.7 = (bf16[512,1792]{1,0:T(8,128)(2,1)S(1)}, bf16[512,1792]{1,0:T(8,128)(2,1)S(1)}, u32[]{:S(2)}, u32[]{:S(2)}) collective-permute-start(bf16[512,1792]{1,0:T(8,128)(2,1)S(1)} %multiply_convert_fusion.x_ref.refs_4_), channel_id=1, source_target_pairs={{0,2},{1,3},{2,0},{3,1},{4,6},{5,7},{6,4},{7,5},{8,10},{9,11},{10,... | collective-permute-start | bytes 5505032 | tf_op jit(solution)/shard_map/ppermute | solution.py:382
  174.8 75.5 %collective-permute-start.14 = (bf16[256,1792]{1,0:T(8,128)(2,1)}, bf16[256,1792]{1,0:T(8,128)(2,1)S(1)}, u32[]{:S(2)}, u32[]{:S(2)}) collective-permute-start(bf16[256,1792]{1,0:T(8,128)(2,1)} %slice.180), channel_id=1, source_target_pairs={{0,2},{1,3},{2,0},{3,1},{4,6},{5,7},{6,4},{7,5},{8,10},{9,11},{10,... | collective-permute-start | bytes 2752520 | tf_op jit(solution)/shard_map/ppermute | solution.py:382
  178.4 71.8 %collective-permute-start.13 = (bf16[256,1792]{1,0:T(8,128)(2,1)}, bf16[256,1792]{1,0:T(8,128)(2,1)}, u32[]{:S(2)}, u32[]{:S(2)}) collective-permute-start(bf16[256,1792]{1,0:T(8,128)(2,1)} %slice.179), channel_id=1, source_target_pairs={{0,4},{1,5},{2,6},{3,7},{4,0},{5,1},{6,2},{7,3},{8,12},{9,13},{10,... | collective-permute-start | bytes 2752520 | tf_op jit(solution)/shard_map/ppermute | solution.py:382
  232.9 63.8 %collective-permute-start.15 = (bf16[512,1792]{1,0:T(8,128)(2,1)}, bf16[512,1792]{1,0:T(8,128)(2,1)}, u32[]{:S(2)}, u32[]{:S(2)}) collective-permute-start(bf16[512,1792]{1,0:T(8,128)(2,1)} %get-tuple-element.187), channel_id=1, source_target_pairs={{0,2},{1,3},{2,0},{3,1},{4,6},{5,7},{6,4},{7,5},{8,10},{9,11},{10,... | collective-permute-start | bytes 5505032 | tf_op jit(solution)/shard_map/ppermute | solution.py:382
  252.4 44.2 %collective-permute-start.16 = (bf16[512,1792]{1,0:T(8,128)(2,1)}, bf16[512,1792]{1,0:T(8,128)(2,1)}, u32[]{:S(2)}, u32[]{:S(2)}) collective-permute-start(bf16[512,1792]{1,0:T(8,128)(2,1)} %get-tuple-element.188), channel_id=1, source_target_pairs={{0,4},{1,5},{2,6},{3,7},{4,0},{5,1},{6,2},{7,3},{8,12},{9,13},{10,... | collective-permute-start | bytes 5505032 | tf_op jit(solution)/shard_map/ppermute | solution.py:382
  296.8 43.6 %collective-permute-start.17 = (bf16[512,1792]{1,0:T(8,128)(2,1)}, bf16[512,1792]{1,0:T(8,128)(2,1)}, u32[]{:S(2)}, u32[]{:S(2)}) collective-permute-start(bf16[512,1792]{1,0:T(8,128)(2,1)} %get-tuple-element.191), channel_id=1, source_target_pairs={{0,6},{1,7},{2,4},{3,5},{4,2},{5,3},{6,0},{7,1},{8,14},{9,15},{10,... | collective-permute-start | bytes 5505032 | tf_op jit(solution)/shard_map/ppermute | solution.py:382
  340.3 41.8 %collective-permute-start.20 = (bf16[512,1792]{1,0:T(8,128)(2,1)}, bf16[512,1792]{1,0:T(8,128)(2,1)}, u32[]{:S(2)}, u32[]{:S(2)}) collective-permute-start(bf16[512,1792]{1,0:T(8,128)(2,1)} %convolution_convert_fusion.2), channel_id=1, source_target_pairs={{0,2},{1,3},{2,0},{3,1},{4,6},{5,7},{6,4},{7,5},{8,10},{9,11},{10,... | collective-permute-start | bytes 5505032 | tf_op jit(solution)/shard_map/ppermute | solution.py:382
  341.0 41.5 %collective-permute-start.21 = (bf16[512,1792]{1,0:T(8,128)(2,1)}, bf16[512,1792]{1,0:T(8,128)(2,1)}, u32[]{:S(2)}, u32[]{:S(2)}) collective-permute-start(bf16[512,1792]{1,0:T(8,128)(2,1)} %convolution_convert_fusion.1), channel_id=1, source_target_pairs={{0,4},{1,5},{2,6},{3,7},{4,0},{5,1},{6,2},{7,3},{8,12},{9,13},{10,... | collective-permute-start | bytes 5505032 | tf_op jit(solution)/shard_map/ppermute | solution.py:382
  342.4 53.5 %collective-permute-start.22 = (bf16[224,3584]{1,0:T(8,128)(2,1)}, bf16[224,3584]{1,0:T(8,128)(2,1)}, u32[]{:S(2)}, u32[]{:S(2)}) collective-permute-start(bf16[224,3584]{1,0:T(8,128)(2,1)} %get-tuple-element.214), channel_id=1, source_target_pairs={{0,8},{8,0},{16,24},{24,16},{1,9},{9,1},{17,25},{25,17},{2,10},{10... | collective-permute-start | bytes 4816904 | tf_op jit(solution)/shard_map/ppermute | solution.py:434
  343.9 51.0 %collective-permute-start.23 = (bf16[224,1792]{1,0:T(8,128)(2,1)}, bf16[224,1792]{1,0:T(8,128)(2,1)}, u32[]{:S(2)}, u32[]{:S(2)}) collective-permute-start(bf16[224,1792]{1,0:T(8,128)(2,1)} %get-tuple-element.215), channel_id=1, source_target_pairs={{0,16},{8,24},{16,0},{24,8},{1,17},{9,25},{17,1},{25,9},{2,18},{10... | collective-permute-start | bytes 2408456 | tf_op jit(solution)/shard_map/ppermute | solution.py:434
  382.5 42.4 %collective-permute-start.26 = (bf16[16,160,128]{2,1,0:T(8,128)(2,1)S(1)}, bf16[16,160,128]{2,1,0:T(8,128)(2,1)}, u32[]{:S(2)}, u32[]{:S(2)}) collective-permute-start(bf16[16,160,128]{2,1,0:T(8,128)(2,1)S(1)} %get-tuple-element.222), channel_id=1, source_target_pairs={{0,6},{1,7},{2,4},{3,5},{4,2},{5,3},{6,0},{7,1},{8,14},{9,15},{10,... | collective-permute-start | bytes 1966088 | tf_op jit(solution)/shard_map/ppermute | solution.py:382
  384.1 40.8 %collective-permute-start.25 = (bf16[16,160,128]{2,1,0:T(8,128)(2,1)S(1)}, bf16[16,160,128]{2,1,0:T(8,128)(2,1)}, u32[]{:S(2)}, u32[]{:S(2)}) collective-permute-start(bf16[16,160,128]{2,1,0:T(8,128)(2,1)S(1)} %get-tuple-element.222), channel_id=1, source_target_pairs={{0,4},{1,5},{2,6},{3,7},{4,0},{5,1},{6,2},{7,3},{8,12},{9,13},{10,... | collective-permute-start | bytes 1966088 | tf_op jit(solution)/shard_map/ppermute | solution.py:382
  385.3 39.5 %collective-permute-start.24 = (bf16[16,160,128]{2,1,0:T(8,128)(2,1)S(1)}, bf16[16,160,128]{2,1,0:T(8,128)(2,1)}, u32[]{:S(2)}, u32[]{:S(2)}) collective-permute-start(bf16[16,160,128]{2,1,0:T(8,128)(2,1)S(1)} %get-tuple-element.222), channel_id=1, source_target_pairs={{0,2},{1,3},{2,0},{3,1},{4,6},{5,7},{6,4},{7,5},{8,10},{9,11},{10,... | collective-permute-start | bytes 1966088 | tf_op jit(solution)/shard_map/ppermute | solution.py:382
  438.6 180.9 %reduce-scatter.3.cloned.1.call-start = ((), (), s32[]{:S(2)}) async-start(), calls=%async_computation.4 | async-start | bytes 9289728 | tf_op jit(solution)/shard_map/reduce_scatter | solution.py:819
  489.6 50.4 %collective-permute-start.32 = (bf16[512,1792]{1,0:T(8,128)(2,1)}, bf16[512,1792]{1,0:T(8,128)(2,1)}, u32[]{:S(2)}, u32[]{:S(2)}) collective-permute-start(bf16[512,1792]{1,0:T(8,128)(2,1)} %convolution_convert_fusion), channel_id=1, source_target_pairs={{0,6},{1,7},{2,4},{3,5},{4,2},{5,3},{6,0},{7,1},{8,14},{9,15},{10,... | collective-permute-start | bytes 5505032 | tf_op jit(solution)/shard_map/ppermute | solution.py:382
  543.0 59.9 %collective-permute-start.37 = (bf16[224,3584]{1,0:T(8,128)(2,1)}, bf16[224,3584]{1,0:T(8,128)(2,1)}, u32[]{:S(2)}, u32[]{:S(2)}) collective-permute-start(bf16[224,3584]{1,0:T(8,128)(2,1)} %maximum_select_fusion.1), channel_id=1, source_target_pairs={{0,8},{8,0},{16,24},{24,16},{1,9},{9,1},{17,25},{25,17},{2,10},{10... | collective-permute-start | bytes 4816904 | tf_op jit(solution)/shard_map/ppermute | solution.py:434
  550.6 45.4 %collective-permute-start.38 = (bf16[224,1792]{1,0:T(8,128)(2,1)S(1)}, bf16[224,1792]{1,0:T(8,128)(2,1)}, u32[]{:S(2)}, u32[]{:S(2)}) collective-permute-start(bf16[224,1792]{1,0:T(8,128)(2,1)S(1)} %maximum_select_fusion.3), channel_id=1, source_target_pairs={{0,16},{8,24},{16,0},{24,8},{1,17},{9,25},{17,1},{25,9},{2,18},{10... | collective-permute-start | bytes 2408456 | tf_op jit(solution)/shard_map/ppermute | solution.py:434
  570.6 40.4 %collective-permute-start.34 = (bf16[56,1792]{1,0:T(8,128)(2,1)}, bf16[56,1792]{1,0:T(8,128)(2,1)}, u32[]{:S(2)}, u32[]{:S(2)}) collective-permute-start(bf16[56,1792]{1,0:T(8,128)(2,1)} %get-tuple-element.309), channel_id=1, source_target_pairs={{0,8},{8,16},{16,24},{24,0},{1,9},{9,17},{17,25},{25,1},{2,10},{10... | collective-permute-start | bytes 602120 | tf_op jit(solution)/shard_map/ppermute | solution.py:471
  (115 other events, 1623.9 us)
Sparse Core Ops, SparseCore 0:
  9.9 56.5 all-gather.2
  68.4 72.6 all-gather.4
  438.7 70.1 reduce-scatter.4
  512.4 99.3 reduce-scatter.2
